TPU v7x, 256 devices: a whole 4x4x8 slice. The times are simulated.
256 devices in a mesh: gx: 16 (over z, core), gy: 16 (over y, x).
Axes of the slice: x: 4, y: 4, z: 8, core: 2. Of those that a mesh axis runs over, the one named last changes fastest.
Arguments:
- velocity: float32 [256, 128, 1024], P('gx', 'gy'), may hold values from -18 to 18
- cotangent: float32 [256, 128, 1024], P('gx', 'gy'), may hold values from -15 to 15
- shape_coef: float32 [256, 1024], P('gx'), may hold values from 0.5 to 4
- patch_map: int32 [256, 1024], P('gx'), may hold values from 0 to 1023
- broken: int32 [1024], P(('gx', 'gy')), may hold values 0 or 1
Outputs:
- new_velocity: float32 [256, 128, 1024], P('gx', 'gy')
- grad_velocity: float32 [256, 128, 1024], P('gx', 'gy')
- patch_sens: float32 [1024], P(('gx', 'gy'))
All inputs are finite; a program needn't handle non-finite values. No bound on the sum of `broken` on one device may be relied on, other than what follows from the above.
Results may differ from a plain program's by a relative error of at most 0.0003.
Values sent between devices are 32-bit elements; how exact they have to be, the bound alone decides.
No kernel may reach another device: no remote copies, remote signals or barrier semaphores. Data moves between devices by JAX's collectives and lax.ppermute only.
A program may use at most 64 MiB of HBM per device.

v0:
```python
import math

import jax
import jax.numpy as jnp
from jax import lax
from jax.sharding import PartitionSpec as P

wall_coef = 0.2
span_coef = 0.15
wall_decay = 8.0


def extended(cells, sides, width):
    for axis, dim in sides:
        count = lax.axis_size(axis)
        ends = count - 1
        head = lax.slice_in_dim(cells, 0, width, axis=dim)
        tail = lax.slice_in_dim(cells, cells.shape[dim] - width, cells.shape[dim], axis=dim)
        cells = jnp.concatenate(
            [
                lax.ppermute(tail, axis, [(i, (i + 1) % count) for i in range(ends)]),
                cells,
                lax.ppermute(head, axis, [((i + 1) % count, i) for i in range(ends)]),
            ],
            axis=dim,
        )
    return cells


def thomas(diagonal, right_sides, stiffness):

    def down(state_in, row_data):
        upper_prev, reduced_prev = state_in
        diag_row, rhs_row = row_data
        pivot_value = diag_row + stiffness * upper_prev
        upper_now = -stiffness / pivot_value
        reduced_now = (rhs_row + stiffness * reduced_prev) / pivot_value
        return ((upper_now, reduced_now), (upper_now, reduced_now))

    start_state = (
        jnp.zeros(diagonal.shape[1:], diagonal.dtype),
        jnp.zeros(right_sides.shape[1:], right_sides.dtype),
    )
    _, (uppers, reduced) = lax.scan(down, start_state, (diagonal, right_sides))

    def upward(next_value, row_data):
        upper_now, reduced_now = row_data
        value_now = reduced_now - upper_now * next_value
        return (value_now, value_now)

    _, solution = lax.scan(
        upward, jnp.zeros(right_sides.shape[1:], right_sides.dtype), (uppers, reduced), reverse=True
    )
    return solution


def explicit(field):
    padded = extended(field, (("gy", 1),), 1)
    wall_term = padded[:, 2:, :] + padded[:, :-2, :] - 2.0 * field
    span_term = jnp.roll(field, 1, 2) + jnp.roll(field, -1, 2) - 2.0 * field
    return field + wall_coef * wall_term + span_coef * span_term


def partition_solve(diagonal, right_sides, stiffness):
    planes, count, line_count = right_sides.shape
    plane_ids = jnp.arange(planes)[:, None, None]
    unit_line = jnp.ones((1, 1, line_count), jnp.float32)
    left_unit = jnp.where(plane_ids == 0, stiffness, 0.0) * unit_line
    right_unit = jnp.where(plane_ids == planes - 1, stiffness, 0.0) * unit_line
    full = thomas(
        diagonal, jnp.concatenate([left_unit, right_unit, right_sides], axis=1), stiffness
    )
    left_spike = full[:, 0]
    right_spike = full[:, 1]
    local_part = full[:, 2:]
    rims = jnp.concatenate([full[0], full[planes - 1]], axis=0)
    gathered = lax.all_gather(rims[None], "gx", axis=0, tiled=True)
    width = count + 2
    tops = gathered[:, :width]
    bottoms = gathered[:, width:]
    device_data = (
        tops[:, 0],
        tops[:, 1],
        tops[:, 2:],
        bottoms[:, 0],
        bottoms[:, 1],
        bottoms[:, 2:],
    )

    def eliminate(state_in, item):
        beta_in, gamma_in = state_in
        left_top, right_top, local_top, left_bottom, right_bottom, local_bottom = item
        pivot_value = 1.0 - left_top * gamma_in
        tau_now = (local_top + left_top * beta_in) / pivot_value
        sigma_now = right_top / pivot_value
        beta_out = local_bottom + left_bottom * (beta_in + gamma_in * tau_now)
        gamma_out = left_bottom * gamma_in * sigma_now + right_bottom
        return ((beta_out, gamma_out), (tau_now, sigma_now, beta_in, gamma_in))

    zero_rhs = jnp.zeros((count, line_count), jnp.float32)
    zero_line = jnp.zeros((line_count,), jnp.float32)
    _, eliminated = lax.scan(eliminate, (zero_rhs, zero_line), device_data)

    def substitute(top_next, item):
        tau_now, sigma_now, beta_in, gamma_in = item
        top_now = tau_now + sigma_now * top_next
        bottom_prev = beta_in + gamma_in * top_now
        return (top_now, (top_now, bottom_prev))

    _, (top_all, bottom_all) = lax.scan(substitute, zero_rhs, eliminated, reverse=True)
    position = lax.axis_index("gx")
    bottom_prev = lax.dynamic_index_in_dim(bottom_all, position, 0, keepdims=False)
    padded_top = jnp.concatenate([top_all, zero_rhs[None]], axis=0)
    top_next = lax.dynamic_index_in_dim(padded_top, position + 1, 0, keepdims=False)
    return (
        local_part + left_spike[:, None] * bottom_prev[None] + right_spike[:, None] * top_next[None]
    )


def local(velocity, cotangent, shape_coef, patch_map, broken):
    planes, rows_here, spanwise = velocity.shape
    groups_x = lax.axis_size("gx")
    groups_y = lax.axis_size("gy")
    total_rows = rows_here * groups_y
    stiffness = 3.0 * planes * planes
    line_count = rows_here * spanwise
    heights = (lax.axis_index("gy") * rows_here + jnp.arange(rows_here)).astype(jnp.float32)
    damping = jnp.exp(-wall_decay * heights / total_rows)
    diagonal = (1.0 + 2.0 * stiffness + shape_coef[:, None, :] * damping[None, :, None]).reshape(
        planes, line_count
    )
    forcing = explicit(velocity).reshape(planes, line_count)
    target = cotangent.reshape(planes, line_count)
    both = partition_solve(diagonal, jnp.stack([forcing, target], axis=1), stiffness)
    new_flat = both[:, 0]
    adjoint_flat = both[:, 1]
    new_velocity = new_flat.reshape(planes, rows_here, spanwise)
    adjoint = adjoint_flat.reshape(planes, rows_here, spanwise)
    grad_velocity = explicit(adjoint)
    cell_sens = jnp.sum(adjoint * new_velocity * damping[None, :, None], axis=1)
    owned_count = broken.shape[0]
    patch_count = owned_count * groups_x * groups_y
    norm_factor = 1.0 / math.sqrt(planes * groups_x * total_rows * spanwise / patch_count)
    keep = (1 - broken).astype(jnp.float32)
    wall_share = lax.psum_scatter(cell_sens, "gy", scatter_dimension=1, tiled=True)
    share_width = wall_share.shape[1]
    owned_map = lax.dynamic_slice_in_dim(
        patch_map, lax.axis_index("gy") * share_width, share_width, 1
    )
    partial_sums = jax.ops.segment_sum(
        wall_share.reshape(-1), owned_map.reshape(-1), num_segments=patch_count
    )
    own_patches = lax.psum_scatter(partial_sums, ("gx", "gy"), scatter_dimension=0, tiled=True)
    patch_sens = -keep * norm_factor * own_patches
    return (new_velocity, grad_velocity, patch_sens)


def solution(mesh):
    return jax.shard_map(
        local,
        mesh=mesh,
        in_specs=(
            P("gx", "gy", None),
            P("gx", "gy", None),
            P("gx", None),
            P("gx", None),
            P(("gx", "gy")),
        ),
        out_specs=(P("gx", "gy", None), P("gx", "gy", None), P(("gx", "gy"))),
        check_vma=False,
    )
```

profile of v0, /device:TPU:1, one launch (start us, length us, event | category | flops | bytes accessed | tf_op | source)
XLA Modules:
  0.0 480.5 jit_solution(11787352124508495855)
XLA Ops:
  7.2 2.0 fusion.30
  10.6 5.2 %collective-permute-start.1 = (f32[16,1,1024]{2,1,0:T(1,128)}, f32[16,1,1024]{2,1,0:T(1,128)}, u32[]{:S(2)}, u32[]{:S(2)}) collective-permute-start(f32[16,1,1024]{2,1,0:T(1,128)} %get-tuple-element.617), channel_id=1, source_target_pairs={{0,1},{1,2},{2,3},{3,4},{4,5},{5,6},{6,7},{7,8},{8,9},{9,10},{10,1... | collective-permute-start | bytes 196616 | tf_op jit(solution)/shard_map/ppermute | solution.py:21
  23.3 2.1 pad_maximum_fusion
  25.5 1.8 broadcast.112.clone
  27.3 31.3 %while.74 = (s32[]{:T(128)}, f32[8192]{0:T(1024)S(1)}, f32[4,8192]{1,0:T(4,128)S(1)}, f32[16,8192]{1,0:T(8,128)S(1)}, f32[16,4,8192]{2,1,0:T(4,128)}, /*index=5*...) while((s32[]{:T(128)}, f32[8192]{0:T(1024)S(1)}, f32[4,8192]{1,0:T(4,128)S(1)}, ...), condition=%wide.region_1.2_spmd.clone, body=%wide.region_0.1_spmd.clone.sunk | while | flops 163843 | bytes 819824 | solution.py:44
  59.0 18.2 %while.75 = (s32[]{:T(128)}, f32[4,8192]{1,0:T(4,128)S(1)}, f32[16,4,8192]{2,1,0:T(4,128)S(1)}, f32[16,4,8192]{2,1,0:T(4,128)}, f32[16,8192]{1,0:T(8,128)S(1)}, /*index=5*/s32[]{:T(128)}, s32[]{:T(128)}, s32[]{:T(128)}) while((s32[]{:T(128)}, f32[4,8192]{1,0:T(4,128)S(1)}, f32[16,4,8192]{2,1,0:T(4,128)S(1)}, ...), condition=%wide.region_3.4_spmd.clone, body=%wide.region_2.3_spmd.clone.sunk | while | flops 98308 | bytes 622707 | solution.py:51
  79.6 1.6 copy_bitcast_fusion
  81.2 44.5 %all-gather.3.cloned.1.call-done = f32[128,8192]{1,0:T(8,128)} async-done(((f32[8,8192]{1,0:T(8,128)}), f32[128,8192]{1,0:T(8,128)}) %all-gather.3.cloned.1.call-update) | async-done | bytes 4194320 | tf_op jit(solution)/shard_map/all_gather | solution.py:77
  125.7 8.4 %fusion.22 = (f32[16,1,8192]{2,1,0:T(1,128)S(1)}, f32[16,1,8192]{2,1,0:T(1,128)S(1)}, f32[16,1,8192]{2,1,0:T(1,128)S(1)}, f32[16,1,8192]{2,1,0:T(1,128)S(1)}) fusion(f32[16,8,8192]{2,1,0:T(8,128)} %bitcast.132), kind=kLoop, calls=%fused_computation.80 | loop fusion | bytes 4194304 | tf_op jit(solution)/shard_map/slice | solution.py:86
  134.1 2.5 fusion.23
  136.7 1.6 copy_bitcast_fusion.1
  138.3 1.6 copy_bitcast_fusion.3
  143.6 107.4 %while.76 = (s32[]{:T(128)}, f32[2,8192]{1,0:T(2,128)S(1)}, f32[8192]{0:T(1024)S(1)}, f32[16,2,8192]{2,1,0:T(2,128)}, f32[16,8192]{1,0:T(8,128)S(1)}, /*index=5*...) while((s32[]{:T(128)}, f32[2,8192]{1,0:T(2,128)S(1)}, ...), condition=%wide.region_5.6_spmd.clone, body=%wide.region_4.5_spmd.clone.sunk | while | flops 253955 | bytes 1409709 | solution.py:102
  145.8 1.6 bitcast_dynamic-update-slice_fusion.13
  147.5 1.8 dynamic_update_slice.76
  152.5 1.6 bitcast_dynamic-update-slice_fusion.13
  154.3 1.8 dynamic_update_slice.76
  161.0 1.8 dynamic_update_slice.76
  165.9 1.6 bitcast_dynamic-update-slice_fusion.13
  167.7 1.8 dynamic_update_slice.76
  172.7 1.6 bitcast_dynamic-update-slice_fusion.13
  174.4 1.8 dynamic_update_slice.76
  181.1 1.8 dynamic_update_slice.76
  187.8 1.8 dynamic_update_slice.76
  192.8 1.6 bitcast_dynamic-update-slice_fusion.13
  194.5 1.8 dynamic_update_slice.76
  199.5 1.6 bitcast_dynamic-update-slice_fusion.13
  201.2 1.8 dynamic_update_slice.76
  208.0 1.8 dynamic_update_slice.76
  212.9 1.6 bitcast_dynamic-update-slice_fusion.13
  214.7 1.8 dynamic_update_slice.76
  219.7 1.6 bitcast_dynamic-update-slice_fusion.13
  221.4 1.8 dynamic_update_slice.76
  226.4 1.6 bitcast_dynamic-update-slice_fusion.13
  228.1 1.8 dynamic_update_slice.76
  233.1 1.6 bitcast_dynamic-update-slice_fusion.13
  234.8 1.8 dynamic_update_slice.76
  239.8 1.6 bitcast_dynamic-update-slice_fusion.13
  241.5 1.8 dynamic_update_slice.76
  246.5 1.6 bitcast_dynamic-update-slice_fusion.13
  248.2 1.8 dynamic_update_slice.76
  253.7 43.8 %while.77 = (s32[]{:T(128)}, f32[2,8192]{1,0:T(2,128)S(1)}, f32[16,2,8192]{2,1,0:T(2,128)S(1)}, f32[16,2,8192]{2,1,0:T(2,128)}, f32[16,2,8192]{2,1,0:T(2,128)}, ...) while((s32[]{:T(128)}, f32[2,8192]{1,0:T(2,128)S(1)}, ...), condition=%wide.region_7.8_spmd.clone, body=%wide.region_6.7_spmd.clone.sunk | while | flops 81924 | bytes 655503 | solution.py:110
  254.7 1.6 bitcast_dynamic-update-slice_fusion.14
  257.5 1.6 bitcast_dynamic-update-slice_fusion.14
  260.2 1.6 bitcast_dynamic-update-slice_fusion.14
  263.0 1.6 bitcast_dynamic-update-slice_fusion.14
  265.7 1.6 bitcast_dynamic-update-slice_fusion.14
  268.4 1.6 bitcast_dynamic-update-slice_fusion.14
  271.2 1.6 bitcast_dynamic-update-slice_fusion.14
  273.9 1.6 bitcast_dynamic-update-slice_fusion.14
  276.7 1.6 bitcast_dynamic-update-slice_fusion.14
  279.4 1.6 bitcast_dynamic-update-slice_fusion.14
  282.2 1.6 bitcast_dynamic-update-slice_fusion.14
  284.9 1.6 bitcast_dynamic-update-slice_fusion.14
  287.6 1.6 bitcast_dynamic-update-slice_fusion.14
  290.4 1.6 bitcast_dynamic-update-slice_fusion.14
  293.1 1.6 bitcast_dynamic-update-slice_fusion.14
  295.9 1.6 bitcast_dynamic-update-slice_fusion.14
  298.4 2.2 multiply_add_fusion.1
  300.6 2.7 slice_reduce_fusion
  305.7 4.0 collective-permute-start.3
  312.2 75.1 %reduce-scatter.4.cloned.1.call-done = f32[64,16]{1,0:T(8,128)} async-done(((f32[1024,16]{1,0:T(8,128)}), f32[64,16]{1,0:T(8,128)}) %reduce-scatter.4.cloned.1.call-update) | async-done | bytes 4112
  388.2 7.6 %scatter_custom_fusion = f32[1024]{0:T(1024)S(1)} fusion(s32[1024]{0:T(1024)S(1)} %reshape.48, f32[1024]{0:T(1024)S(1)} %reshape.50, f32[]{:T(128)} %constant.154.clone.1), kind=kCustom, calls=%fused_computation.73 | custom fusion | flops 1024 | bytes 4100 | tf_op jit(solution)/shard_map/scatter-add | solution.py:150
  395.8 77.2 %all-reduce.1 = f32[1024]{0:T(1024)S(1)} all-reduce(f32[1024]{0:T(1024)S(1)} %scatter_custom_fusion), channel_id=4, replica_groups=mesh['gx'=16,'gy'=16] {'gx','gy'}, use_global_device_ids=true, to_apply=%region_11.12.clone | all-reduce | flops 1024 | bytes 8192
  (287 shorter events, 150.6 us)
Async XLA Ops:
  7.2 71.1 %copy-start = (s32[16,1024]{1,0:T(8,128)S(1)}, s32[16,1024]{1,0:T(8,128)}, u32[]{:S(2)}) copy-start(s32[16,1024]{1,0:T(8,128)} %param.16) | copy-start | bytes 196612
  7.2 10.0 %copy-start.1 = (f32[16,8,1024]{2,1,0:T(8,128)S(1)}, f32[16,8,1024]{2,1,0:T(8,128)}, u32[]{:S(2)}) copy-start(f32[16,8,1024]{2,1,0:T(8,128)} %param.13) | copy-start | bytes 1572868
  7.2 10.7 %copy-start.5 = (f32[16,8,1024]{2,1,0:T(8,128)S(1)}, f32[16,8,1024]{2,1,0:T(8,128)}, u32[]{:S(2)}) copy-start(f32[16,8,1024]{2,1,0:T(8,128)} %param.14) | copy-start | bytes 1572868
  7.2 118.5 %all-gather.3.cloned.1.call-start = ((), (), s32[]{:S(2)}) async-start(), calls=%async_computation.1 | async-start | bytes 4456448 | tf_op jit(solution)/shard_map/all_gather | solution.py:77
  9.3 11.5 %collective-permute-start = (f32[16,1,1024]{2,1,0:T(1,128)}, f32[16,1,1024]{2,1,0:T(1,128)}, u32[]{:S(2)}, u32[]{:S(2)}) collective-permute-start(f32[16,1,1024]{2,1,0:T(1,128)} %get-tuple-element.616), channel_id=1, source_target_pairs={{1,0},{2,1},{3,2},{4,3},{5,4},{6,5},{7,6},{8,7},{9,8},{10,9},{11,1... | collective-permute-start | bytes 196616 | tf_op jit(solution)/shard_map/ppermute | solution.py:23
  10.6 10.2 %collective-permute-start.1 = (f32[16,1,1024]{2,1,0:T(1,128)}, f32[16,1,1024]{2,1,0:T(1,128)}, u32[]{:S(2)}, u32[]{:S(2)}) collective-permute-start(f32[16,1,1024]{2,1,0:T(1,128)} %get-tuple-element.617), channel_id=1, source_target_pairs={{0,1},{1,2},{2,3},{3,4},{4,5},{5,6},{6,7},{7,8},{8,9},{9,10},{10,1... | collective-permute-start | bytes 196616 | tf_op jit(solution)/shard_map/ppermute | solution.py:21
  18.6 2.2 copy-start.6
  18.6 2.2 copy-start.7
  78.0 309.3 %reduce-scatter.4.cloned.1.call-start = ((), (), s32[]{:S(2)}) async-start(), calls=%async_computation.2 | async-start | bytes 557056
  125.7 8.4 %copy-start.2 = (f32[128,8192]{1,0:T(8,128)S(1)}, f32[128,8192]{1,0:T(8,128)}, u32[]{:S(2)}) copy-start(f32[128,8192]{1,0:T(8,128)} %all-gather.3.cloned.1.call-done) | copy-start | bytes 12582916
  251.0 0.8 copy-start.4
  304.4 7.8 %copy-start.3 = (f32[2,8,8,1024]{3,2,1,0:T(8,128)}, f32[2,8,8,1024]{3,2,1,0:T(8,128)S(1)}, u32[]{:S(2)}) copy-start(f32[2,8,8,1024]{3,2,1,0:T(8,128)S(1)} %copy.23) | copy-start | bytes 1572868
  304.4 6.6 %collective-permute-start.2 = (f32[16,1,1024]{2,1,0:T(1,128)S(1)}, f32[16,1,1024]{2,1,0:T(1,128)S(1)}, u32[]{:S(2)}, u32[]{:S(2)}) collective-permute-start(f32[16,1,1024]{2,1,0:T(1,128)S(1)} %get-tuple-element.610), channel_id=1, source_target_pairs={{1,0},{2,1},{3,2},{4,3},{5,4},{6,5},{7,6},{8,7},{9,8},{10,9},{11,1... | collective-permute-start | bytes 196616 | tf_op jit(solution)/shard_map/ppermute | solution.py:23
  305.7 167.4 %copy-start.8 = (s32[4]{0:T(128)S(1)}, s32[4]{0:T(128)}, u32[]{:S(2)}) copy-start(s32[4]{0:T(128)} %param.17) | copy-start | bytes 52
  305.7 5.3 %collective-permute-start.3 = (f32[16,1,1024]{2,1,0:T(1,128)S(1)}, f32[16,1,1024]{2,1,0:T(1,128)S(1)}, u32[]{:S(2)}, u32[]{:S(2)}) collective-permute-start(f32[16,1,1024]{2,1,0:T(1,128)S(1)} %get-tuple-element.611), channel_id=1, source_target_pairs={{0,1},{1,2},{2,3},{3,4},{4,5},{5,6},{6,7},{7,8},{8,9},{9,10},{10,1... | collective-permute-start | bytes 196616 | tf_op jit(solution)/shard_map/ppermute | solution.py:21
Sparse Core Ops, SparseCore 0:
  78.2 47.5 all-gather.2
  311.1 76.1 reduce-scatter.3
where the time goes:
time: 486 us; the launch traced here: 480 us
  local copies, waits for them, and re-layouts  141 us (29%)
  waiting for transfers between devices  120 us (25%)
  other arithmetic  115 us (24%)
  blocking collectives  77.2 us (16%)
  between operations  14.4 us (3%)
  starting transfers between devices  12 us (2%)
    unnamed x1, blocking collectives  77.2 us
    unnamed x3, waiting for transfers between devices  75.2 us
    dynamic_slice x80, local copies, waits for them, and re-layouts, thomas(): _, (uppers, reduced) = lax.scan(down, start_state, (diagonal, right_sides))  68.1 us
    dynamic_update_slice x32, other arithmetic, partition_solve(): _, eliminated = lax.scan(eliminate, (zero_rhs, zero_line), device_data)  51.3 us
    all_gather x1, waiting for transfers between devices, partition_solve(): gathered = lax.all_gather(rims[None], 'gx', axis=0, tiled=True)  44.5 us
    dynamic_update_slice x48, local copies, waits for them, and re-layouts, thomas(): _, (uppers, reduced) = lax.scan(down, start_state, (diagonal, right_sides))  32.8 us
    dynamic_update_slice x32, other arithmetic, thomas(): _, (uppers, reduced) = lax.scan(down, start_state, (diagonal, right_sides))  29.9 us
    add x16, other arithmetic, eliminate(): beta_out = local_bottom + left_bottom * (beta_in + gamma_in * tau_now)  16 us
  transfers between devices with their start and end apart: 6, of which 2 were waited for; matrix products, arithmetic and copies ran while one was open for 2% of the time, Pallas kernels for 0%

commit v1 on v0

v1 whole, which is shorter than its diff:
```python
import math

import jax
import jax.numpy as jnp
from jax import lax
from jax.experimental import pallas as pl
from jax.experimental.pallas import tpu as pltpu
from jax.sharding import PartitionSpec as P

wall_coef = 0.2
span_coef = 0.15
wall_decay = 8.0
VMEM = pl.BlockSpec(memory_space=pltpu.VMEM)
F32 = jnp.float32
LANES = 128


def shape_of(*dims):
    return jax.ShapeDtypeStruct(dims, F32)


def explicit(field, below, above):
    rows, span = field.shape
    row_ids = lax.broadcasted_iota(jnp.int32, (rows, span), 0)
    lower = jnp.where(row_ids == 0, below, pltpu.roll(field, 1, 0))
    upper = jnp.where(row_ids == rows - 1, above, pltpu.roll(field, rows - 1, 0))
    wall_term = upper + lower - 2.0 * field
    span_term = pltpu.roll(field, 1, 1) + pltpu.roll(field, span - 1, 1) - 2.0 * field
    return field + wall_coef * wall_term + span_coef * span_term


def damping_rows(rows, total_rows):
    first = lax.axis_index("gy") * rows
    heights = (first + lax.broadcasted_iota(jnp.int32, (rows, 1), 0)).astype(F32)
    return jnp.exp(-wall_decay * heights / total_rows)


def matrix_kernel(stiffness, total_rows, coef_ref, target_ref, factor_ref, adj_down_ref, rims_ref, left_ref):
    planes, rows, span = target_ref.shape
    damping = damping_rows(rows, total_rows)
    factor = jnp.zeros((rows, span), F32)
    reduced = jnp.zeros((rows, span), F32)
    left = jnp.ones((rows, span), F32)
    for k in range(planes):
        diagonal = 1.0 + 2.0 * stiffness + coef_ref[k : k + 1, :] * damping
        factor = stiffness / (diagonal - stiffness * factor)
        reduced = (target_ref[k] + reduced) * factor
        left = left * factor
        factor_ref[k] = factor
        adj_down_ref[k] = reduced
        left_ref[k] = left
    value, right = reduced, factor
    rims_ref[1] = left
    rims_ref[2] = factor
    rims_ref[4] = reduced
    for k in range(planes - 2, -1, -1):
        factor = factor_ref[k]
        value = adj_down_ref[k] + factor * value
        left = left_ref[k] + factor * left
    rims_ref[0] = left
    rims_ref[3] = value


def velocity_kernel(velocity_ref, below_ref, above_ref, factor_ref, rims_ref, down_ref, send_ref):
    planes, rows, span = velocity_ref.shape
    reduced = jnp.zeros((rows, span), F32)
    for k in range(planes):
        forcing = explicit(velocity_ref[k], below_ref[k : k + 1, :], above_ref[k : k + 1, :])
        reduced = (forcing + reduced) * factor_ref[k]
        down_ref[k] = reduced
    value = reduced
    for k in range(planes - 2, -1, -1):
        value = down_ref[k] + factor_ref[k] * value
    parts = send_ref.shape[0]
    half = send_ref.shape[2]
    pieces = [rims_ref[i] for i in range(5)] + [value, reduced]
    for i, piece in enumerate(pieces):
        for j in range(parts):
            chunk, side = divmod(j, rows // half)
            send_ref[j, i] = piece[side * half : (side + 1) * half, chunk * LANES : (chunk + 1) * LANES]


def reduced_kernel(in_ref, out_ref, keep_ref):
    blocks = in_ref.shape[0]
    tile = in_ref.shape[2:]
    zero = jnp.zeros(tile, F32)
    gamma, beta_a, beta_v = zero, zero, zero
    for i in range(blocks):
        top, cross, low = in_ref[i, 0], in_ref[i, 1], in_ref[i, 2]
        top_a, low_a, top_v, low_v = in_ref[i, 3], in_ref[i, 4], in_ref[i, 5], in_ref[i, 6]
        inverse = 1.0 / (1.0 - top * gamma)
        tau_a = (top_a + top * beta_a) * inverse
        tau_v = (top_v + top * beta_v) * inverse
        sigma = cross * inverse
        keep_ref[i, 0] = tau_a
        keep_ref[i, 1] = tau_v
        keep_ref[i, 2] = sigma
        keep_ref[i, 3] = gamma
        keep_ref[i, 4] = beta_a
        keep_ref[i, 5] = beta_v
        beta_a = low_a + cross * (beta_a + gamma * tau_a)
        beta_v = low_v + cross * (beta_v + gamma * tau_v)
        gamma = low + cross * gamma * sigma
    next_a, next_v = zero, zero
    for i in range(blocks - 1, -1, -1):
        out_ref[i, 1] = next_a
        out_ref[i, 3] = next_v
        next_a = keep_ref[i, 0] + keep_ref[i, 2] * next_a
        next_v = keep_ref[i, 1] + keep_ref[i, 2] * next_v
        out_ref[i, 0] = keep_ref[i, 4] + keep_ref[i, 3] * next_a
        out_ref[i, 2] = keep_ref[i, 5] + keep_ref[i, 3] * next_v


def combine_kernel(
    stiffness, total_rows, factor_ref, adj_down_ref, down_ref, back_ref, map_ref,
    new_ref, adj_ref, sums_ref, low_ref, high_ref, left_ref,
):
    planes, rows, span = factor_ref.shape
    half = back_ref.shape[2]
    per = rows // half
    damping = damping_rows(rows, total_rows)
    scale = 1.0 / stiffness

    def assembled(i):
        return jnp.concatenate(
            [
                jnp.concatenate([back_ref[chunk * per + side, i] for side in range(per)], axis=0)
                for chunk in range(span // LANES)
            ],
            axis=1,
        )

    prev_a, value_a, prev_v, value_v = (assembled(i) for i in range(4))
    left = jnp.ones((rows, span), F32)
    for k in range(planes):
        left = left * factor_ref[k]
        left_ref[k] = left
    patch_rows, patch_lanes = sums_ref.shape
    row_ids = lax.broadcasted_iota(jnp.int32, (patch_rows, span), 0)
    lane_ids = lax.broadcasted_iota(jnp.int32, (patch_lanes, span), 0)
    total = jnp.zeros((3 * patch_rows, patch_lanes), F32)
    for k in range(planes - 1, -1, -1):
        factor, left = factor_ref[k], left_ref[k]
        value_a = adj_down_ref[k] + left * prev_a + factor * value_a
        value_v = down_ref[k] + left * prev_v + factor * value_v
        adjoint = value_a * scale
        new = value_v * scale
        adj_ref[k] = adjoint
        new_ref[k] = new
        low_ref[k : k + 1, :] = adjoint[:1]
        high_ref[k : k + 1, :] = adjoint[rows - 1 :]
        cells = jnp.sum(adjoint * new * damping, axis=0, keepdims=True)
        patches = map_ref[k : k + 1, :]
        first = cells.astype(jnp.bfloat16).astype(F32)
        rest = cells - first
        second = rest.astype(jnp.bfloat16).astype(F32)
        third = rest - second
        in_row = row_ids == patches // patch_lanes
        parts = jnp.concatenate(
            [jnp.where(in_row, part, 0.0) for part in (first, second, third)], axis=0
        ).astype(jnp.bfloat16)
        places = jnp.where(lane_ids == patches % patch_lanes, 1.0, 0.0).astype(jnp.bfloat16)
        total = total + lax.dot_general(
            parts, places, (((1,), (1,)), ((), ())), preferred_element_type=F32
        )
    sums_ref[...] = (
        total[:patch_rows] + total[patch_rows : 2 * patch_rows] + total[2 * patch_rows :]
    )


def gradient_kernel(adj_ref, below_ref, above_ref, out_ref):
    for k in range(adj_ref.shape[0]):
        out_ref[k] = explicit(adj_ref[k], below_ref[k : k + 1, :], above_ref[k : k + 1, :])


def call(kernel, outs, scratch, *operands):
    return pl.pallas_call(
        kernel,
        out_shape=outs,
        in_specs=[VMEM] * len(operands),
        out_specs=[VMEM] * len(outs),
        scratch_shapes=[pltpu.VMEM(dims, F32) for dims in scratch],
        compiler_params=pltpu.CompilerParams(vmem_limit_bytes=32 * 1024 * 1024),
    )(*operands)


def from_neighbours(low, high):
    count = lax.axis_size("gy")
    ends = count - 1
    below = lax.ppermute(high, "gy", [(i, i + 1) for i in range(ends)])
    above = lax.ppermute(low, "gy", [(i + 1, i) for i in range(ends)])
    return below, above


def local(velocity, cotangent, shape_coef, patch_map, broken):
    planes, rows, span = velocity.shape
    groups_x = lax.axis_size("gx")
    groups_y = lax.axis_size("gy")
    total_rows = rows * groups_y
    stiffness = 3.0 * planes * planes
    field = (planes, rows, span)
    half = rows * span // (groups_x * LANES)
    below, above = from_neighbours(velocity[:, 0], velocity[:, rows - 1])

    def with_sizes(kernel):
        return lambda *refs: kernel(stiffness, total_rows, *refs)

    factor, adj_down, rims = call(
        with_sizes(matrix_kernel),
        [shape_of(*field), shape_of(*field), shape_of(5, rows, span)],
        [field],
        shape_coef,
        cotangent,
    )
    down, send = call(
        velocity_kernel,
        [shape_of(*field), shape_of(groups_x, 7, half, LANES)],
        [],
        velocity,
        below,
        above,
        factor,
        rims,
    )
    blocks = lax.all_to_all(send, "gx", 0, 0, tiled=True)
    (solved,) = call(
        reduced_kernel,
        [shape_of(groups_x, 4, half, LANES)],
        [(groups_x, 6, half, LANES)],
        blocks,
    )
    back = lax.all_to_all(solved, "gx", 0, 0, tiled=True)
    owned_count = broken.shape[0]
    patch_count = owned_count * groups_x * groups_y
    new_velocity, adjoint, sums, low, high = call(
        with_sizes(combine_kernel),
        [
            shape_of(*field),
            shape_of(*field),
            shape_of(patch_count // LANES, LANES),
            shape_of(planes, span),
            shape_of(planes, span),
        ],
        [field],
        factor,
        adj_down,
        down,
        back,
        patch_map,
    )
    below, above = from_neighbours(low, high)
    shares = lax.all_to_all(
        sums.reshape(groups_x * groups_y, owned_count), ("gx", "gy"), 0, 0, tiled=True
    )
    own_patches = jnp.sum(shares, axis=0)
    (grad_velocity,) = call(gradient_kernel, [shape_of(*field)], [], adjoint, below, above)
    norm_factor = 1.0 / math.sqrt(planes * groups_x * total_rows * span / patch_count)
    keep = (1 - broken).astype(F32)
    patch_sens = -keep * norm_factor * own_patches
    return (new_velocity, grad_velocity, patch_sens)


def solution(mesh):
    return jax.shard_map(
        local,
        mesh=mesh,
        in_specs=(
            P("gx", "gy", None),
            P("gx", "gy", None),
            P("gx", None),
            P("gx", None),
            P(("gx", "gy")),
        ),
        out_specs=(P("gx", "gy", None), P("gx", "gy", None), P(("gx", "gy"))),
        check_vma=False,
    )
```

time: 486 us -> 73.1 us (0.15); the launches traced: 480 us -> 72.7 us
  local copies, waits for them, and re-layouts: 141 us -> 4.06 us
  other arithmetic: 115 us -> 0.8 us
  waiting for transfers between devices: 120 us -> 9.9 us
  blocking collectives: 77.2 us -> 33.4 us
  between operations: 14.4 us -> 0.75 us
  starting transfers between devices: 12 us -> 19.7 us
    dynamic_update_slice x64 -> x0, other arithmetic: 81.2 us -> none  [the longest x32 51.3 us: partition_solve(): _, eliminated = lax.scan(eliminate, (zero_rhs, zero_line), device_data)]
    unnamed x1 -> x0, blocking collectives: 77.2 us -> none
    unnamed x3 -> x0, waiting for transfers between devices: 75.2 us -> none
    dynamic_slice x81 -> x0, local copies, waits for them, and re-layouts: 68.2 us -> none  [the longest x80 68.1 us: thomas(): _, (uppers, reduced) = lax.scan(down, start_state, (diagonal, right_sides))]
    all_gather x1 -> x0, waiting for transfers between devices: 44.5 us -> none  [partition_solve(): gathered = lax.all_gather(rims[None], 'gx', axis=0, tiled=True)]
    all_to_all x0 -> x2, blocking collectives: none -> 33.4 us  [the longest x1 21.4 us: local(): blocks = lax.all_to_all(send, 'gx', 0, 0, tiled=True)]
    dynamic_update_slice x64 -> x0, local copies, waits for them, and re-layouts: 33 us -> none  [the longest x48 32.8 us: thomas(): _, (uppers, reduced) = lax.scan(down, start_state, (diagonal, right_sides))]
    add x36 -> x0, other arithmetic: 21.8 us -> none  [the longest x16 16 us: eliminate(): beta_out = local_bottom + left_bottom * (beta_in + gamma_in * tau_now)]
  transfers between devices with their start and end apart: 6 -> 5, of which waited for: 2 -> 2; matrix products, arithmetic and copies ran while one was open for 2% -> 1% of each run, Pallas kernels for 0% -> 0%
where the time goes in v1:
time: 73.1 us; the launch traced here: 72.7 us
  blocking collectives  33.4 us (46%)
  starting transfers between devices  19.7 us (27%)
  waiting for transfers between devices  9.9 us (14%)
  Pallas kernels  4.12 us (6%)
  local copies, waits for them, and re-layouts  4.06 us (6%)
  other arithmetic  0.8 us (1%)
  between operations  0.75 us (1%)
    all_to_all x1, blocking collectives, local(): blocks = lax.all_to_all(send, 'gx', 0, 0, tiled=True)  21.4 us
    all_to_all x1, blocking collectives, local(): back = lax.all_to_all(solved, 'gx', 0, 0, tiled=True)  11.9 us
    all_to_all x1, starting transfers between devices, local(): lax.all_to_all(sums.reshape(groups_x * groups_y, owned_count), ('gx', 'gy...  9.86 us
    all_to_all x1, waiting for transfers between devices, local(): lax.all_to_all(sums.reshape(groups_x * groups_y, owned_count), ('gx', 'gy...  8.39 us
    ppermute x2, starting transfers between devices, from_neighbours(): below = lax.ppermute(high, 'gy', [(i, i + 1) for i in range(ends)])  7.24 us
    pallas_call x5, Pallas kernels, call(): pl.pallas_call(kernel, out_shape=outs, in_specs=[VMEM] * len(operands), o...  4.12 us
    ppermute x2, starting transfers between devices, from_neighbours(): above = lax.ppermute(low, 'gy', [(i + 1, i) for i in range(ends)])  2.58 us
    unnamed x12, local copies, waits for them, and re-layouts  1.92 us
  transfers between devices with their start and end apart: 5, of which 2 were waited for; matrix products, arithmetic and copies ran while one was open for 1% of the time, Pallas kernels for 0%

profile of v1, /device:TPU:1, one launch (start us, length us, event | category | flops | bytes accessed | tf_op | source)
XLA Modules:
  0.0 72.7 jit_solution(6946281648158645220)
XLA Ops:
  0.6 0.0 copy-start
  0.6 1.4 %fusion = (f32[16,1,1024]{2,1,0:T(1,128)S(1)}, f32[16,1,1024]{2,1,0:T(1,128)S(1)}) fusion(f32[16,8,1024]{2,1,0:T(8,128)} %velocity_ref.1), kind=kLoop, calls=%fused_computation.3 | loop fusion | bytes 262144 | tf_op jit(solution)/shard_map/slice | solution.py:203
  2.0 3.9 %collective-permute-start = (f32[16,1024]{1,0:T(8,128)S(1)}, f32[16,1024]{1,0:T(8,128)S(1)}, u32[]{:S(2)}, u32[]{:S(2)}) collective-permute-start(f32[16,1024]{1,0:T(8,128)S(1)} %bitcast.7), channel_id=1, source_target_pairs={{0,1},{1,2},{2,3},{3,4},{4,5},{5,6},{6,7},{7,8},{8,9},{9,10},{10,1... | collective-permute-start | bytes 196616 | tf_op jit(solution)/shard_map/ppermute | solution.py:190
  6.0 1.3 %collective-permute-start.1 = (f32[16,1024]{1,0:T(8,128)S(1)}, f32[16,1024]{1,0:T(8,128)S(1)}, u32[]{:S(2)}, u32[]{:S(2)}) collective-permute-start(f32[16,1024]{1,0:T(8,128)S(1)} %bitcast.8), channel_id=1, source_target_pairs={{1,0},{2,1},{3,2},{4,3},{5,4},{6,5},{7,6},{8,7},{9,8},{10,9},{11,1... | collective-permute-start | bytes 196616 | tf_op jit(solution)/shard_map/ppermute | solution.py:191
  7.3 0.0 copy-start.1
  7.3 1.0 %copy-done.1 = f32[16,8,1024]{2,1,0:T(8,128)S(1)} copy-done((f32[16,8,1024]{2,1,0:T(8,128)S(1)}, f32[16,8,1024]{2,1,0:T(8,128)}, u32[]{:S(2)}) %copy-start.1) | copy-done | bytes 524312
  8.3 0.0 copy-start.3
  8.3 0.8 %copy-done.3 = f32[16,1024]{1,0:T(8,128)S(1)} copy-done((f32[16,1024]{1,0:T(8,128)S(1)}, f32[16,1024]{1,0:T(8,128)}, u32[]{:S(2)}) %copy-start.3) | copy-done | bytes 65560
  9.2 0.3 shard_map.76
  9.5 0.0 collective-permute-done.below_ref
  9.5 1.5 %collective-permute-done.1.above_ref = f32[16,1024]{1,0:T(8,128)S(1)} collective-permute-done((f32[16,1024]{1,0:T(8,128)S(1)}, f32[16,1024]{1,0:T(8,128)S(1)}, u32[]{:S(2)}, u32[]{:S(2)}) %collective-permute-start.1) | collective-permute-done | bytes 65568 | tf_op jit(solution)/shard_map/ppermute | solution.py:191
  11.0 0.0 copy-done
  11.0 0.5 shard_map.77
  11.5 21.4 %all_to_all.19.in_ref = f32[16,7,4,128]{3,2,1,0:T(4,128)S(1)} all-to-all(f32[16,7,4,128]{3,2,1,0:T(4,128)S(1)} %get-tuple-element.17), channel_id=1, replica_groups=mesh['gx'=16,'gy'=16] {'gx'}, dimensions={0} | all-to-all | bytes 458752 | tf_op jit(solution)/shard_map/all_to_all | solution.py:225
  32.9 0.2 shard_map.78
  33.1 0.0 copy-start.2
  33.1 11.9 %all_to_all.20.refs_3_ = f32[16,4,4,128]{3,2,1,0:T(4,128)S(1)} all-to-all(f32[16,4,4,128]{3,2,1,0:T(4,128)S(1)} %shard_map.78), channel_id=1, replica_groups=mesh['gx'=16,'gy'=16] {'gx'}, dimensions={0} | all-to-all | bytes 262144 | tf_op jit(solution)/shard_map/all_to_all | solution.py:232
  45.1 0.0 copy-done.2
  45.1 2.0 %shard_map.79 = (f32[16,8,1024]{2,1,0:T(8,128)}, f32[16,8,1024]{2,1,0:T(8,128)S(1)}, f32[8,128]{1,0:T(8,128)S(1)}, f32[16,1024]{1,0:T(8,128)S(1)}, f32[16,1024]{1,0:T(8,128)S(1)}) custom-call(f32[16,8,1024]{2,1,0:T(8,128)S(1)} %get-tuple-element.13.factor_ref.refs_0_, f32[16,8,1024]{2,1,0:T(8,128)S(1)} %get-tuple-element.14.refs_1_, ...), custom_call_target="tpu_custom_call" | custom-call | tf_op jit(solution)/shard_map/pallas_call | solution.py:177
  47.1 0.8 %all_to_all.14 = f32[256,1,4]{2,0,1:T(8,128)} reshape(f32[8,128]{1,0:T(8,128)S(1)} %get-tuple-element.22) | data formatting | bytes 8192 | tf_op jit(solution)/shard_map/all_to_all | solution.py:252
  47.8 9.9 %all-to-all-start.2 = ((f32[256,1,4]{2,1,0:T(1,128)}), f32[256,1,4]{2,1,0:T(1,128)S(1)}, u32[]{:S(2)}, u32[]{:S(2)}) async-start(f32[256,1,4]{2,1,0:T(1,128)} %bitcast.2), calls=%async_computation.2 | async-start | bytes 262144 | tf_op jit(solution)/shard_map/all_to_all | solution.py:252
  57.7 3.3 %collective-permute-start.2 = (f32[16,1024]{1,0:T(8,128)S(1)}, f32[16,1024]{1,0:T(8,128)S(1)}, u32[]{:S(2)}, u32[]{:S(2)}) collective-permute-start(f32[16,1024]{1,0:T(8,128)S(1)} %get-tuple-element.20), channel_id=1, source_target_pairs={{0,1},{1,2},{2,3},{3,4},{4,5},{5,6},{6,7},{7,8},{8,9},{9,10},{10,1... | collective-permute-start | bytes 196616 | tf_op jit(solution)/shard_map/ppermute | solution.py:190
  61.0 0.0 copy-start.4
  61.0 1.3 %collective-permute-start.3 = (f32[16,1024]{1,0:T(8,128)S(1)}, f32[16,1024]{1,0:T(8,128)S(1)}, u32[]{:S(2)}, u32[]{:S(2)}) collective-permute-start(f32[16,1024]{1,0:T(8,128)S(1)} %get-tuple-element.21), channel_id=1, source_target_pairs={{1,0},{2,1},{3,2},{4,3},{5,4},{6,5},{7,6},{8,7},{9,8},{10,9},{11,1... | collective-permute-start | bytes 196616 | tf_op jit(solution)/shard_map/ppermute | solution.py:191
  62.3 8.4 %all-to-all-done.2 = f32[256,1,4]{2,1,0:T(1,128)S(1)} async-done(((f32[256,1,4]{2,1,0:T(1,128)}), f32[256,1,4]{2,1,0:T(1,128)S(1)}, u32[]{:S(2)}, u32[]{:S(2)}) %all-to-all-start.2) | async-done | bytes 4128 | tf_op jit(solution)/shard_map/all_to_all | solution.py:252
  70.7 0.3 reduce_sum.9
  71.0 0.0 copy-done.4
  71.0 0.5 multiply_multiply_fusion
  71.5 0.0 collective-permute-done.2.below_ref
  71.5 0.0 collective-permute-done.3.above_ref
  71.5 1.2 %shard_map.80 = f32[16,8,1024]{2,1,0:T(8,128)} custom-call(f32[16,8,1024]{2,1,0:T(8,128)S(1)} %get-tuple-element.19.adj_ref, f32[16,1024]{1,0:T(8,128)S(1)} %collective-permute-done.2.below_ref, f32[16,1024]{1,0:T(8,128)S(1)} %collective-permute-done.3.above_ref), custom_call_target="tpu_custom_call" | custom-call | tf_op jit(solution)/shard_map/pallas_call | solution.py:177
  (2 shorter events, 0.0 us)
Async XLA Ops:
  0.6 10.4 %copy-start = (f32[16,8,1024]{2,1,0:T(8,128)S(1)}, f32[16,8,1024]{2,1,0:T(8,128)}, u32[]{:S(2)}) copy-start(f32[16,8,1024]{2,1,0:T(8,128)} %velocity_ref.1) | copy-start | bytes 1572868
  2.0 7.5 %collective-permute-start = (f32[16,1024]{1,0:T(8,128)S(1)}, f32[16,1024]{1,0:T(8,128)S(1)}, u32[]{:S(2)}, u32[]{:S(2)}) collective-permute-start(f32[16,1024]{1,0:T(8,128)S(1)} %bitcast.7), channel_id=1, source_target_pairs={{0,1},{1,2},{2,3},{3,4},{4,5},{5,6},{6,7},{7,8},{8,9},{9,10},{10,1... | collective-permute-start | bytes 196616 | tf_op jit(solution)/shard_map/ppermute | solution.py:190
  6.0 5.0 %collective-permute-start.1 = (f32[16,1024]{1,0:T(8,128)S(1)}, f32[16,1024]{1,0:T(8,128)S(1)}, u32[]{:S(2)}, u32[]{:S(2)}) collective-permute-start(f32[16,1024]{1,0:T(8,128)S(1)} %bitcast.8), channel_id=1, source_target_pairs={{1,0},{2,1},{3,2},{4,3},{5,4},{6,5},{7,6},{8,7},{9,8},{10,9},{11,1... | collective-permute-start | bytes 196616 | tf_op jit(solution)/shard_map/ppermute | solution.py:191
  7.3 1.0 %copy-start.1 = (f32[16,8,1024]{2,1,0:T(8,128)S(1)}, f32[16,8,1024]{2,1,0:T(8,128)}, u32[]{:S(2)}) copy-start(f32[16,8,1024]{2,1,0:T(8,128)} %refs_1_.1) | copy-start | bytes 1572868
  8.3 0.8 %copy-start.3 = (f32[16,1024]{1,0:T(8,128)S(1)}, f32[16,1024]{1,0:T(8,128)}, u32[]{:S(2)}) copy-start(f32[16,1024]{1,0:T(8,128)} %refs_0_.1) | copy-start | bytes 196612
  33.1 12.0 %copy-start.2 = (s32[16,1024]{1,0:T(8,128)S(1)}, s32[16,1024]{1,0:T(8,128)}, u32[]{:S(2)}) copy-start(s32[16,1024]{1,0:T(8,128)} %refs_4_.1) | copy-start | bytes 196612
  47.8 22.9 %all-to-all-start.2 = ((f32[256,1,4]{2,1,0:T(1,128)}), f32[256,1,4]{2,1,0:T(1,128)S(1)}, u32[]{:S(2)}, u32[]{:S(2)}) async-start(f32[256,1,4]{2,1,0:T(1,128)} %bitcast.2), calls=%async_computation.2 | async-start | bytes 262144 | tf_op jit(solution)/shard_map/all_to_all | solution.py:252
  57.7 13.8 %collective-permute-start.2 = (f32[16,1024]{1,0:T(8,128)S(1)}, f32[16,1024]{1,0:T(8,128)S(1)}, u32[]{:S(2)}, u32[]{:S(2)}) collective-permute-start(f32[16,1024]{1,0:T(8,128)S(1)} %get-tuple-element.20), channel_id=1, source_target_pairs={{0,1},{1,2},{2,3},{3,4},{4,5},{5,6},{6,7},{7,8},{8,9},{9,10},{10,1... | collective-permute-start | bytes 196616 | tf_op jit(solution)/shard_map/ppermute | solution.py:190
  61.0 10.0 %copy-start.4 = (s32[4]{0:T(128)S(1)}, s32[4]{0:T(128)}, u32[]{:S(2)}) copy-start(s32[4]{0:T(128)} %param.9) | copy-start | bytes 52
  61.0 10.5 %collective-permute-start.3 = (f32[16,1024]{1,0:T(8,128)S(1)}, f32[16,1024]{1,0:T(8,128)S(1)}, u32[]{:S(2)}, u32[]{:S(2)}) collective-permute-start(f32[16,1024]{1,0:T(8,128)S(1)} %get-tuple-element.21), channel_id=1, source_target_pairs={{1,0},{2,1},{3,2},{4,3},{5,4},{6,5},{7,6},{8,7},{9,8},{10,9},{11,1... | collective-permute-start | bytes 196616 | tf_op jit(solution)/shard_map/ppermute | solution.py:191

commit v2 on v1

--- a/solution.py
+++ b/solution.py
@@ -1,3 +1,4 @@
+import functools
 import math
 
 import jax
@@ -27,6 +28,40 @@
     wall_term = upper + lower - 2.0 * field
     span_term = pltpu.roll(field, 1, 1) + pltpu.roll(field, span - 1, 1) - 2.0 * field
     return field + wall_coef * wall_term + span_coef * span_term
+
+
+def edges(refs, k, field):
+    first_ref, second_ref = refs
+    rows = field.shape[0]
+    even = lax.axis_index("gy") % 2 == 0
+    low, high = field[:1], field[rows - 1 :]
+    first_ref[k : k + 1, :] = jnp.where(even, high, low)
+    second_ref[k : k + 1, :] = jnp.where(even, low, high)
+
+
+def halo(first_ref, second_ref, k):
+    position = lax.axis_index("gy")
+    even = position % 2 == 0
+    inner = (position > 0) & (position < lax.axis_size("gy") - 1)
+    first = first_ref[k : k + 1, :]
+    second = jnp.where(inner, second_ref[k : k + 1, :], 0.0)
+    return jnp.where(even, second, first), jnp.where(even, first, second)
+
+
+def pair_swap(first, second):
+    count = lax.axis_size("gy")
+    inner = [(i, i + 1 if i % 2 else i - 1) for i in range(1, count - 1)]
+    ends = [(0, 0), (count - 1, count - 1)]
+    return (
+        lax.ppermute(first, "gy", [(i, i ^ 1) for i in range(count)]),
+        lax.ppermute(second, "gy", inner + ends),
+    )
+
+
+def edge_kernel(velocity_ref, held_ref, first_ref, second_ref):
+    for k in range(velocity_ref.shape[0]):
+        held_ref[k] = velocity_ref[k]
+        edges((first_ref, second_ref), k, velocity_ref[k])
 
 
 def damping_rows(rows, total_rows):
@@ -61,11 +96,11 @@
     rims_ref[3] = value
 
 
-def velocity_kernel(velocity_ref, below_ref, above_ref, factor_ref, rims_ref, down_ref, send_ref):
+def velocity_kernel(velocity_ref, first_ref, second_ref, factor_ref, rims_ref, down_ref, send_ref):
     planes, rows, span = velocity_ref.shape
     reduced = jnp.zeros((rows, span), F32)
     for k in range(planes):
-        forcing = explicit(velocity_ref[k], below_ref[k : k + 1, :], above_ref[k : k + 1, :])
+        forcing = explicit(velocity_ref[k], *halo(first_ref, second_ref, k))
         reduced = (forcing + reduced) * factor_ref[k]
         down_ref[k] = reduced
     value = reduced
@@ -112,8 +147,8 @@
 
 
 def combine_kernel(
-    stiffness, total_rows, factor_ref, adj_down_ref, down_ref, back_ref, map_ref,
-    new_ref, adj_ref, sums_ref, low_ref, high_ref, left_ref,
+    patch_count, stiffness, total_rows, factor_ref, adj_down_ref, down_ref, back_ref, map_ref,
+    new_ref, adj_ref, sums_ref, first_ref, second_ref, left_ref,
 ):
     planes, rows, span = factor_ref.shape
     half = back_ref.shape[2]
@@ -135,7 +170,8 @@
     for k in range(planes):
         left = left * factor_ref[k]
         left_ref[k] = left
-    patch_rows, patch_lanes = sums_ref.shape
+    patch_rows = 16
+    patch_lanes = patch_count // patch_rows
     row_ids = lax.broadcasted_iota(jnp.int32, (patch_rows, span), 0)
     lane_ids = lax.broadcasted_iota(jnp.int32, (patch_lanes, span), 0)
     total = jnp.zeros((3 * patch_rows, patch_lanes), F32)
@@ -147,8 +183,7 @@
         new = value_v * scale
         adj_ref[k] = adjoint
         new_ref[k] = new
-        low_ref[k : k + 1, :] = adjoint[:1]
-        high_ref[k : k + 1, :] = adjoint[rows - 1 :]
+        edges((first_ref, second_ref), k, adjoint)
         cells = jnp.sum(adjoint * new * damping, axis=0, keepdims=True)
         patches = map_ref[k : k + 1, :]
         first = cells.astype(jnp.bfloat16).astype(F32)
@@ -163,33 +198,43 @@
         total = total + lax.dot_general(
             parts, places, (((1,), (1,)), ((), ())), preferred_element_type=F32
         )
-    sums_ref[...] = (
-        total[:patch_rows] + total[patch_rows : 2 * patch_rows] + total[2 * patch_rows :]
-    )
-
-
-def gradient_kernel(adj_ref, below_ref, above_ref, out_ref):
+    sums = total[:patch_rows] + total[patch_rows : 2 * patch_rows] + total[2 * patch_rows :]
+    merged = LANES // patch_lanes
+    copies = sums_ref.shape[0] * LANES // patch_count
+    for i in range(patch_rows // merged):
+        row = jnp.concatenate([sums[i * merged + j : i * merged + j + 1] for j in range(merged)], axis=1)
+        sums_ref[i * copies : (i + 1) * copies, :] = jnp.broadcast_to(row, (copies, LANES))
+
+
+def gradient_kernel(
+    norm_factor, adj_ref, new_in_ref, first_ref, second_ref, broken_ref, out_ref, new_ref, weight_ref
+):
     for k in range(adj_ref.shape[0]):
-        out_ref[k] = explicit(adj_ref[k], below_ref[k : k + 1, :], above_ref[k : k + 1, :])
-
-
-def call(kernel, outs, scratch, *operands):
+        out_ref[k] = explicit(adj_ref[k], *halo(first_ref, second_ref, k))
+        new_ref[k] = new_in_ref[k]
+    weight_ref[...] = -(1 - broken_ref[...]).astype(F32) * norm_factor
+
+
+def patch_kernel(shares_ref, weight_ref, out_ref):
+    owned = weight_ref.shape[1]
+    per_row = LANES // owned
+    device = lax.axis_index("gx") * lax.axis_size("gy") + lax.axis_index("gy")
+    total = jnp.sum(shares_ref[...], axis=0, keepdims=True)
+    total = jnp.broadcast_to(total, (8, LANES))
+    shift = lax.rem(LANES - owned * lax.rem(device, per_row), LANES)
+    out_ref[...] = weight_ref[...] * pltpu.roll(total, shift, 1)[:1, :owned]
+
+
+def call(kernel, outs, scratch, *operands, cost=None):
     return pl.pallas_call(
         kernel,
         out_shape=outs,
         in_specs=[VMEM] * len(operands),
         out_specs=[VMEM] * len(outs),
-        scratch_shapes=[pltpu.VMEM(dims, F32) for dims in scratch],
+        scratch_shapes=scratch,
+        cost_estimate=cost,
         compiler_params=pltpu.CompilerParams(vmem_limit_bytes=32 * 1024 * 1024),
     )(*operands)
-
-
-def from_neighbours(low, high):
-    count = lax.axis_size("gy")
-    ends = count - 1
-    below = lax.ppermute(high, "gy", [(i, i + 1) for i in range(ends)])
-    above = lax.ppermute(low, "gy", [(i + 1, i) for i in range(ends)])
-    return below, above
 
 
 def local(velocity, cotangent, shape_coef, patch_map, broken):
@@ -199,16 +244,24 @@
     total_rows = rows * groups_y
     stiffness = 3.0 * planes * planes
     field = (planes, rows, span)
+    plane = (planes, span)
     half = rows * span // (groups_x * LANES)
-    below, above = from_neighbours(velocity[:, 0], velocity[:, rows - 1])
 
     def with_sizes(kernel):
         return lambda *refs: kernel(stiffness, total_rows, *refs)
 
+    velocity, first, second = call(
+        edge_kernel, [shape_of(*field), shape_of(*plane), shape_of(*plane)], [], velocity
+    )
+    first, second = pair_swap(first, second)
     factor, adj_down, rims = call(
         with_sizes(matrix_kernel),
-        [shape_of(*field), shape_of(*field), shape_of(5, rows, span)],
-        [field],
+        [
+            shape_of(*field),
+            shape_of(*field),
+            shape_of(5, rows, span),
+        ],
+        [pltpu.VMEM(field, F32)],
         shape_coef,
         cotangent,
     )
@@ -217,8 +270,8 @@
         [shape_of(*field), shape_of(groups_x, 7, half, LANES)],
         [],
         velocity,
-        below,
-        above,
+        first,
+        second,
         factor,
         rims,
     )
@@ -226,38 +279,43 @@
     (solved,) = call(
         reduced_kernel,
         [shape_of(groups_x, 4, half, LANES)],
-        [(groups_x, 6, half, LANES)],
+        [pltpu.VMEM((groups_x, 6, half, LANES), F32)],
         blocks,
     )
     back = lax.all_to_all(solved, "gx", 0, 0, tiled=True)
-    owned_count = broken.shape[0]
-    patch_count = owned_count * groups_x * groups_y
-    new_velocity, adjoint, sums, low, high = call(
-        with_sizes(combine_kernel),
+    owned = broken.shape[0]
+    devices = groups_x * groups_y
+    new, adjoint, sums, first, second = call(
+        with_sizes(functools.partial(combine_kernel, owned * devices)),
         [
             shape_of(*field),
             shape_of(*field),
-            shape_of(patch_count // LANES, LANES),
-            shape_of(planes, span),
-            shape_of(planes, span),
+            shape_of(devices, LANES),
+            shape_of(*plane),
+            shape_of(*plane),
         ],
-        [field],
+        [pltpu.VMEM(field, F32)],
         factor,
         adj_down,
         down,
         back,
         patch_map,
     )
-    below, above = from_neighbours(low, high)
-    shares = lax.all_to_all(
-        sums.reshape(groups_x * groups_y, owned_count), ("gx", "gy"), 0, 0, tiled=True
-    )
-    own_patches = jnp.sum(shares, axis=0)
-    (grad_velocity,) = call(gradient_kernel, [shape_of(*field)], [], adjoint, below, above)
-    norm_factor = 1.0 / math.sqrt(planes * groups_x * total_rows * span / patch_count)
-    keep = (1 - broken).astype(F32)
-    patch_sens = -keep * norm_factor * own_patches
-    return (new_velocity, grad_velocity, patch_sens)
+    first, second = pair_swap(first, second)
+    shares = lax.all_to_all(sums, ("gx", "gy"), 0, 0, tiled=True)
+    norm_factor = 1.0 / math.sqrt(planes * groups_x * total_rows * span / (owned * devices))
+    grad_velocity, new_velocity, weight = call(
+        functools.partial(gradient_kernel, norm_factor),
+        [shape_of(*field), shape_of(*field), shape_of(1, owned)],
+        [],
+        adjoint,
+        new,
+        first,
+        second,
+        broken.reshape(1, owned),
+    )
+    (patch_sens,) = call(patch_kernel, [shape_of(1, owned)], [], shares, weight)
+    return (new_velocity, grad_velocity, patch_sens.reshape(owned))
 
 
 def solution(mesh):

time: 73.1 us -> 68.5 us (0.937)
  starting transfers between devices: 19.7 us -> 17.8 us
  local copies, waits for them, and re-layouts: 4.06 us -> 2.59 us
  waiting for transfers between devices: 9.9 us -> 8.97 us
  Pallas kernels: 4.12 us -> 4.95 us
  other arithmetic: 0.8 us -> 0 us
    ppermute x4, starting transfers between devices: 9.82 us -> 4.9 us  [the longest x2 3.6 us: pair_swap(): lax.ppermute(first, 'gy', [(i, i ^ 1) for i in range(count)])]
    all_to_all x1, starting transfers between devices: 9.86 us -> 12.9 us  [local(): shares = lax.all_to_all(sums, ('gx', 'gy'), 0, 0, tiled=True)]
    slice x1 -> x0, local copies, waits for them, and re-layouts: 1.35 us -> none  [local(): below, above = from_neighbours(velocity[:, 0], velocity[:, rows - 1])]
    all_to_all x1, waiting for transfers between devices: 8.39 us -> 7.42 us  [local(): shares = lax.all_to_all(sums, ('gx', 'gy'), 0, 0, tiled=True)]
    pallas_call x5 -> x7, Pallas kernels: 4.12 us -> 4.95 us  [call(): pl.pallas_call(kernel, out_shape=outs, in_specs=[VMEM] * len(operands), o...]
    all_to_all x1 -> x0, local copies, waits for them, and re-layouts: 0.79 us -> none  [local(): lax.all_to_all(sums.reshape(groups_x * groups_y, owned_count), ('gx', 'gy...]
    unnamed x12 -> x10, local copies, waits for them, and re-layouts: 1.92 us -> 2.59 us
  transfers between devices with their start and end apart: 5 -> 5, of which waited for: 2 -> 2; matrix products, arithmetic and copies ran while one was open for 1% -> 0% of each run, Pallas kernels for 0% -> 2%
where the time goes in v2:
time: 68.5 us; the launch traced here: 68.2 us
  blocking collectives  33.2 us (48%)
  starting transfers between devices  17.8 us (26%)
  waiting for transfers between devices  8.97 us (13%)
  Pallas kernels  4.95 us (7%)
  local copies, waits for them, and re-layouts  2.59 us (4%)
  between operations  0.74 us (1%)
    all_to_all x1, blocking collectives, local(): blocks = lax.all_to_all(send, 'gx', 0, 0, tiled=True)  21.2 us
    all_to_all x1, starting transfers between devices, local(): shares = lax.all_to_all(sums, ('gx', 'gy'), 0, 0, tiled=True)  12.9 us
    all_to_all x1, blocking collectives, local(): back = lax.all_to_all(solved, 'gx', 0, 0, tiled=True)  11.9 us
    all_to_all x1, waiting for transfers between devices, local(): shares = lax.all_to_all(sums, ('gx', 'gy'), 0, 0, tiled=True)  7.42 us
    pallas_call x7, Pallas kernels, call(): pl.pallas_call(kernel, out_shape=outs, in_specs=[VMEM] * len(operands), o...  4.95 us
    ppermute x2, starting transfers between devices, pair_swap(): lax.ppermute(first, 'gy', [(i, i ^ 1) for i in range(count)])  3.6 us
    unnamed x10, local copies, waits for them, and re-layouts  2.59 us
    ppermute x2, waiting for transfers between devices, pair_swap(): lax.ppermute(first, 'gy', [(i, i ^ 1) for i in range(count)])  1.55 us
  transfers between devices with their start and end apart: 5, of which 2 were waited for; matrix products, arithmetic and copies ran while one was open for 0% of the time, Pallas kernels for 2%

profile of v2, /device:TPU:1, one launch (start us, length us, event | category | flops | bytes accessed | tf_op | source)
XLA Modules:
  0.0 68.2 jit_solution(10215241372934363495)
XLA Ops:
  0.6 0.0 copy-start
  0.6 0.0 copy-start.1
  0.6 1.1 %copy-done.1 = f32[16,8,1024]{2,1,0:T(8,128)S(1)} copy-done((f32[16,8,1024]{2,1,0:T(8,128)S(1)}, f32[16,8,1024]{2,1,0:T(8,128)}, u32[]{:S(2)}) %copy-start.1) | copy-done | bytes 524312
  1.7 0.1 shard_map.77
  1.9 2.1 %collective-permute-start = (f32[16,1024]{1,0:T(8,128)S(1)}, f32[16,1024]{1,0:T(8,128)S(1)}, u32[]{:S(2)}, u32[]{:S(2)}) collective-permute-start(f32[16,1024]{1,0:T(8,128)S(1)} %get-tuple-element.22), channel_id=1, source_target_pairs={{0,1},{1,0},{2,3},{3,2},{4,5},{5,4},{6,7},{7,6},{8,9},{9,8},{10,11... | collective-permute-start | bytes 196616 | tf_op jit(solution)/shard_map/ppermute | solution.py:56
  4.0 0.7 collective-permute-start.1
  4.7 0.0 copy-done
  4.7 0.0 copy-start.3
  4.7 0.8 %copy-done.3 = f32[16,1024]{1,0:T(8,128)S(1)} copy-done((f32[16,1024]{1,0:T(8,128)S(1)}, f32[16,1024]{1,0:T(8,128)}, u32[]{:S(2)}) %copy-start.3) | copy-done | bytes 65560
  5.5 0.3 shard_map.76
  5.8 0.0 collective-permute-done.first_ref
  5.8 0.0 collective-permute-done.1.second_ref
  5.8 0.4 shard_map.78
  6.3 21.2 %all_to_all.21.in_ref = f32[16,7,4,128]{3,2,1,0:T(4,128)S(1)} all-to-all(f32[16,7,4,128]{3,2,1,0:T(4,128)S(1)} %get-tuple-element.26), channel_id=1, replica_groups=mesh['gx'=16,'gy'=16] {'gx'}, dimensions={0} | all-to-all | bytes 458752 | tf_op jit(solution)/shard_map/all_to_all | solution.py:278
  27.5 0.2 shard_map.79
  27.7 0.0 copy-start.2
  27.8 11.9 %all_to_all.22.refs_3_ = f32[16,4,4,128]{3,2,1,0:T(4,128)S(1)} all-to-all(f32[16,4,4,128]{3,2,1,0:T(4,128)S(1)} %shard_map.79), channel_id=1, replica_groups=mesh['gx'=16,'gy'=16] {'gx'}, dimensions={0} | all-to-all | bytes 262144 | tf_op jit(solution)/shard_map/all_to_all | solution.py:285
  39.7 0.0 copy-done.2
  39.7 1.9 %shard_map.80 = (f32[16,8,1024]{2,1,0:T(8,128)S(1)}, f32[16,8,1024]{2,1,0:T(8,128)S(1)}, f32[256,128]{1,0:T(8,128)}, f32[16,1024]{1,0:T(8,128)S(1)}, f32[16,1024]{1,0:T(8,128)S(1)}) custom-call(f32[16,8,1024]{2,1,0:T(8,128)S(1)} %get-tuple-element.19.factor_ref.refs_0_, f32[16,8,1024]{2,1,0:T(8,128)S(1)} %get-tuple-element.20.refs_1_, ...), custom_call_target="tpu_custom_call" | custom-call | tf_op jit(solution)/shard_map/pallas_call | solution.py:229
  41.6 12.9 %all-to-all-start.2 = ((f32[256,1,128]{2,1,0:T(1,128)}), f32[256,1,128]{2,1,0:T(1,128)S(1)}, u32[]{:S(2)}, u32[]{:S(2)}) async-start(f32[256,1,128]{2,1,0:T(1,128)} %bitcast.2), calls=%async_computation.2 | async-start | bytes 262144 | tf_op jit(solution)/shard_map/all_to_all | solution.py:305
  54.5 1.5 %collective-permute-start.2 = (f32[16,1024]{1,0:T(8,128)S(1)}, f32[16,1024]{1,0:T(8,128)S(1)}, u32[]{:S(2)}, u32[]{:S(2)}) collective-permute-start(f32[16,1024]{1,0:T(8,128)S(1)} %get-tuple-element.29), channel_id=1, source_target_pairs={{0,1},{1,0},{2,3},{3,2},{4,5},{5,4},{6,7},{7,6},{8,9},{9,8},{10,11... | collective-permute-start | bytes 196616 | tf_op jit(solution)/shard_map/ppermute | solution.py:56
  56.0 0.7 collective-permute-start.3
  56.6 1.5 %collective-permute-done.2.first_ref = f32[16,1024]{1,0:T(8,128)S(1)} collective-permute-done((f32[16,1024]{1,0:T(8,128)S(1)}, f32[16,1024]{1,0:T(8,128)S(1)}, u32[]{:S(2)}, u32[]{:S(2)}) %collective-permute-start.2) | collective-permute-done | bytes 65568 | tf_op jit(solution)/shard_map/ppermute | solution.py:56
  58.2 0.0 collective-permute-done.3.second_ref
  58.2 0.0 copy-start.4
  58.2 0.7 copy-done.4
  58.8 1.3 %shard_map.81 = (f32[16,8,1024]{2,1,0:T(8,128)}, f32[16,8,1024]{2,1,0:T(8,128)}, f32[1,4]{1,0:T(1,128)S(1)}) custom-call(f32[16,8,1024]{2,1,0:T(8,128)S(1)} %get-tuple-element.27.adj_ref, f32[16,8,1024]{2,1,0:T(8,128)S(1)} %get-tuple-element.28.new_in_ref, f32[16,1024]{1,0:T(8,128)S(1)} %collective-permute-done.2.first_ref, ...), custom_call_target="tpu_custom_call" | custom-call | tf_op jit(solution)/shard_map/pallas_call | solution.py:229
  60.1 7.4 %all-to-all-done.2 = f32[256,1,128]{2,1,0:T(1,128)S(1)} async-done(((f32[256,1,128]{2,1,0:T(1,128)}), f32[256,1,128]{2,1,0:T(1,128)S(1)}, u32[]{:S(2)}, u32[]{:S(2)}) %all-to-all-start.2) | async-done | bytes 131104 | tf_op jit(solution)/shard_map/all_to_all | solution.py:305
  67.6 0.6 shard_map.82
Async XLA Ops:
  0.6 4.1 %copy-start = (f32[16,8,1024]{2,1,0:T(8,128)S(1)}, f32[16,8,1024]{2,1,0:T(8,128)}, u32[]{:S(2)}) copy-start(f32[16,8,1024]{2,1,0:T(8,128)} %refs_1_.1) | copy-start | bytes 1572868
  0.6 1.1 %copy-start.1 = (f32[16,8,1024]{2,1,0:T(8,128)S(1)}, f32[16,8,1024]{2,1,0:T(8,128)}, u32[]{:S(2)}) copy-start(f32[16,8,1024]{2,1,0:T(8,128)} %velocity_ref.1) | copy-start | bytes 1572868
  1.9 3.9 %collective-permute-start = (f32[16,1024]{1,0:T(8,128)S(1)}, f32[16,1024]{1,0:T(8,128)S(1)}, u32[]{:S(2)}, u32[]{:S(2)}) collective-permute-start(f32[16,1024]{1,0:T(8,128)S(1)} %get-tuple-element.22), channel_id=1, source_target_pairs={{0,1},{1,0},{2,3},{3,2},{4,5},{5,4},{6,7},{7,6},{8,9},{9,8},{10,11... | collective-permute-start | bytes 196616 | tf_op jit(solution)/shard_map/ppermute | solution.py:56
  4.0 1.8 %collective-permute-start.1 = (f32[16,1024]{1,0:T(8,128)S(1)}, f32[16,1024]{1,0:T(8,128)S(1)}, u32[]{:S(2)}, u32[]{:S(2)}) collective-permute-start(f32[16,1024]{1,0:T(8,128)S(1)} %get-tuple-element.23), channel_id=1, source_target_pairs={{1,2},{2,1},{3,4},{4,3},{5,6},{6,5},{7,8},{8,7},{9,10},{10,9},{11,... | collective-permute-start | bytes 196616 | tf_op jit(solution)/shard_map/ppermute | solution.py:57
  4.7 0.8 %copy-start.3 = (f32[16,1024]{1,0:T(8,128)S(1)}, f32[16,1024]{1,0:T(8,128)}, u32[]{:S(2)}) copy-start(f32[16,1024]{1,0:T(8,128)} %refs_0_.1) | copy-start | bytes 196612
  27.7 12.0 %copy-start.2 = (s32[16,1024]{1,0:T(8,128)S(1)}, s32[16,1024]{1,0:T(8,128)}, u32[]{:S(2)}) copy-start(s32[16,1024]{1,0:T(8,128)} %refs_4_.1) | copy-start | bytes 196612
  41.6 25.9 %all-to-all-start.2 = ((f32[256,1,128]{2,1,0:T(1,128)}), f32[256,1,128]{2,1,0:T(1,128)S(1)}, u32[]{:S(2)}, u32[]{:S(2)}) async-start(f32[256,1,128]{2,1,0:T(1,128)} %bitcast.2), calls=%async_computation.2 | async-start | bytes 262144 | tf_op jit(solution)/shard_map/all_to_all | solution.py:305
  54.5 3.7 %collective-permute-start.2 = (f32[16,1024]{1,0:T(8,128)S(1)}, f32[16,1024]{1,0:T(8,128)S(1)}, u32[]{:S(2)}, u32[]{:S(2)}) collective-permute-start(f32[16,1024]{1,0:T(8,128)S(1)} %get-tuple-element.29), channel_id=1, source_target_pairs={{0,1},{1,0},{2,3},{3,2},{4,5},{5,4},{6,7},{7,6},{8,9},{9,8},{10,11... | collective-permute-start | bytes 196616 | tf_op jit(solution)/shard_map/ppermute | solution.py:56
  56.0 2.2 %collective-permute-start.3 = (f32[16,1024]{1,0:T(8,128)S(1)}, f32[16,1024]{1,0:T(8,128)S(1)}, u32[]{:S(2)}, u32[]{:S(2)}) collective-permute-start(f32[16,1024]{1,0:T(8,128)S(1)} %get-tuple-element.30), channel_id=1, source_target_pairs={{1,2},{2,1},{3,4},{4,3},{5,6},{6,5},{7,8},{8,7},{9,10},{10,9},{11,... | collective-permute-start | bytes 196616 | tf_op jit(solution)/shard_map/ppermute | solution.py:57
  58.2 0.7 copy-start.4

commit v3 on v2

--- a/solution.py
+++ b/solution.py
@@ -96,7 +96,7 @@
     rims_ref[3] = value
 
 
-def velocity_kernel(velocity_ref, first_ref, second_ref, factor_ref, rims_ref, down_ref, send_ref):
+def velocity_kernel(velocity_ref, first_ref, second_ref, factor_ref, rims_ref, down_ref, mine_ref, give_ref):
     planes, rows, span = velocity_ref.shape
     reduced = jnp.zeros((rows, span), F32)
     for k in range(planes):
@@ -106,66 +106,168 @@
     value = reduced
     for k in range(planes - 2, -1, -1):
         value = down_ref[k] + factor_ref[k] * value
-    parts = send_ref.shape[0]
-    half = send_ref.shape[2]
     pieces = [rims_ref[i] for i in range(5)] + [value, reduced]
+    split(half_first(), pieces, mine_ref, give_ref)
+
+
+def place():
+    position = lax.axis_index("gx")
+    return position % 2, position // 2
+
+
+def split(first, pieces, mine_ref, give_ref):
+    width = mine_ref.shape[2]
     for i, piece in enumerate(pieces):
-        for j in range(parts):
-            chunk, side = divmod(j, rows // half)
-            send_ref[j, i] = piece[side * half : (side + 1) * half, chunk * LANES : (chunk + 1) * LANES]
-
-
-def reduced_kernel(in_ref, out_ref, keep_ref):
-    blocks = in_ref.shape[0]
-    tile = in_ref.shape[2:]
-    zero = jnp.zeros(tile, F32)
-    gamma, beta_a, beta_v = zero, zero, zero
-    for i in range(blocks):
-        top, cross, low = in_ref[i, 0], in_ref[i, 1], in_ref[i, 2]
-        top_a, low_a, top_v, low_v = in_ref[i, 3], in_ref[i, 4], in_ref[i, 5], in_ref[i, 6]
-        inverse = 1.0 / (1.0 - top * gamma)
-        tau_a = (top_a + top * beta_a) * inverse
-        tau_v = (top_v + top * beta_v) * inverse
-        sigma = cross * inverse
-        keep_ref[i, 0] = tau_a
-        keep_ref[i, 1] = tau_v
-        keep_ref[i, 2] = sigma
-        keep_ref[i, 3] = gamma
-        keep_ref[i, 4] = beta_a
-        keep_ref[i, 5] = beta_v
-        beta_a = low_a + cross * (beta_a + gamma * tau_a)
-        beta_v = low_v + cross * (beta_v + gamma * tau_v)
-        gamma = low + cross * gamma * sigma
-    next_a, next_v = zero, zero
-    for i in range(blocks - 1, -1, -1):
-        out_ref[i, 1] = next_a
-        out_ref[i, 3] = next_v
-        next_a = keep_ref[i, 0] + keep_ref[i, 2] * next_a
-        next_v = keep_ref[i, 1] + keep_ref[i, 2] * next_v
-        out_ref[i, 0] = keep_ref[i, 4] + keep_ref[i, 3] * next_a
-        out_ref[i, 2] = keep_ref[i, 5] + keep_ref[i, 3] * next_v
+        low, high = piece[:, :width], piece[:, width:]
+        mine_ref[i] = jnp.where(first, low, high)
+        give_ref[i] = jnp.where(first, high, low)
+
+
+def joined(first, mine, other):
+    return jnp.concatenate([jnp.where(first, mine, other), jnp.where(first, other, mine)], axis=1)
+
+
+def merged(is_left, mine_ref, other_ref, tie_ref):
+    left, right = [], []
+    for i in range(7):
+        mine, other = mine_ref[i], other_ref[i]
+        left.append(jnp.where(is_left, mine, other))
+        right.append(jnp.where(is_left, other, mine))
+    top_l, cross_l, low_l, *sides_l = left
+    top_r, cross_r, low_r, *sides_r = right
+    inverse = 1.0 / (1.0 - low_l * top_r)
+    to_left, to_right = cross_l * inverse, cross_r * inverse
+    through_top, through_low = top_r * to_left, low_l * to_right
+    tie_ref[0], tie_ref[1], tie_ref[2], tie_ref[3] = to_left, through_low, through_top, to_right
+    block = [top_l + cross_l * through_top, cross_l * to_right, low_r + cross_r * through_low]
+    for side in range(2):
+        tops_l, lows_l = sides_l[2 * side], sides_l[2 * side + 1]
+        tops_r, lows_r = sides_r[2 * side], sides_r[2 * side + 1]
+        low = (lows_l + low_l * tops_r) * inverse
+        top = (tops_r + top_r * lows_l) * inverse
+        tie_ref[4 + 2 * side], tie_ref[5 + 2 * side] = low, top
+        block += [tops_l + cross_l * top, lows_r + cross_r * low]
+    return block
+
+
+def untied(tie_ref, outer):
+    inner = []
+    for side in range(2):
+        below, above = outer[2 * side], outer[2 * side + 1]
+        low = tie_ref[4 + 2 * side] + tie_ref[0] * below + tie_ref[1] * above
+        top = tie_ref[5 + 2 * side] + tie_ref[2] * below + tie_ref[3] * above
+        inner.append((low, top))
+    (low_a, top_a), (low_v, top_v) = inner
+    return (
+        [outer[0], top_a, outer[2], top_v],
+        [low_a, outer[1], low_v, outer[3]],
+    )
+
+
+def chosen(is_left, pair):
+    return [jnp.where(is_left, x, y) for x, y in zip(*pair)]
+
+
+def half_first():
+    core, chip = place()
+    return (core + chip) % 2 == 0
+
+
+def quarter_first():
+    _, chip = place()
+    return (chip + chip // 2) % 2 == 0
+
+
+def core_kernel(mine_ref, got_ref, tie_ref, keep_ref, give_ref):
+    core, _ = place()
+    split(quarter_first(), merged(core == 0, mine_ref, got_ref, tie_ref), keep_ref, give_ref)
+
+
+def chip_kernel(mine_ref, got_ref, tie_ref, block_ref):
+    _, chip = place()
+    for i, value in enumerate(merged(chip % 2 == 0, mine_ref, got_ref, tie_ref)):
+        block_ref[i] = value
+
+
+def four_kernel(mine_ref, got_ref, tie_ref, rim_ref):
+    _, chip = place()
+    top, _, low, *sides = merged(chip // 2 % 2 == 0, mine_ref, got_ref, tie_ref)
+    is_left = chip < 4
+    rim_ref[0] = jnp.where(is_left, low, top)
+    rim_ref[1] = jnp.where(is_left, sides[1], sides[0])
+    rim_ref[2] = jnp.where(is_left, sides[3], sides[2])
+
+
+def middle_kernel(rim_ref, got_ref, four_tie_ref, chip_tie_ref, mine_ref, give_ref):
+    _, chip = place()
+    is_left = chip < 4
+    rim, got = rim_ref[0], got_ref[0]
+    inverse = 1.0 / (1.0 - rim * got)
+    outer = []
+    for side in (1, 2):
+        across = (got_ref[side] + got * rim_ref[side]) * inverse
+        outer += [jnp.where(is_left, 0.0, across), jnp.where(is_left, across, 0.0)]
+    outer = chosen(chip // 2 % 2 == 0, untied(four_tie_ref, outer))
+    left, right = untied(chip_tie_ref, outer)
+    for i in range(4):
+        mine_ref[i] = jnp.where(chip % 2 == 0, left[i], right[i])
+        give_ref[i] = jnp.where(chip % 2 == 0, right[i], left[i])
+
+
+def spread_kernel(part_ref, got_ref, tie_ref, mine_ref, give_ref):
+    core, _ = place()
+    first = quarter_first()
+    outer = [joined(first, part_ref[i], got_ref[i]) for i in range(4)]
+    left, right = untied(tie_ref, outer)
+    for i in range(4):
+        mine_ref[i] = jnp.where(core == 0, left[i], right[i])
+        give_ref[i] = jnp.where(core == 0, right[i], left[i])
+
+
+def swap(array, distance):
+    pairs = [(i, i ^ distance) for i in range(lax.axis_size("gx"))]
+    return lax.ppermute(array, "gx", pairs)
+
+
+def line_ends(mine, give):
+    rows, width = mine.shape[1:]
+    half = width // 2
+    got = swap(give, 1)
+    core_tie, part, give = call(
+        core_kernel,
+        [shape_of(8, rows, width), shape_of(7, rows, half), shape_of(7, rows, half)],
+        [],
+        mine,
+        got,
+    )
+    got = swap(give, 3)
+    chip_tie, block = call(
+        chip_kernel, [shape_of(8, rows, half), shape_of(7, rows, half)], [], part, got
+    )
+    got = swap(block, 7)
+    four_tie, rim = call(
+        four_kernel, [shape_of(8, rows, half), shape_of(3, rows, half)], [], block, got
+    )
+    got = swap(rim, 15)
+    part, give = call(
+        middle_kernel, [shape_of(4, rows, half)] * 2, [], rim, got, four_tie, chip_tie
+    )
+    got = swap(give, 3)
+    mine, give = call(spread_kernel, [shape_of(4, rows, width)] * 2, [], part, got, core_tie)
+    return mine, swap(give, 1)
 
 
 def combine_kernel(
-    patch_count, stiffness, total_rows, factor_ref, adj_down_ref, down_ref, back_ref, map_ref,
+    patch_count, stiffness, total_rows, factor_ref, adj_down_ref, down_ref, mine_ref, got_ref, map_ref,
     new_ref, adj_ref, sums_ref, first_ref, second_ref, left_ref,
 ):
     planes, rows, span = factor_ref.shape
-    half = back_ref.shape[2]
-    per = rows // half
     damping = damping_rows(rows, total_rows)
     scale = 1.0 / stiffness
 
-    def assembled(i):
-        return jnp.concatenate(
-            [
-                jnp.concatenate([back_ref[chunk * per + side, i] for side in range(per)], axis=0)
-                for chunk in range(span // LANES)
-            ],
-            axis=1,
-        )
-
-    prev_a, value_a, prev_v, value_v = (assembled(i) for i in range(4))
+    prev_a, value_a, prev_v, value_v = (
+        joined(half_first(), mine_ref[i], got_ref[i]) for i in range(4)
+    )
     left = jnp.ones((rows, span), F32)
     for k in range(planes):
         left = left * factor_ref[k]
@@ -225,14 +327,13 @@
     out_ref[...] = weight_ref[...] * pltpu.roll(total, shift, 1)[:1, :owned]
 
 
-def call(kernel, outs, scratch, *operands, cost=None):
+def call(kernel, outs, scratch, *operands):
     return pl.pallas_call(
         kernel,
         out_shape=outs,
         in_specs=[VMEM] * len(operands),
         out_specs=[VMEM] * len(outs),
         scratch_shapes=scratch,
-        cost_estimate=cost,
         compiler_params=pltpu.CompilerParams(vmem_limit_bytes=32 * 1024 * 1024),
     )(*operands)
 
@@ -245,7 +346,6 @@
     stiffness = 3.0 * planes * planes
     field = (planes, rows, span)
     plane = (planes, span)
-    half = rows * span // (groups_x * LANES)
 
     def with_sizes(kernel):
         return lambda *refs: kernel(stiffness, total_rows, *refs)
@@ -265,9 +365,9 @@
         shape_coef,
         cotangent,
     )
-    down, send = call(
+    down, mine, give = call(
         velocity_kernel,
-        [shape_of(*field), shape_of(groups_x, 7, half, LANES)],
+        [shape_of(*field)] + [shape_of(7, rows, span // 2)] * 2,
         [],
         velocity,
         first,
@@ -275,14 +375,7 @@
         factor,
         rims,
     )
-    blocks = lax.all_to_all(send, "gx", 0, 0, tiled=True)
-    (solved,) = call(
-        reduced_kernel,
-        [shape_of(groups_x, 4, half, LANES)],
-        [pltpu.VMEM((groups_x, 6, half, LANES), F32)],
-        blocks,
-    )
-    back = lax.all_to_all(solved, "gx", 0, 0, tiled=True)
+    mine, got = line_ends(mine, give)
     owned = broken.shape[0]
     devices = groups_x * groups_y
     new, adjoint, sums, first, second = call(
@@ -298,7 +391,8 @@
         factor,
         adj_down,
         down,
-        back,
+        mine,
+        got,
         patch_map,
     )
     first, second = pair_swap(first, second)

time: 68.5 us -> 63.7 us (0.930)
  blocking collectives: 33.2 us -> 0 us
  starting transfers between devices: 17.8 us -> 32.8 us
  waiting for transfers between devices: 8.97 us -> 22.5 us
    all_to_all x2 -> x0, blocking collectives: 33.2 us -> none  [the longest x1 21.2 us: local(): blocks = lax.all_to_all(send, 'gx', 0, 0, tiled=True)]
    ppermute x0 -> x6, waiting for transfers between devices: none -> 13.5 us  [swap(): return lax.ppermute(array, 'gx', pairs)]
    ppermute x0 -> x6, starting transfers between devices: none -> 11.4 us  [swap(): return lax.ppermute(array, 'gx', pairs)]
    all_to_all x1, starting transfers between devices: 12.9 us -> 16.5 us  [local(): shares = lax.all_to_all(sums, ('gx', 'gy'), 0, 0, tiled=True)]
    pallas_call x7 -> x11, Pallas kernels: 4.95 us -> 4.88 us  [call(): pl.pallas_call(kernel, out_shape=outs, in_specs=[VMEM] * len(operands), o...]
  transfers between devices with their start and end apart: 5 -> 11, of which waited for: 2 -> 8; matrix products, arithmetic and copies ran while one was open for 0% -> 0% of each run, Pallas kernels for 2% -> 2%
where the time goes in v3:
time: 63.7 us; the launch traced here: 63.5 us
  starting transfers between devices  32.8 us (51%)
  waiting for transfers between devices  22.5 us (35%)
  Pallas kernels  4.88 us (8%)
  local copies, waits for them, and re-layouts  2.59 us (4%)
  between operations  0.76 us (1%)
    all_to_all x1, starting transfers between devices, local(): shares = lax.all_to_all(sums, ('gx', 'gy'), 0, 0, tiled=True)  16.5 us
    ppermute x6, waiting for transfers between devices, swap(): return lax.ppermute(array, 'gx', pairs)  13.5 us
    ppermute x6, starting transfers between devices, swap(): return lax.ppermute(array, 'gx', pairs)  11.4 us
    all_to_all x1, waiting for transfers between devices, local(): shares = lax.all_to_all(sums, ('gx', 'gy'), 0, 0, tiled=True)  7.47 us
    pallas_call x11, Pallas kernels, call(): pl.pallas_call(kernel, out_shape=outs, in_specs=[VMEM] * len(operands), o...  4.88 us
    ppermute x2, starting transfers between devices, pair_swap(): lax.ppermute(first, 'gy', [(i, i ^ 1) for i in range(count)])  3.6 us
    unnamed x10, local copies, waits for them, and re-layouts  2.59 us
    ppermute x2, waiting for transfers between devices, pair_swap(): lax.ppermute(first, 'gy', [(i, i ^ 1) for i in range(count)])  1.5 us
  transfers between devices with their start and end apart: 11, of which 8 were waited for; matrix products, arithmetic and copies ran while one was open for 0% of the time, Pallas kernels for 2%

profile of v3, /device:TPU:1, one launch (start us, length us, event | category | flops | bytes accessed | tf_op | source)
XLA Modules:
  0.0 63.5 jit_solution(8745052017955292978)
XLA Ops:
  0.6 0.0 copy-start
  0.6 0.0 copy-start.1
  0.6 1.1 %copy-done.1 = f32[16,8,1024]{2,1,0:T(8,128)S(1)} copy-done((f32[16,8,1024]{2,1,0:T(8,128)S(1)}, f32[16,8,1024]{2,1,0:T(8,128)}, u32[]{:S(2)}) %copy-start.1) | copy-done | bytes 524312
  1.7 0.1 shard_map.77
  1.9 2.1 %collective-permute-start = (f32[16,1024]{1,0:T(8,128)S(1)}, f32[16,1024]{1,0:T(8,128)S(1)}, u32[]{:S(2)}, u32[]{:S(2)}) collective-permute-start(f32[16,1024]{1,0:T(8,128)S(1)} %get-tuple-element.34), channel_id=1, source_target_pairs={{0,1},{1,0},{2,3},{3,2},{4,5},{5,4},{6,7},{7,6},{8,9},{9,8},{10,11... | collective-permute-start | bytes 196616 | tf_op jit(solution)/shard_map/ppermute | solution.py:56
  4.0 0.7 %collective-permute-start.1 = (f32[16,1024]{1,0:T(8,128)S(1)}, f32[16,1024]{1,0:T(8,128)S(1)}, u32[]{:S(2)}, u32[]{:S(2)}) collective-permute-start(f32[16,1024]{1,0:T(8,128)S(1)} %get-tuple-element.35), channel_id=1, source_target_pairs={{1,2},{2,1},{3,4},{4,3},{5,6},{6,5},{7,8},{8,7},{9,10},{10,9},{11,... | collective-permute-start | bytes 196616 | tf_op jit(solution)/shard_map/ppermute | solution.py:57
  4.7 0.0 copy-done
  4.7 0.0 copy-start.3
  4.7 0.8 %copy-done.3 = f32[16,1024]{1,0:T(8,128)S(1)} copy-done((f32[16,1024]{1,0:T(8,128)S(1)}, f32[16,1024]{1,0:T(8,128)}, u32[]{:S(2)}) %copy-start.3) | copy-done | bytes 65560
  5.5 0.3 shard_map.76
  5.8 0.0 collective-permute-done.first_ref
  5.8 0.0 collective-permute-done.1.second_ref
  5.8 0.4 shard_map.78
  6.3 3.7 %collective-permute-start.2 = (f32[7,8,512]{2,1,0:T(8,128)S(1)}, f32[7,8,512]{2,1,0:T(8,128)S(1)}, u32[]{:S(2)}, u32[]{:S(2)}) collective-permute-start(f32[7,8,512]{2,1,0:T(8,128)S(1)} %get-tuple-element.39), channel_id=1, source_target_pairs={{0,16},{16,0},{32,48},{48,32},{64,80},{80,64},{96,112},{112,96},{1... | collective-permute-start | bytes 344072 | tf_op jit(solution)/shard_map/ppermute | solution.py:229
  10.0 1.0 %collective-permute-done.2.got_ref = f32[7,8,512]{2,1,0:T(8,128)S(1)} collective-permute-done((f32[7,8,512]{2,1,0:T(8,128)S(1)}, f32[7,8,512]{2,1,0:T(8,128)S(1)}, u32[]{:S(2)}, u32[]{:S(2)}) %collective-permute-start.2) | collective-permute-done | bytes 114720 | tf_op jit(solution)/shard_map/ppermute | solution.py:229
  11.0 0.2 collective-permute-start.3
  11.3 3.7 %collective-permute-done.3.got_ref = f32[7,8,256]{2,1,0:T(8,128)S(1)} collective-permute-done((f32[7,8,256]{2,1,0:T(8,128)S(1)}, f32[7,8,256]{2,1,0:T(8,128)S(1)}, u32[]{:S(2)}, u32[]{:S(2)}) %collective-permute-start.3) | collective-permute-done | bytes 57376 | tf_op jit(solution)/shard_map/ppermute | solution.py:229
  15.0 2.9 %collective-permute-start.4 = (f32[7,8,256]{2,1,0:T(8,128)S(1)}, f32[7,8,256]{2,1,0:T(8,128)S(1)}, u32[]{:S(2)}, u32[]{:S(2)}) collective-permute-start(f32[7,8,256]{2,1,0:T(8,128)S(1)} %get-tuple-element.42.mine_ref), channel_id=1, source_target_pairs={{0,112},{16,96},{32,80},{48,64},{64,48},{80,32},{96,16},{112,0},{1... | collective-permute-start | bytes 172040 | tf_op jit(solution)/shard_map/ppermute | solution.py:229
  18.0 2.8 %collective-permute-done.4.got_ref = f32[7,8,256]{2,1,0:T(8,128)S(1)} collective-permute-done((f32[7,8,256]{2,1,0:T(8,128)S(1)}, f32[7,8,256]{2,1,0:T(8,128)S(1)}, u32[]{:S(2)}, u32[]{:S(2)}) %collective-permute-start.4) | collective-permute-done | bytes 57376 | tf_op jit(solution)/shard_map/ppermute | solution.py:229
  20.8 4.2 %collective-permute-start.5 = (f32[3,8,256]{2,1,0:T(8,128)S(1)}, f32[3,8,256]{2,1,0:T(8,128)S(1)}, u32[]{:S(2)}, u32[]{:S(2)}) collective-permute-start(f32[3,8,256]{2,1,0:T(8,128)S(1)} %get-tuple-element.43.rim_ref), channel_id=1, source_target_pairs={{0,240},{16,224},{32,208},{48,192},{64,176},{80,160},{96,144},{112... | collective-permute-start | bytes 73736 | tf_op jit(solution)/shard_map/ppermute | solution.py:229
  25.0 1.5 %collective-permute-done.5.got_ref = f32[3,8,256]{2,1,0:T(8,128)S(1)} collective-permute-done((f32[3,8,256]{2,1,0:T(8,128)S(1)}, f32[3,8,256]{2,1,0:T(8,128)S(1)}, u32[]{:S(2)}, u32[]{:S(2)}) %collective-permute-start.5) | collective-permute-done | bytes 24608 | tf_op jit(solution)/shard_map/ppermute | solution.py:229
  26.5 0.1 collective-permute-start.6
  26.6 3.3 %collective-permute-done.6.got_ref = f32[4,8,256]{2,1,0:T(8,128)S(1)} collective-permute-done((f32[4,8,256]{2,1,0:T(8,128)S(1)}, f32[4,8,256]{2,1,0:T(8,128)S(1)}, u32[]{:S(2)}, u32[]{:S(2)}) %collective-permute-start.6) | collective-permute-done | bytes 32800 | tf_op jit(solution)/shard_map/ppermute | solution.py:229
  30.0 0.0 copy-start.2
  30.0 0.2 collective-permute-start.7
  30.3 1.1 %collective-permute-done.7.refs_4_ = f32[4,8,512]{2,1,0:T(8,128)S(1)} collective-permute-done((f32[4,8,512]{2,1,0:T(8,128)S(1)}, f32[4,8,512]{2,1,0:T(8,128)S(1)}, u32[]{:S(2)}, u32[]{:S(2)}) %collective-permute-start.7) | collective-permute-done | bytes 65568 | tf_op jit(solution)/shard_map/ppermute | solution.py:229
  31.4 0.0 copy-done.2
  31.4 1.9 %shard_map.84 = (f32[16,8,1024]{2,1,0:T(8,128)S(1)}, f32[16,8,1024]{2,1,0:T(8,128)S(1)}, f32[256,128]{1,0:T(8,128)}, f32[16,1024]{1,0:T(8,128)S(1)}, f32[16,1024]{1,0:T(8,128)S(1)}) custom-call(f32[16,8,1024]{2,1,0:T(8,128)S(1)} %get-tuple-element.31.factor_ref.refs_0_, f32[16,8,1024]{2,1,0:T(8,128)S(1)} %get-tuple-element.32.refs_1_, ...), custom_call_target="tpu_custom_call" | custom-call | tf_op jit(solution)/shard_map/pallas_call | solution.py:331
  33.3 16.5 %all-to-all-start = ((f32[256,1,128]{2,1,0:T(1,128)}), f32[256,1,128]{2,1,0:T(1,128)S(1)}, u32[]{:S(2)}, u32[]{:S(2)}) async-start(f32[256,1,128]{2,1,0:T(1,128)} %bitcast.2), calls=%async_computation | async-start | bytes 262144 | tf_op jit(solution)/shard_map/all_to_all | solution.py:399
  49.8 1.5 %collective-permute-start.8 = (f32[16,1024]{1,0:T(8,128)S(1)}, f32[16,1024]{1,0:T(8,128)S(1)}, u32[]{:S(2)}, u32[]{:S(2)}) collective-permute-start(f32[16,1024]{1,0:T(8,128)S(1)} %get-tuple-element.53), channel_id=1, source_target_pairs={{0,1},{1,0},{2,3},{3,2},{4,5},{5,4},{6,7},{7,6},{8,9},{9,8},{10,11... | collective-permute-start | bytes 196616 | tf_op jit(solution)/shard_map/ppermute | solution.py:56
  51.3 0.7 %collective-permute-start.9 = (f32[16,1024]{1,0:T(8,128)S(1)}, f32[16,1024]{1,0:T(8,128)S(1)}, u32[]{:S(2)}, u32[]{:S(2)}) collective-permute-start(f32[16,1024]{1,0:T(8,128)S(1)} %get-tuple-element.54), channel_id=1, source_target_pairs={{1,2},{2,1},{3,4},{4,3},{5,6},{6,5},{7,8},{8,7},{9,10},{10,9},{11,... | collective-permute-start | bytes 196616 | tf_op jit(solution)/shard_map/ppermute | solution.py:57
  51.9 1.5 %collective-permute-done.8.first_ref = f32[16,1024]{1,0:T(8,128)S(1)} collective-permute-done((f32[16,1024]{1,0:T(8,128)S(1)}, f32[16,1024]{1,0:T(8,128)S(1)}, u32[]{:S(2)}, u32[]{:S(2)}) %collective-permute-start.8) | collective-permute-done | bytes 65568 | tf_op jit(solution)/shard_map/ppermute | solution.py:56
  53.4 0.0 collective-permute-done.9.second_ref
  53.4 0.0 copy-start.4
  53.4 0.7 %copy-done.4 = s32[4]{0:T(128)S(1)} copy-done((s32[4]{0:T(128)S(1)}, s32[4]{0:T(128)}, u32[]{:S(2)}) %copy-start.4) | copy-done | bytes 40
  54.1 1.3 %shard_map.85 = (f32[16,8,1024]{2,1,0:T(8,128)}, f32[16,8,1024]{2,1,0:T(8,128)}, f32[1,4]{1,0:T(1,128)S(1)}) custom-call(f32[16,8,1024]{2,1,0:T(8,128)S(1)} %get-tuple-element.51.adj_ref, f32[16,8,1024]{2,1,0:T(8,128)S(1)} %get-tuple-element.52.new_in_ref, f32[16,1024]{1,0:T(8,128)S(1)} %collective-permute-done.8.first_ref, ...), custom_call_target="tpu_custom_call" | custom-call | tf_op jit(solution)/shard_map/pallas_call | solution.py:331
  55.4 7.5 %all-to-all-done = f32[256,1,128]{2,1,0:T(1,128)S(1)} async-done(((f32[256,1,128]{2,1,0:T(1,128)}), f32[256,1,128]{2,1,0:T(1,128)S(1)}, u32[]{:S(2)}, u32[]{:S(2)}) %all-to-all-start) | async-done | bytes 131104 | tf_op jit(solution)/shard_map/all_to_all | solution.py:399
  62.9 0.6 shard_map.86
  (5 shorter events, 0.2 us)
Async XLA Ops:
  0.6 4.1 %copy-start = (f32[16,8,1024]{2,1,0:T(8,128)S(1)}, f32[16,8,1024]{2,1,0:T(8,128)}, u32[]{:S(2)}) copy-start(f32[16,8,1024]{2,1,0:T(8,128)} %refs_1_.1) | copy-start | bytes 1572868
  0.6 1.1 %copy-start.1 = (f32[16,8,1024]{2,1,0:T(8,128)S(1)}, f32[16,8,1024]{2,1,0:T(8,128)}, u32[]{:S(2)}) copy-start(f32[16,8,1024]{2,1,0:T(8,128)} %velocity_ref.1) | copy-start | bytes 1572868
  1.9 3.9 %collective-permute-start = (f32[16,1024]{1,0:T(8,128)S(1)}, f32[16,1024]{1,0:T(8,128)S(1)}, u32[]{:S(2)}, u32[]{:S(2)}) collective-permute-start(f32[16,1024]{1,0:T(8,128)S(1)} %get-tuple-element.34), channel_id=1, source_target_pairs={{0,1},{1,0},{2,3},{3,2},{4,5},{5,4},{6,7},{7,6},{8,9},{9,8},{10,11... | collective-permute-start | bytes 196616 | tf_op jit(solution)/shard_map/ppermute | solution.py:56
  4.0 1.8 %collective-permute-start.1 = (f32[16,1024]{1,0:T(8,128)S(1)}, f32[16,1024]{1,0:T(8,128)S(1)}, u32[]{:S(2)}, u32[]{:S(2)}) collective-permute-start(f32[16,1024]{1,0:T(8,128)S(1)} %get-tuple-element.35), channel_id=1, source_target_pairs={{1,2},{2,1},{3,4},{4,3},{5,6},{6,5},{7,8},{8,7},{9,10},{10,9},{11,... | collective-permute-start | bytes 196616 | tf_op jit(solution)/shard_map/ppermute | solution.py:57
  4.7 0.8 %copy-start.3 = (f32[16,1024]{1,0:T(8,128)S(1)}, f32[16,1024]{1,0:T(8,128)}, u32[]{:S(2)}) copy-start(f32[16,1024]{1,0:T(8,128)} %refs_0_.1) | copy-start | bytes 196612
  6.3 4.7 %collective-permute-start.2 = (f32[7,8,512]{2,1,0:T(8,128)S(1)}, f32[7,8,512]{2,1,0:T(8,128)S(1)}, u32[]{:S(2)}, u32[]{:S(2)}) collective-permute-start(f32[7,8,512]{2,1,0:T(8,128)S(1)} %get-tuple-element.39), channel_id=1, source_target_pairs={{0,16},{16,0},{32,48},{48,32},{64,80},{80,64},{96,112},{112,96},{1... | collective-permute-start | bytes 344072 | tf_op jit(solution)/shard_map/ppermute | solution.py:229
  11.0 4.0 %collective-permute-start.3 = (f32[7,8,256]{2,1,0:T(8,128)S(1)}, f32[7,8,256]{2,1,0:T(8,128)S(1)}, u32[]{:S(2)}, u32[]{:S(2)}) collective-permute-start(f32[7,8,256]{2,1,0:T(8,128)S(1)} %get-tuple-element.41), channel_id=1, source_target_pairs={{0,48},{16,32},{32,16},{48,0},{64,112},{80,96},{96,80},{112,64},{1... | collective-permute-start | bytes 172040 | tf_op jit(solution)/shard_map/ppermute | solution.py:229
  15.0 5.8 %collective-permute-start.4 = (f32[7,8,256]{2,1,0:T(8,128)S(1)}, f32[7,8,256]{2,1,0:T(8,128)S(1)}, u32[]{:S(2)}, u32[]{:S(2)}) collective-permute-start(f32[7,8,256]{2,1,0:T(8,128)S(1)} %get-tuple-element.42.mine_ref), channel_id=1, source_target_pairs={{0,112},{16,96},{32,80},{48,64},{64,48},{80,32},{96,16},{112,0},{1... | collective-permute-start | bytes 172040 | tf_op jit(solution)/shard_map/ppermute | solution.py:229
  20.8 5.7 %collective-permute-start.5 = (f32[3,8,256]{2,1,0:T(8,128)S(1)}, f32[3,8,256]{2,1,0:T(8,128)S(1)}, u32[]{:S(2)}, u32[]{:S(2)}) collective-permute-start(f32[3,8,256]{2,1,0:T(8,128)S(1)} %get-tuple-element.43.rim_ref), channel_id=1, source_target_pairs={{0,240},{16,224},{32,208},{48,192},{64,176},{80,160},{96,144},{112... | collective-permute-start | bytes 73736 | tf_op jit(solution)/shard_map/ppermute | solution.py:229
  26.5 3.4 %collective-permute-start.6 = (f32[4,8,256]{2,1,0:T(8,128)S(1)}, f32[4,8,256]{2,1,0:T(8,128)S(1)}, u32[]{:S(2)}, u32[]{:S(2)}) collective-permute-start(f32[4,8,256]{2,1,0:T(8,128)S(1)} %get-tuple-element.47), channel_id=1, source_target_pairs={{0,48},{16,32},{32,16},{48,0},{64,112},{80,96},{96,80},{112,64},{1... | collective-permute-start | bytes 98312 | tf_op jit(solution)/shard_map/ppermute | solution.py:229
  30.0 1.4 %copy-start.2 = (s32[16,1024]{1,0:T(8,128)S(1)}, s32[16,1024]{1,0:T(8,128)}, u32[]{:S(2)}) copy-start(s32[16,1024]{1,0:T(8,128)} %refs_5_.1) | copy-start | bytes 196612
  30.0 1.3 %collective-permute-start.7 = (f32[4,8,512]{2,1,0:T(8,128)S(1)}, f32[4,8,512]{2,1,0:T(8,128)S(1)}, u32[]{:S(2)}, u32[]{:S(2)}) collective-permute-start(f32[4,8,512]{2,1,0:T(8,128)S(1)} %get-tuple-element.50), channel_id=1, source_target_pairs={{0,16},{16,0},{32,48},{48,32},{64,80},{80,64},{96,112},{112,96},{1... | collective-permute-start | bytes 196616 | tf_op jit(solution)/shard_map/ppermute | solution.py:229
  33.3 29.6 %all-to-all-start = ((f32[256,1,128]{2,1,0:T(1,128)}), f32[256,1,128]{2,1,0:T(1,128)S(1)}, u32[]{:S(2)}, u32[]{:S(2)}) async-start(f32[256,1,128]{2,1,0:T(1,128)} %bitcast.2), calls=%async_computation | async-start | bytes 262144 | tf_op jit(solution)/shard_map/all_to_all | solution.py:399
  49.8 3.6 %collective-permute-start.8 = (f32[16,1024]{1,0:T(8,128)S(1)}, f32[16,1024]{1,0:T(8,128)S(1)}, u32[]{:S(2)}, u32[]{:S(2)}) collective-permute-start(f32[16,1024]{1,0:T(8,128)S(1)} %get-tuple-element.53), channel_id=1, source_target_pairs={{0,1},{1,0},{2,3},{3,2},{4,5},{5,4},{6,7},{7,6},{8,9},{9,8},{10,11... | collective-permute-start | bytes 196616 | tf_op jit(solution)/shard_map/ppermute | solution.py:56
  51.3 2.2 %collective-permute-start.9 = (f32[16,1024]{1,0:T(8,128)S(1)}, f32[16,1024]{1,0:T(8,128)S(1)}, u32[]{:S(2)}, u32[]{:S(2)}) collective-permute-start(f32[16,1024]{1,0:T(8,128)S(1)} %get-tuple-element.54), channel_id=1, source_target_pairs={{1,2},{2,1},{3,4},{4,3},{5,6},{6,5},{7,8},{8,7},{9,10},{10,9},{11,... | collective-permute-start | bytes 196616 | tf_op jit(solution)/shard_map/ppermute | solution.py:57
  53.4 0.7 %copy-start.4 = (s32[4]{0:T(128)S(1)}, s32[4]{0:T(128)}, u32[]{:S(2)}) copy-start(s32[4]{0:T(128)} %param.9) | copy-start | bytes 52

commit v4 on v3

--- a/solution.py
+++ b/solution.py
@@ -14,6 +14,7 @@
 VMEM = pl.BlockSpec(memory_space=pltpu.VMEM)
 F32 = jnp.float32
 LANES = 128
+PATCH_ROWS = 16
 
 
 def shape_of(*dims):
@@ -48,14 +49,23 @@
     return jnp.where(even, second, first), jnp.where(even, first, second)
 
 
+def near_swap(edge):
+    return lax.ppermute(edge, "gy", [(i, i ^ 1) for i in range(lax.axis_size("gy"))])
+
+
+def far_swap(edge):
+    count_x, count = lax.axis_size("gx"), lax.axis_size("gy")
+    pairs = []
+    for i in range(count_x):
+        for j in range(count):
+            target = j + 1 if j % 2 else j - 1
+            inside = 0 <= target < count
+            pairs.append((i * count + j, i * count + target if inside else (i ^ 1) * count + j))
+    return lax.ppermute(edge, ("gx", "gy"), pairs)
+
+
 def pair_swap(first, second):
-    count = lax.axis_size("gy")
-    inner = [(i, i + 1 if i % 2 else i - 1) for i in range(1, count - 1)]
-    ends = [(0, 0), (count - 1, count - 1)]
-    return (
-        lax.ppermute(first, "gy", [(i, i ^ 1) for i in range(count)]),
-        lax.ppermute(second, "gy", inner + ends),
-    )
+    return near_swap(first), far_swap(second)
 
 
 def edge_kernel(velocity_ref, held_ref, first_ref, second_ref):
@@ -70,7 +80,7 @@
     return jnp.exp(-wall_decay * heights / total_rows)
 
 
-def matrix_kernel(stiffness, total_rows, coef_ref, target_ref, factor_ref, adj_down_ref, rims_ref, left_ref):
+def matrix_kernel(stiffness, total_rows, coef_ref, target_ref, factor_ref, adj_down_ref, left_ref, rims_ref):
     planes, rows, span = target_ref.shape
     damping = damping_rows(rows, total_rows)
     factor = jnp.zeros((rows, span), F32)
@@ -96,7 +106,7 @@
     rims_ref[3] = value
 
 
-def velocity_kernel(velocity_ref, first_ref, second_ref, factor_ref, rims_ref, down_ref, mine_ref, give_ref):
+def velocity_kernel(velocity_ref, second_ref, first_ref, factor_ref, rims_ref, down_ref, mine_ref, give_ref):
     planes, rows, span = velocity_ref.shape
     reduced = jnp.zeros((rows, span), F32)
     for k in range(planes):
@@ -253,41 +263,32 @@
         middle_kernel, [shape_of(4, rows, half)] * 2, [], rim, got, four_tie, chip_tie
     )
     got = swap(give, 3)
-    mine, give = call(spread_kernel, [shape_of(4, rows, width)] * 2, [], part, got, core_tie)
-    return mine, swap(give, 1)
-
-
-def combine_kernel(
-    patch_count, stiffness, total_rows, factor_ref, adj_down_ref, down_ref, mine_ref, got_ref, map_ref,
-    new_ref, adj_ref, sums_ref, first_ref, second_ref, left_ref,
-):
-    planes, rows, span = factor_ref.shape
+    return call(spread_kernel, [shape_of(4, rows, width)] * 2, [], part, got, core_tie)
+
+
+def lanes_of(is_mine, width):
+    first = half_first() if is_mine else jnp.logical_not(half_first())
+    return pl.ds(pl.multiple_of(jnp.where(first, 0, width), LANES), width)
+
+
+def back_sweep(lanes, factor_ref, left_ref, down_ref, below, above, scale, out_ref):
+    value = above
+    for k in range(out_ref.shape[0] - 1, -1, -1):
+        value = down_ref[k, :, lanes] + left_ref[k, :, lanes] * below + factor_ref[k, :, lanes] * value
+        out_ref[k] = value * scale
+
+
+def patch_sums(patch_count, total_rows, lanes, map_ref, adj_ref, new_ref):
+    planes, rows, width = adj_ref.shape
     damping = damping_rows(rows, total_rows)
-    scale = 1.0 / stiffness
-
-    prev_a, value_a, prev_v, value_v = (
-        joined(half_first(), mine_ref[i], got_ref[i]) for i in range(4)
-    )
-    left = jnp.ones((rows, span), F32)
+    patch_rows = PATCH_ROWS
+    patch_lanes = patch_count // patch_rows
+    row_ids = lax.broadcasted_iota(jnp.int32, (patch_rows, width), 0)
+    lane_ids = lax.broadcasted_iota(jnp.int32, (patch_lanes, width), 0)
+    total = jnp.zeros((3 * patch_rows, patch_lanes), F32)
     for k in range(planes):
-        left = left * factor_ref[k]
-        left_ref[k] = left
-    patch_rows = 16
-    patch_lanes = patch_count // patch_rows
-    row_ids = lax.broadcasted_iota(jnp.int32, (patch_rows, span), 0)
-    lane_ids = lax.broadcasted_iota(jnp.int32, (patch_lanes, span), 0)
-    total = jnp.zeros((3 * patch_rows, patch_lanes), F32)
-    for k in range(planes - 1, -1, -1):
-        factor, left = factor_ref[k], left_ref[k]
-        value_a = adj_down_ref[k] + left * prev_a + factor * value_a
-        value_v = down_ref[k] + left * prev_v + factor * value_v
-        adjoint = value_a * scale
-        new = value_v * scale
-        adj_ref[k] = adjoint
-        new_ref[k] = new
-        edges((first_ref, second_ref), k, adjoint)
-        cells = jnp.sum(adjoint * new * damping, axis=0, keepdims=True)
-        patches = map_ref[k : k + 1, :]
+        cells = jnp.sum(adj_ref[k] * new_ref[k] * damping, axis=0, keepdims=True)
+        patches = map_ref[k : k + 1, lanes]
         first = cells.astype(jnp.bfloat16).astype(F32)
         rest = cells - first
         second = rest.astype(jnp.bfloat16).astype(F32)
@@ -300,20 +301,59 @@
         total = total + lax.dot_general(
             parts, places, (((1,), (1,)), ((), ())), preferred_element_type=F32
         )
-    sums = total[:patch_rows] + total[patch_rows : 2 * patch_rows] + total[2 * patch_rows :]
-    merged = LANES // patch_lanes
-    copies = sums_ref.shape[0] * LANES // patch_count
-    for i in range(patch_rows // merged):
-        row = jnp.concatenate([sums[i * merged + j : i * merged + j + 1] for j in range(merged)], axis=1)
-        sums_ref[i * copies : (i + 1) * copies, :] = jnp.broadcast_to(row, (copies, LANES))
+    return total[:patch_rows] + total[patch_rows : 2 * patch_rows] + total[2 * patch_rows :]
+
+
+def own_half_kernel(
+    patch_count, stiffness, total_rows, factor_ref, left_ref, adj_down_ref, down_ref, ends_ref, map_ref,
+    adj_ref, new_ref, sums_ref,
+):
+    lanes = lanes_of(True, adj_ref.shape[2])
+    sweep = (lanes, factor_ref, left_ref)
+    back_sweep(*sweep, adj_down_ref, ends_ref[0], ends_ref[1], 1.0 / stiffness, adj_ref)
+    back_sweep(*sweep, down_ref, ends_ref[2], ends_ref[3], 1.0 / stiffness, new_ref)
+    sums_ref[...] = patch_sums(patch_count, total_rows, lanes, map_ref, adj_ref, new_ref)
+
+
+def adjoint_kernel(
+    stiffness, total_rows, factor_ref, left_ref, adj_down_ref, ends_ref, mine_ref,
+    adj_ref, first_ref, second_ref,
+):
+    lanes = lanes_of(False, adj_ref.shape[2])
+    back_sweep(
+        lanes, factor_ref, left_ref, adj_down_ref, ends_ref[0], ends_ref[1], 1.0 / stiffness, adj_ref
+    )
+    for k in range(adj_ref.shape[0]):
+        edges((first_ref, second_ref), k, joined(half_first(), mine_ref[k], adj_ref[k]))
+
+
+def shares_kernel(
+    patch_count, stiffness, total_rows, factor_ref, left_ref, down_ref, ends_ref, map_ref, adj_ref, mine_ref,
+    new_ref, shares_ref,
+):
+    lanes = lanes_of(False, adj_ref.shape[2])
+    back_sweep(
+        lanes, factor_ref, left_ref, down_ref, ends_ref[2], ends_ref[3], 1.0 / stiffness, new_ref
+    )
+    sums = mine_ref[...] + patch_sums(patch_count, total_rows, lanes, map_ref, adj_ref, new_ref)
+    patch_rows, patch_lanes = sums.shape
+    merged_rows = LANES // patch_lanes
+    copies = shares_ref.shape[0] * LANES // patch_count
+    for i in range(patch_rows // merged_rows):
+        row = jnp.concatenate(
+            [sums[i * merged_rows + j : i * merged_rows + j + 1] for j in range(merged_rows)], axis=1
+        )
+        shares_ref[i * copies : (i + 1) * copies, :] = jnp.broadcast_to(row, (copies, LANES))
 
 
 def gradient_kernel(
-    norm_factor, adj_ref, new_in_ref, first_ref, second_ref, broken_ref, out_ref, new_ref, weight_ref
+    norm_factor, adj_ref, adj_got_ref, new_in_ref, new_got_ref, second_ref, first_ref, broken_ref,
+    out_ref, new_ref, weight_ref,
 ):
     for k in range(adj_ref.shape[0]):
-        out_ref[k] = explicit(adj_ref[k], *halo(first_ref, second_ref, k))
-        new_ref[k] = new_in_ref[k]
+        adjoint = joined(half_first(), adj_ref[k], adj_got_ref[k])
+        out_ref[k] = explicit(adjoint, *halo(first_ref, second_ref, k))
+        new_ref[k] = joined(half_first(), new_in_ref[k], new_got_ref[k])
     weight_ref[...] = -(1 - broken_ref[...]).astype(F32) * norm_factor
 
 
@@ -354,14 +394,10 @@
         edge_kernel, [shape_of(*field), shape_of(*plane), shape_of(*plane)], [], velocity
     )
     first, second = pair_swap(first, second)
-    factor, adj_down, rims = call(
+    factor, adj_down, left, rims = call(
         with_sizes(matrix_kernel),
-        [
-            shape_of(*field),
-            shape_of(*field),
-            shape_of(5, rows, span),
-        ],
-        [pltpu.VMEM(field, F32)],
+        [shape_of(*field)] * 3 + [shape_of(5, rows, span)],
+        [],
         shape_coef,
         cotangent,
     )
@@ -370,42 +406,63 @@
         [shape_of(*field)] + [shape_of(7, rows, span // 2)] * 2,
         [],
         velocity,
+        second,
         first,
-        second,
         factor,
         rims,
     )
-    mine, got = line_ends(mine, give)
+    mine, give = line_ends(mine, give)
+    got = swap(give, 1)
     owned = broken.shape[0]
     devices = groups_x * groups_y
-    new, adjoint, sums, first, second = call(
-        with_sizes(functools.partial(combine_kernel, owned * devices)),
-        [
-            shape_of(*field),
-            shape_of(*field),
-            shape_of(devices, LANES),
-            shape_of(*plane),
-            shape_of(*plane),
-        ],
-        [pltpu.VMEM(field, F32)],
+    patch_count = owned * devices
+    half = (planes, rows, span // 2)
+    adj_mine, new_mine, sums = call(
+        with_sizes(functools.partial(own_half_kernel, patch_count)),
+        [shape_of(*half), shape_of(*half), shape_of(PATCH_ROWS, patch_count // PATCH_ROWS)],
+        [],
         factor,
+        left,
         adj_down,
         down,
         mine,
+        patch_map,
+    )
+    adj_got, first, second = call(
+        with_sizes(adjoint_kernel),
+        [shape_of(*half), shape_of(*plane), shape_of(*plane)],
+        [],
+        factor,
+        left,
+        adj_down,
+        got,
+        adj_mine,
+    )
+    first, second = pair_swap(first, second)
+    new_got, sums = call(
+        with_sizes(functools.partial(shares_kernel, patch_count)),
+        [shape_of(*half), shape_of(devices, LANES)],
+        [],
+        factor,
+        left,
+        down,
         got,
         patch_map,
-    )
-    first, second = pair_swap(first, second)
+        adj_got,
+        sums,
+    )
     shares = lax.all_to_all(sums, ("gx", "gy"), 0, 0, tiled=True)
     norm_factor = 1.0 / math.sqrt(planes * groups_x * total_rows * span / (owned * devices))
     grad_velocity, new_velocity, weight = call(
         functools.partial(gradient_kernel, norm_factor),
         [shape_of(*field), shape_of(*field), shape_of(1, owned)],
         [],
-        adjoint,
-        new,
+        adj_mine,
+        adj_got,
+        new_mine,
+        new_got,
+        second,
         first,
-        second,
         broken.reshape(1, owned),
     )
     (patch_sens,) = call(patch_kernel, [shape_of(1, owned)], [], shares, weight)

time: 63.7 us -> 60.7 us (0.953)
  starting transfers between devices: 32.8 us -> 29.5 us
    ppermute x4, waiting for transfers between devices: 1.51 us -> 6.19 us  [the longest x2 5.71 us: near_swap(): lax.ppermute(edge, 'gy', [(i, i ^ 1) for i in range(lax.axis_size('gy'))])]
    all_to_all x1, starting transfers between devices: 16.5 us -> 12.8 us  [local(): shares = lax.all_to_all(sums, ('gx', 'gy'), 0, 0, tiled=True)]
    all_to_all x1, waiting for transfers between devices: 7.47 us -> 4.72 us  [local(): shares = lax.all_to_all(sums, ('gx', 'gy'), 0, 0, tiled=True)]
    ppermute x6, waiting for transfers between devices: 13.5 us -> 11 us  [swap(): return lax.ppermute(array, 'gx', pairs)]
    ppermute x4, starting transfers between devices: 4.9 us -> 6 us  [the longest x2 5.56 us: far_swap(): return lax.ppermute(edge, ('gx', 'gy'), pairs)]
    ppermute x6, starting transfers between devices: 11.4 us -> 10.7 us  [swap(): return lax.ppermute(array, 'gx', pairs)]
    pallas_call x11 -> x13, Pallas kernels: 4.88 us -> 5.16 us  [call(): pl.pallas_call(kernel, out_shape=outs, in_specs=[VMEM] * len(operands), o...]
  transfers between devices with their start and end apart: 11 -> 11, of which waited for: 8 -> 9; matrix products, arithmetic and copies ran while one was open for 0% -> 0% of each run, Pallas kernels for 2% -> 4%
where the time goes in v4:
time: 60.7 us; the launch traced here: 60.4 us
  starting transfers between devices  29.5 us (49%)
  waiting for transfers between devices  21.9 us (36%)
  Pallas kernels  5.16 us (9%)
  local copies, waits for them, and re-layouts  3.13 us (5%)
  between operations  0.73 us (1%)
    all_to_all x1, starting transfers between devices, local(): shares = lax.all_to_all(sums, ('gx', 'gy'), 0, 0, tiled=True)  12.8 us
    ppermute x6, waiting for transfers between devices, swap(): return lax.ppermute(array, 'gx', pairs)  11 us
    ppermute x6, starting transfers between devices, swap(): return lax.ppermute(array, 'gx', pairs)  10.7 us
    ppermute x2, waiting for transfers between devices, near_swap(): lax.ppermute(edge, 'gy', [(i, i ^ 1) for i in range(lax.axis_size('gy'))])  5.71 us
    ppermute x2, starting transfers between devices, far_swap(): return lax.ppermute(edge, ('gx', 'gy'), pairs)  5.56 us
    pallas_call x13, Pallas kernels, call(): pl.pallas_call(kernel, out_shape=outs, in_specs=[VMEM] * len(operands), o...  5.16 us
    all_to_all x1, waiting for transfers between devices, local(): shares = lax.all_to_all(sums, ('gx', 'gy'), 0, 0, tiled=True)  4.72 us
    unnamed x10, local copies, waits for them, and re-layouts  3.13 us
  transfers between devices with their start and end apart: 11, of which 9 were waited for; matrix products, arithmetic and copies ran while one was open for 0% of the time, Pallas kernels for 4%

profile of v4, /device:TPU:1, one launch (start us, length us, event | category | flops | bytes accessed | tf_op | source)
XLA Modules:
  0.0 60.4 jit_solution(42775182620066694)
XLA Ops:
  0.6 0.0 copy-start
  0.6 0.0 copy-start.1
  0.6 1.1 %copy-done.1 = f32[16,8,1024]{2,1,0:T(8,128)S(1)} copy-done((f32[16,8,1024]{2,1,0:T(8,128)S(1)}, f32[16,8,1024]{2,1,0:T(8,128)}, u32[]{:S(2)}) %copy-start.1) | copy-done | bytes 524312
  1.7 0.1 shard_map.77
  1.9 3.3 %collective-permute-start = (f32[16,1024]{1,0:T(8,128)S(1)}, f32[16,1024]{1,0:T(8,128)S(1)}, u32[]{:S(2)}, u32[]{:S(2)}) collective-permute-start(f32[16,1024]{1,0:T(8,128)S(1)} %get-tuple-element.39), channel_id=1, source_target_pairs={{0,16},{1,2},{2,1},{3,4},{4,3},{5,6},{6,5},{7,8},{8,7},{9,10},{10,... | collective-permute-start | bytes 196616 | tf_op jit(solution)/shard_map/ppermute | solution.py:64
  5.2 0.0 collective-permute-start.1
  5.2 0.0 copy-done
  5.2 0.0 copy-start.3
  5.2 0.8 %copy-done.3 = f32[16,1024]{1,0:T(8,128)S(1)} copy-done((f32[16,1024]{1,0:T(8,128)S(1)}, f32[16,1024]{1,0:T(8,128)}, u32[]{:S(2)}) %copy-start.3) | copy-done | bytes 65560
  6.1 0.3 shard_map.76
  6.4 0.0 collective-permute-done.second_ref
  6.4 2.5 %collective-permute-done.1.first_ref = f32[16,1024]{1,0:T(8,128)S(1)} collective-permute-done((f32[16,1024]{1,0:T(8,128)S(1)}, f32[16,1024]{1,0:T(8,128)S(1)}, u32[]{:S(2)}, u32[]{:S(2)}) %collective-permute-start.1) | collective-permute-done | bytes 65568 | tf_op jit(solution)/shard_map/ppermute | solution.py:53
  8.9 0.5 shard_map.78
  9.3 1.0 %collective-permute-start.2 = (f32[7,8,512]{2,1,0:T(8,128)S(1)}, f32[7,8,512]{2,1,0:T(8,128)S(1)}, u32[]{:S(2)}, u32[]{:S(2)}) collective-permute-start(f32[7,8,512]{2,1,0:T(8,128)S(1)} %get-tuple-element.44), channel_id=1, source_target_pairs={{0,16},{16,0},{32,48},{48,32},{64,80},{80,64},{96,112},{112,96},{1... | collective-permute-start | bytes 344072 | tf_op jit(solution)/shard_map/ppermute | solution.py:239
  10.3 1.0 %collective-permute-done.2.got_ref = f32[7,8,512]{2,1,0:T(8,128)S(1)} collective-permute-done((f32[7,8,512]{2,1,0:T(8,128)S(1)}, f32[7,8,512]{2,1,0:T(8,128)S(1)}, u32[]{:S(2)}, u32[]{:S(2)}) %collective-permute-start.2) | collective-permute-done | bytes 114720 | tf_op jit(solution)/shard_map/ppermute | solution.py:239
  11.3 0.9 %collective-permute-start.3 = (f32[7,8,256]{2,1,0:T(8,128)S(1)}, f32[7,8,256]{2,1,0:T(8,128)S(1)}, u32[]{:S(2)}, u32[]{:S(2)}) collective-permute-start(f32[7,8,256]{2,1,0:T(8,128)S(1)} %get-tuple-element.46), channel_id=1, source_target_pairs={{0,48},{16,32},{32,16},{48,0},{64,112},{80,96},{96,80},{112,64},{1... | collective-permute-start | bytes 172040 | tf_op jit(solution)/shard_map/ppermute | solution.py:239
  12.2 3.0 %collective-permute-done.3.got_ref = f32[7,8,256]{2,1,0:T(8,128)S(1)} collective-permute-done((f32[7,8,256]{2,1,0:T(8,128)S(1)}, f32[7,8,256]{2,1,0:T(8,128)S(1)}, u32[]{:S(2)}, u32[]{:S(2)}) %collective-permute-start.3) | collective-permute-done | bytes 57376 | tf_op jit(solution)/shard_map/ppermute | solution.py:239
  15.3 3.6 %collective-permute-start.4 = (f32[7,8,256]{2,1,0:T(8,128)S(1)}, f32[7,8,256]{2,1,0:T(8,128)S(1)}, u32[]{:S(2)}, u32[]{:S(2)}) collective-permute-start(f32[7,8,256]{2,1,0:T(8,128)S(1)} %get-tuple-element.47.mine_ref), channel_id=1, source_target_pairs={{0,112},{16,96},{32,80},{48,64},{64,48},{80,32},{96,16},{112,0},{1... | collective-permute-start | bytes 172040 | tf_op jit(solution)/shard_map/ppermute | solution.py:239
  18.9 2.1 %collective-permute-done.4.got_ref = f32[7,8,256]{2,1,0:T(8,128)S(1)} collective-permute-done((f32[7,8,256]{2,1,0:T(8,128)S(1)}, f32[7,8,256]{2,1,0:T(8,128)S(1)}, u32[]{:S(2)}, u32[]{:S(2)}) %collective-permute-start.4) | collective-permute-done | bytes 57376 | tf_op jit(solution)/shard_map/ppermute | solution.py:239
  21.1 4.9 %collective-permute-start.5 = (f32[3,8,256]{2,1,0:T(8,128)S(1)}, f32[3,8,256]{2,1,0:T(8,128)S(1)}, u32[]{:S(2)}, u32[]{:S(2)}) collective-permute-start(f32[3,8,256]{2,1,0:T(8,128)S(1)} %get-tuple-element.48.rim_ref), channel_id=1, source_target_pairs={{0,240},{16,224},{32,208},{48,192},{64,176},{80,160},{96,144},{112... | collective-permute-start | bytes 73736 | tf_op jit(solution)/shard_map/ppermute | solution.py:239
  26.0 1.5 %collective-permute-done.5.got_ref = f32[3,8,256]{2,1,0:T(8,128)S(1)} collective-permute-done((f32[3,8,256]{2,1,0:T(8,128)S(1)}, f32[3,8,256]{2,1,0:T(8,128)S(1)}, u32[]{:S(2)}, u32[]{:S(2)}) %collective-permute-start.5) | collective-permute-done | bytes 24608 | tf_op jit(solution)/shard_map/ppermute | solution.py:239
  27.5 0.1 collective-permute-start.6
  27.6 3.3 %collective-permute-done.6.got_ref = f32[4,8,256]{2,1,0:T(8,128)S(1)} collective-permute-done((f32[4,8,256]{2,1,0:T(8,128)S(1)}, f32[4,8,256]{2,1,0:T(8,128)S(1)}, u32[]{:S(2)}, u32[]{:S(2)}) %collective-permute-start.6) | collective-permute-done | bytes 32800 | tf_op jit(solution)/shard_map/ppermute | solution.py:239
  30.9 0.0 copy-start.2
  31.0 0.2 collective-permute-start.7
  31.2 0.5 copy-done.2
  31.8 0.6 shard_map.84
  32.4 0.0 collective-permute-done.7.refs_3_
  32.4 0.2 shard_map.85
  32.6 1.3 %shard_map.86 = (f32[16,8,512]{2,1,0:T(8,128)S(1)}, f32[256,128]{1,0:T(8,128)}) custom-call(f32[16,8,1024]{2,1,0:T(8,128)S(1)} %get-tuple-element.35.factor_ref.refs_0_, f32[16,8,1024]{2,1,0:T(8,128)S(1)} %get-tuple-element.36.refs_1_, f32[16,8,1024]{2,1,0:T(8,128)S(1)} %get-tuple-element.42.refs_3_.refs_2_, ...), custom_call_target="tpu_custom_call" | custom-call | tf_op jit(solution)/shard_map/pallas_call | solution.py:371
  33.9 12.8 %all-to-all-start = ((f32[256,1,128]{2,1,0:T(1,128)}), f32[256,1,128]{2,1,0:T(1,128)S(1)}, u32[]{:S(2)}, u32[]{:S(2)}) async-start(f32[256,1,128]{2,1,0:T(1,128)} %bitcast.2), calls=%async_computation | async-start | bytes 262144 | tf_op jit(solution)/shard_map/all_to_all | solution.py:454
  46.8 2.2 %collective-permute-start.8 = (f32[16,1024]{1,0:T(8,128)S(1)}, f32[16,1024]{1,0:T(8,128)S(1)}, u32[]{:S(2)}, u32[]{:S(2)}) collective-permute-start(f32[16,1024]{1,0:T(8,128)S(1)} %get-tuple-element.61), channel_id=1, source_target_pairs={{0,16},{1,2},{2,1},{3,4},{4,3},{5,6},{6,5},{7,8},{8,7},{9,10},{10,... | collective-permute-start | bytes 196616 | tf_op jit(solution)/shard_map/ppermute | solution.py:64
  49.0 0.4 collective-permute-start.9
  49.4 0.5 collective-permute-done.8.second_ref
  49.9 3.2 %collective-permute-done.9.first_ref = f32[16,1024]{1,0:T(8,128)S(1)} collective-permute-done((f32[16,1024]{1,0:T(8,128)S(1)}, f32[16,1024]{1,0:T(8,128)S(1)}, u32[]{:S(2)}, u32[]{:S(2)}) %collective-permute-start.9) | collective-permute-done | bytes 65568 | tf_op jit(solution)/shard_map/ppermute | solution.py:53
  53.1 0.0 copy-start.4
  53.1 0.7 %copy-done.4 = s32[4]{0:T(128)S(1)} copy-done((s32[4]{0:T(128)S(1)}, s32[4]{0:T(128)}, u32[]{:S(2)}) %copy-start.4) | copy-done | bytes 40
  53.8 1.3 %shard_map.87 = (f32[16,8,1024]{2,1,0:T(8,128)}, f32[16,8,1024]{2,1,0:T(8,128)}, f32[1,4]{1,0:T(1,128)S(1)}) custom-call(f32[16,8,512]{2,1,0:T(8,128)S(1)} %get-tuple-element.55.refs_4_.adj_ref, f32[16,8,512]{2,1,0:T(8,128)S(1)} %get-tuple-element.57.refs_5_.adj_got_ref, f32[16,8,512]{2,1,0:T(8,128)S(1)} %get-tuple-element.58.new_in_ref, ...), custom_call_target="tpu_custom_call" | custom-call | tf_op jit(solution)/shard_map/pallas_call | solution.py:371
  55.1 4.7 %all-to-all-done = f32[256,1,128]{2,1,0:T(1,128)S(1)} async-done(((f32[256,1,128]{2,1,0:T(1,128)}), f32[256,1,128]{2,1,0:T(1,128)S(1)}, u32[]{:S(2)}, u32[]{:S(2)}) %all-to-all-start) | async-done | bytes 131104 | tf_op jit(solution)/shard_map/all_to_all | solution.py:454
  59.8 0.6 %shard_map.88 = f32[1,4]{1,0:T(1,128)} custom-call(f32[256,128]{1,0:T(8,128)S(1)} %bitcast.6, f32[1,4]{1,0:T(1,128)S(1)} %get-tuple-element.66.weight_ref), custom_call_target="tpu_custom_call" | custom-call | tf_op jit(solution)/shard_map/pallas_call | solution.py:371
  (5 shorter events, 0.2 us)
Async XLA Ops:
  0.6 4.6 %copy-start = (f32[16,8,1024]{2,1,0:T(8,128)S(1)}, f32[16,8,1024]{2,1,0:T(8,128)}, u32[]{:S(2)}) copy-start(f32[16,8,1024]{2,1,0:T(8,128)} %refs_1_.1) | copy-start | bytes 1572868
  0.6 1.1 %copy-start.1 = (f32[16,8,1024]{2,1,0:T(8,128)S(1)}, f32[16,8,1024]{2,1,0:T(8,128)}, u32[]{:S(2)}) copy-start(f32[16,8,1024]{2,1,0:T(8,128)} %velocity_ref.1) | copy-start | bytes 1572868
  1.9 4.5 %collective-permute-start = (f32[16,1024]{1,0:T(8,128)S(1)}, f32[16,1024]{1,0:T(8,128)S(1)}, u32[]{:S(2)}, u32[]{:S(2)}) collective-permute-start(f32[16,1024]{1,0:T(8,128)S(1)} %get-tuple-element.39), channel_id=1, source_target_pairs={{0,16},{1,2},{2,1},{3,4},{4,3},{5,6},{6,5},{7,8},{8,7},{9,10},{10,... | collective-permute-start | bytes 196616 | tf_op jit(solution)/shard_map/ppermute | solution.py:64
  5.2 3.7 %collective-permute-start.1 = (f32[16,1024]{1,0:T(8,128)S(1)}, f32[16,1024]{1,0:T(8,128)S(1)}, u32[]{:S(2)}, u32[]{:S(2)}) collective-permute-start(f32[16,1024]{1,0:T(8,128)S(1)} %get-tuple-element.40), channel_id=1, source_target_pairs={{0,1},{1,0},{2,3},{3,2},{4,5},{5,4},{6,7},{7,6},{8,9},{9,8},{10,11... | collective-permute-start | bytes 196616 | tf_op jit(solution)/shard_map/ppermute | solution.py:53
  5.2 0.8 %copy-start.3 = (f32[16,1024]{1,0:T(8,128)S(1)}, f32[16,1024]{1,0:T(8,128)}, u32[]{:S(2)}) copy-start(f32[16,1024]{1,0:T(8,128)} %refs_0_.1) | copy-start | bytes 196612
  9.3 1.9 %collective-permute-start.2 = (f32[7,8,512]{2,1,0:T(8,128)S(1)}, f32[7,8,512]{2,1,0:T(8,128)S(1)}, u32[]{:S(2)}, u32[]{:S(2)}) collective-permute-start(f32[7,8,512]{2,1,0:T(8,128)S(1)} %get-tuple-element.44), channel_id=1, source_target_pairs={{0,16},{16,0},{32,48},{48,32},{64,80},{80,64},{96,112},{112,96},{1... | collective-permute-start | bytes 344072 | tf_op jit(solution)/shard_map/ppermute | solution.py:239
  11.3 4.0 %collective-permute-start.3 = (f32[7,8,256]{2,1,0:T(8,128)S(1)}, f32[7,8,256]{2,1,0:T(8,128)S(1)}, u32[]{:S(2)}, u32[]{:S(2)}) collective-permute-start(f32[7,8,256]{2,1,0:T(8,128)S(1)} %get-tuple-element.46), channel_id=1, source_target_pairs={{0,48},{16,32},{32,16},{48,0},{64,112},{80,96},{96,80},{112,64},{1... | collective-permute-start | bytes 172040 | tf_op jit(solution)/shard_map/ppermute | solution.py:239
  15.3 5.8 %collective-permute-start.4 = (f32[7,8,256]{2,1,0:T(8,128)S(1)}, f32[7,8,256]{2,1,0:T(8,128)S(1)}, u32[]{:S(2)}, u32[]{:S(2)}) collective-permute-start(f32[7,8,256]{2,1,0:T(8,128)S(1)} %get-tuple-element.47.mine_ref), channel_id=1, source_target_pairs={{0,112},{16,96},{32,80},{48,64},{64,48},{80,32},{96,16},{112,0},{1... | collective-permute-start | bytes 172040 | tf_op jit(solution)/shard_map/ppermute | solution.py:239
  21.1 6.4 %collective-permute-start.5 = (f32[3,8,256]{2,1,0:T(8,128)S(1)}, f32[3,8,256]{2,1,0:T(8,128)S(1)}, u32[]{:S(2)}, u32[]{:S(2)}) collective-permute-start(f32[3,8,256]{2,1,0:T(8,128)S(1)} %get-tuple-element.48.rim_ref), channel_id=1, source_target_pairs={{0,240},{16,224},{32,208},{48,192},{64,176},{80,160},{96,144},{112... | collective-permute-start | bytes 73736 | tf_op jit(solution)/shard_map/ppermute | solution.py:239
  27.5 3.4 %collective-permute-start.6 = (f32[4,8,256]{2,1,0:T(8,128)S(1)}, f32[4,8,256]{2,1,0:T(8,128)S(1)}, u32[]{:S(2)}, u32[]{:S(2)}) collective-permute-start(f32[4,8,256]{2,1,0:T(8,128)S(1)} %get-tuple-element.52), channel_id=1, source_target_pairs={{0,48},{16,32},{32,16},{48,0},{64,112},{80,96},{96,80},{112,64},{1... | collective-permute-start | bytes 98312 | tf_op jit(solution)/shard_map/ppermute | solution.py:239
  30.9 0.8 %copy-start.2 = (s32[16,1024]{1,0:T(8,128)S(1)}, s32[16,1024]{1,0:T(8,128)}, u32[]{:S(2)}) copy-start(s32[16,1024]{1,0:T(8,128)} %refs_4_.1) | copy-start | bytes 196612
  31.0 1.4 %collective-permute-start.7 = (f32[4,8,512]{2,1,0:T(8,128)S(1)}, f32[4,8,512]{2,1,0:T(8,128)S(1)}, u32[]{:S(2)}, u32[]{:S(2)}) collective-permute-start(f32[4,8,512]{2,1,0:T(8,128)S(1)} %get-tuple-element.56), channel_id=1, source_target_pairs={{0,16},{16,0},{32,48},{48,32},{64,80},{80,64},{96,112},{112,96},{1... | collective-permute-start | bytes 196616 | tf_op jit(solution)/shard_map/ppermute | solution.py:239
  33.9 25.9 %all-to-all-start = ((f32[256,1,128]{2,1,0:T(1,128)}), f32[256,1,128]{2,1,0:T(1,128)S(1)}, u32[]{:S(2)}, u32[]{:S(2)}) async-start(f32[256,1,128]{2,1,0:T(1,128)} %bitcast.2), calls=%async_computation | async-start | bytes 262144 | tf_op jit(solution)/shard_map/all_to_all | solution.py:454
  46.8 3.1 %collective-permute-start.8 = (f32[16,1024]{1,0:T(8,128)S(1)}, f32[16,1024]{1,0:T(8,128)S(1)}, u32[]{:S(2)}, u32[]{:S(2)}) collective-permute-start(f32[16,1024]{1,0:T(8,128)S(1)} %get-tuple-element.61), channel_id=1, source_target_pairs={{0,16},{1,2},{2,1},{3,4},{4,3},{5,6},{6,5},{7,8},{8,7},{9,10},{10,... | collective-permute-start | bytes 196616 | tf_op jit(solution)/shard_map/ppermute | solution.py:64
  49.0 4.1 %collective-permute-start.9 = (f32[16,1024]{1,0:T(8,128)S(1)}, f32[16,1024]{1,0:T(8,128)S(1)}, u32[]{:S(2)}, u32[]{:S(2)}) collective-permute-start(f32[16,1024]{1,0:T(8,128)S(1)} %get-tuple-element.62), channel_id=1, source_target_pairs={{0,1},{1,0},{2,3},{3,2},{4,5},{5,4},{6,7},{7,6},{8,9},{9,8},{10,11... | collective-permute-start | bytes 196616 | tf_op jit(solution)/shard_map/ppermute | solution.py:53
  53.1 0.7 %copy-start.4 = (s32[4]{0:T(128)S(1)}, s32[4]{0:T(128)}, u32[]{:S(2)}) copy-start(s32[4]{0:T(128)} %param.9) | copy-start | bytes 52

commit v5 on v4

--- a/solution.py
+++ b/solution.py
@@ -224,18 +224,28 @@
         give_ref[i] = jnp.where(chip % 2 == 0, right[i], left[i])
 
 
-def spread_kernel(part_ref, got_ref, tie_ref, mine_ref, give_ref):
-    core, _ = place()
+def spread_kernel(low_part_ref, low_got_ref, high_part_ref, high_got_ref, tie_ref, mine_ref, give_ref):
+    core, chip = place()
     first = quarter_first()
-    outer = [joined(first, part_ref[i], got_ref[i]) for i in range(4)]
+    is_low = chip < 4
+    outer = [
+        joined(
+            first,
+            jnp.where(is_low, low_part_ref[i], high_part_ref[i]),
+            jnp.where(is_low, low_got_ref[i], high_got_ref[i]),
+        )
+        for i in range(4)
+    ]
     left, right = untied(tie_ref, outer)
     for i in range(4):
         mine_ref[i] = jnp.where(core == 0, left[i], right[i])
         give_ref[i] = jnp.where(core == 0, right[i], left[i])
 
 
-def swap(array, distance):
-    pairs = [(i, i ^ distance) for i in range(lax.axis_size("gx"))]
+def swap(array, distance, high_distance=None):
+    count = lax.axis_size("gx")
+    high_distance = high_distance or distance
+    pairs = [(i, i ^ (distance if i < count // 2 else high_distance)) for i in range(count)]
     return lax.ppermute(array, "gx", pairs)
 
 
@@ -254,16 +264,18 @@
     chip_tie, block = call(
         chip_kernel, [shape_of(8, rows, half), shape_of(7, rows, half)], [], part, got
     )
-    got = swap(block, 7)
-    four_tie, rim = call(
-        four_kernel, [shape_of(8, rows, half), shape_of(3, rows, half)], [], block, got
-    )
-    got = swap(rim, 15)
-    part, give = call(
-        middle_kernel, [shape_of(4, rows, half)] * 2, [], rim, got, four_tie, chip_tie
-    )
-    got = swap(give, 3)
-    return call(spread_kernel, [shape_of(4, rows, width)] * 2, [], part, got, core_tie)
+    four = [shape_of(8, rows, half), shape_of(3, rows, half)]
+    ends = [shape_of(4, rows, half)] * 2
+    low_tie, low_rim = call(four_kernel, four, [], block, swap(block, 7, 1))
+    from_low = swap(low_rim, 15)
+    high_tie, high_rim = call(four_kernel, four, [], block, swap(block, 1, 7))
+    from_high = swap(high_rim, 15)
+    high_part, give = call(middle_kernel, ends, [], high_rim, from_low, high_tie, chip_tie)
+    high_got = swap(give, 1, 3)
+    low_part, give = call(middle_kernel, ends, [], low_rim, from_high, low_tie, chip_tie)
+    low_got = swap(give, 3, 1)
+    sides = (low_part, low_got, high_part, high_got)
+    return call(spread_kernel, [shape_of(4, rows, width)] * 2, [], *sides, core_tie)
 
 
 def lanes_of(is_mine, width):
@@ -336,14 +348,9 @@
         lanes, factor_ref, left_ref, down_ref, ends_ref[2], ends_ref[3], 1.0 / stiffness, new_ref
     )
     sums = mine_ref[...] + patch_sums(patch_count, total_rows, lanes, map_ref, adj_ref, new_ref)
-    patch_rows, patch_lanes = sums.shape
-    merged_rows = LANES // patch_lanes
-    copies = shares_ref.shape[0] * LANES // patch_count
-    for i in range(patch_rows // merged_rows):
-        row = jnp.concatenate(
-            [sums[i * merged_rows + j : i * merged_rows + j + 1] for j in range(merged_rows)], axis=1
-        )
-        shares_ref[i * copies : (i + 1) * copies, :] = jnp.broadcast_to(row, (copies, LANES))
+    rows_here = sums.shape[0]
+    for i in range(shares_ref.shape[0] // rows_here):
+        shares_ref[i * rows_here : (i + 1) * rows_here, :] = sums
 
 
 def gradient_kernel(
@@ -359,11 +366,10 @@
 
 def patch_kernel(shares_ref, weight_ref, out_ref):
     owned = weight_ref.shape[1]
-    per_row = LANES // owned
-    device = lax.axis_index("gx") * lax.axis_size("gy") + lax.axis_index("gy")
+    width = shares_ref.shape[1]
     total = jnp.sum(shares_ref[...], axis=0, keepdims=True)
-    total = jnp.broadcast_to(total, (8, LANES))
-    shift = lax.rem(LANES - owned * lax.rem(device, per_row), LANES)
+    total = jnp.broadcast_to(jnp.concatenate([total] * (LANES // width), axis=1), (8, LANES))
+    shift = lax.rem(LANES - owned * lax.axis_index("gy"), LANES)
     out_ref[...] = weight_ref[...] * pltpu.roll(total, shift, 1)[:1, :owned]
 
 
@@ -441,7 +447,7 @@
     first, second = pair_swap(first, second)
     new_got, sums = call(
         with_sizes(functools.partial(shares_kernel, patch_count)),
-        [shape_of(*half), shape_of(devices, LANES)],
+        [shape_of(*half), shape_of(devices, patch_count // PATCH_ROWS)],
         [],
         factor,
         left,
@@ -451,7 +457,7 @@
         adj_got,
         sums,
     )
-    shares = lax.all_to_all(sums, ("gx", "gy"), 0, 0, tiled=True)
+    shares = lax.all_to_all(sums, ("gy", "gx"), 0, 0, tiled=True)
     norm_factor = 1.0 / math.sqrt(planes * groups_x * total_rows * span / (owned * devices))
     grad_velocity, new_velocity, weight = call(
         functools.partial(gradient_kernel, norm_factor),

time: 60.7 us -> 58.6 us (0.965)
  waiting for transfers between devices: 21.9 us -> 19.4 us
    ppermute x6 -> x9, starting transfers between devices: 10.7 us -> 13.6 us  [swap(): return lax.ppermute(array, 'gx', pairs)]
    ppermute x6 -> x9, waiting for transfers between devices: 11 us -> 8.65 us  [swap(): return lax.ppermute(array, 'gx', pairs)]
    all_to_all x1, starting transfers between devices: 12.8 us -> 10.5 us  [local(): shares = lax.all_to_all(sums, ('gy', 'gx'), 0, 0, tiled=True)]
    pallas_call x13 -> x15, Pallas kernels: 5.16 us -> 5.22 us  [call(): pl.pallas_call(kernel, out_shape=outs, in_specs=[VMEM] * len(operands), o...]
  transfers between devices with their start and end apart: 11 -> 14, of which waited for: 9 -> 9; matrix products, arithmetic and copies ran while one was open for 0% -> 0% of each run, Pallas kernels for 4% -> 4%
where the time goes in v5:
time: 58.6 us; the launch traced here: 58.3 us
  starting transfers between devices  30.1 us (51%)
  waiting for transfers between devices  19.4 us (33%)
  Pallas kernels  5.22 us (9%)
  local copies, waits for them, and re-layouts  2.94 us (5%)
  between operations  0.74 us (1%)
    ppermute x9, starting transfers between devices, swap(): return lax.ppermute(array, 'gx', pairs)  13.6 us
    all_to_all x1, starting transfers between devices, local(): shares = lax.all_to_all(sums, ('gy', 'gx'), 0, 0, tiled=True)  10.5 us
    ppermute x9, waiting for transfers between devices, swap(): return lax.ppermute(array, 'gx', pairs)  8.65 us
    ppermute x2, waiting for transfers between devices, near_swap(): lax.ppermute(edge, 'gy', [(i, i ^ 1) for i in range(lax.axis_size('gy'))])  5.66 us
    ppermute x2, starting transfers between devices, far_swap(): return lax.ppermute(edge, ('gx', 'gy'), pairs)  5.56 us
    pallas_call x15, Pallas kernels, call(): pl.pallas_call(kernel, out_shape=outs, in_specs=[VMEM] * len(operands), o...  5.22 us
    all_to_all x1, waiting for transfers between devices, local(): shares = lax.all_to_all(sums, ('gy', 'gx'), 0, 0, tiled=True)  4.57 us
    unnamed x10, local copies, waits for them, and re-layouts  2.94 us
  transfers between devices with their start and end apart: 14, of which 9 were waited for; matrix products, arithmetic and copies ran while one was open for 0% of the time, Pallas kernels for 4%

profile of v5, /device:TPU:1, one launch (start us, length us, event | category | flops | bytes accessed | tf_op | source)
XLA Modules:
  0.0 58.3 jit_solution(912676782715345702)
XLA Ops:
  0.6 0.0 copy-start
  0.6 0.0 copy-start.1
  0.6 1.1 %copy-done.1 = f32[16,8,1024]{2,1,0:T(8,128)S(1)} copy-done((f32[16,8,1024]{2,1,0:T(8,128)S(1)}, f32[16,8,1024]{2,1,0:T(8,128)}, u32[]{:S(2)}) %copy-start.1) | copy-done | bytes 524312
  1.7 0.1 shard_map.77
  1.9 3.3 %collective-permute-start = (f32[16,1024]{1,0:T(8,128)S(1)}, f32[16,1024]{1,0:T(8,128)S(1)}, u32[]{:S(2)}, u32[]{:S(2)}) collective-permute-start(f32[16,1024]{1,0:T(8,128)S(1)} %get-tuple-element.43), channel_id=1, source_target_pairs={{0,16},{1,2},{2,1},{3,4},{4,3},{5,6},{6,5},{7,8},{8,7},{9,10},{10,... | collective-permute-start | bytes 196616 | tf_op jit(solution)/shard_map/ppermute | solution.py:64
  5.2 0.0 collective-permute-start.1
  5.2 0.0 copy-done
  5.2 0.0 copy-start.3
  5.2 0.8 %copy-done.3 = f32[16,1024]{1,0:T(8,128)S(1)} copy-done((f32[16,1024]{1,0:T(8,128)S(1)}, f32[16,1024]{1,0:T(8,128)}, u32[]{:S(2)}) %copy-start.3) | copy-done | bytes 65560
  6.1 0.3 shard_map.76
  6.4 0.0 collective-permute-done.second_ref
  6.4 2.5 %collective-permute-done.1.first_ref = f32[16,1024]{1,0:T(8,128)S(1)} collective-permute-done((f32[16,1024]{1,0:T(8,128)S(1)}, f32[16,1024]{1,0:T(8,128)S(1)}, u32[]{:S(2)}, u32[]{:S(2)}) %collective-permute-start.1) | collective-permute-done | bytes 65568 | tf_op jit(solution)/shard_map/ppermute | solution.py:53
  8.9 0.5 shard_map.78
  9.3 1.0 %collective-permute-start.2 = (f32[7,8,512]{2,1,0:T(8,128)S(1)}, f32[7,8,512]{2,1,0:T(8,128)S(1)}, u32[]{:S(2)}, u32[]{:S(2)}) collective-permute-start(f32[7,8,512]{2,1,0:T(8,128)S(1)} %get-tuple-element.48), channel_id=1, source_target_pairs={{0,16},{16,0},{32,48},{48,32},{64,80},{80,64},{96,112},{112,96},{1... | collective-permute-start | bytes 344072 | tf_op jit(solution)/shard_map/ppermute | solution.py:249
  10.3 1.0 %collective-permute-done.2.got_ref = f32[7,8,512]{2,1,0:T(8,128)S(1)} collective-permute-done((f32[7,8,512]{2,1,0:T(8,128)S(1)}, f32[7,8,512]{2,1,0:T(8,128)S(1)}, u32[]{:S(2)}, u32[]{:S(2)}) %collective-permute-start.2) | collective-permute-done | bytes 114720 | tf_op jit(solution)/shard_map/ppermute | solution.py:249
  11.3 0.9 %collective-permute-start.3 = (f32[7,8,256]{2,1,0:T(8,128)S(1)}, f32[7,8,256]{2,1,0:T(8,128)S(1)}, u32[]{:S(2)}, u32[]{:S(2)}) collective-permute-start(f32[7,8,256]{2,1,0:T(8,128)S(1)} %get-tuple-element.50), channel_id=1, source_target_pairs={{0,48},{16,32},{32,16},{48,0},{64,112},{80,96},{96,80},{112,64},{1... | collective-permute-start | bytes 172040 | tf_op jit(solution)/shard_map/ppermute | solution.py:249
  12.2 3.0 %collective-permute-done.3.got_ref = f32[7,8,256]{2,1,0:T(8,128)S(1)} collective-permute-done((f32[7,8,256]{2,1,0:T(8,128)S(1)}, f32[7,8,256]{2,1,0:T(8,128)S(1)}, u32[]{:S(2)}, u32[]{:S(2)}) %collective-permute-start.3) | collective-permute-done | bytes 57376 | tf_op jit(solution)/shard_map/ppermute | solution.py:249
  15.3 3.6 %collective-permute-start.4 = (f32[7,8,256]{2,1,0:T(8,128)S(1)}, f32[7,8,256]{2,1,0:T(8,128)S(1)}, u32[]{:S(2)}, u32[]{:S(2)}) collective-permute-start(f32[7,8,256]{2,1,0:T(8,128)S(1)} %get-tuple-element.51.mine_ref), channel_id=1, source_target_pairs={{0,112},{16,96},{32,80},{48,64},{64,48},{80,32},{96,16},{112,0},{1... | collective-permute-start | bytes 172040 | tf_op jit(solution)/shard_map/ppermute | solution.py:249
  18.9 0.2 collective-permute-start.5
  19.1 2.0 %collective-permute-done.4.got_ref = f32[7,8,256]{2,1,0:T(8,128)S(1)} collective-permute-done((f32[7,8,256]{2,1,0:T(8,128)S(1)}, f32[7,8,256]{2,1,0:T(8,128)S(1)}, u32[]{:S(2)}, u32[]{:S(2)}) %collective-permute-start.4) | collective-permute-done | bytes 57376 | tf_op jit(solution)/shard_map/ppermute | solution.py:249
  21.1 1.2 %collective-permute-start.8 = (f32[3,8,256]{2,1,0:T(8,128)S(1)}, f32[3,8,256]{2,1,0:T(8,128)S(1)}, u32[]{:S(2)}, u32[]{:S(2)}) collective-permute-start(f32[3,8,256]{2,1,0:T(8,128)S(1)} %get-tuple-element.52.rim_ref), channel_id=1, source_target_pairs={{0,240},{16,224},{32,208},{48,192},{64,176},{80,160},{96,144},{112... | collective-permute-start | bytes 73736 | tf_op jit(solution)/shard_map/ppermute | solution.py:249
  22.3 0.0 collective-permute-done.5.got_ref
  22.4 3.7 %collective-permute-start.6 = (f32[3,8,256]{2,1,0:T(8,128)S(1)}, f32[3,8,256]{2,1,0:T(8,128)S(1)}, u32[]{:S(2)}, u32[]{:S(2)}) collective-permute-start(f32[3,8,256]{2,1,0:T(8,128)S(1)} %get-tuple-element.53.rim_ref), channel_id=1, source_target_pairs={{0,240},{16,224},{32,208},{48,192},{64,176},{80,160},{96,144},{112... | collective-permute-start | bytes 73736 | tf_op jit(solution)/shard_map/ppermute | solution.py:249
  26.0 0.0 collective-permute-done.8.got_ref
  26.1 0.4 collective-permute-start.9
  26.5 1.0 %collective-permute-done.6.got_ref = f32[3,8,256]{2,1,0:T(8,128)S(1)} collective-permute-done((f32[3,8,256]{2,1,0:T(8,128)S(1)}, f32[3,8,256]{2,1,0:T(8,128)S(1)}, u32[]{:S(2)}, u32[]{:S(2)}) %collective-permute-start.6) | collective-permute-done | bytes 24608 | tf_op jit(solution)/shard_map/ppermute | solution.py:249
  27.6 2.1 %collective-permute-start.7 = (f32[4,8,256]{2,1,0:T(8,128)S(1)}, f32[4,8,256]{2,1,0:T(8,128)S(1)}, u32[]{:S(2)}, u32[]{:S(2)}) collective-permute-start(f32[4,8,256]{2,1,0:T(8,128)S(1)} %get-tuple-element.57), channel_id=1, source_target_pairs={{0,48},{16,32},{32,16},{48,0},{64,112},{80,96},{96,80},{112,64},{1... | collective-permute-start | bytes 98312 | tf_op jit(solution)/shard_map/ppermute | solution.py:249
  29.7 0.0 collective-permute-done.9.high_got_ref
  29.7 1.6 %collective-permute-done.7.low_got_ref = f32[4,8,256]{2,1,0:T(8,128)S(1)} collective-permute-done((f32[4,8,256]{2,1,0:T(8,128)S(1)}, f32[4,8,256]{2,1,0:T(8,128)S(1)}, u32[]{:S(2)}, u32[]{:S(2)}) %collective-permute-start.7) | collective-permute-done | bytes 32800 | tf_op jit(solution)/shard_map/ppermute | solution.py:249
  31.3 0.0 copy-start.2
  31.4 0.4 collective-permute-start.10
  31.8 0.4 copy-done.2
  32.2 0.6 shard_map.86
  32.7 0.0 collective-permute-done.10.refs_3_
  32.8 0.2 shard_map.87
  33.0 1.3 %shard_map.88 = (f32[16,8,512]{2,1,0:T(8,128)S(1)}, f32[256,64]{1,0:T(8,128)}) custom-call(f32[16,8,1024]{2,1,0:T(8,128)S(1)} %get-tuple-element.39.factor_ref.refs_0_, f32[16,8,1024]{2,1,0:T(8,128)S(1)} %get-tuple-element.40.refs_1_, f32[16,8,1024]{2,1,0:T(8,128)S(1)} %get-tuple-element.46.refs_3_.refs_2_, ...), custom_call_target="tpu_custom_call" | custom-call | tf_op jit(solution)/shard_map/pallas_call | solution.py:377
  34.2 10.5 %all-to-all-start = ((f32[256,1,64]{2,1,0:T(1,128)}), f32[256,1,64]{2,1,0:T(1,128)S(1)}, u32[]{:S(2)}, u32[]{:S(2)}) async-start(f32[256,1,64]{2,1,0:T(1,128)} %bitcast.2), calls=%async_computation | async-start | bytes 262144 | tf_op jit(solution)/shard_map/all_to_all | solution.py:460
  44.8 2.2 %collective-permute-start.11 = (f32[16,1024]{1,0:T(8,128)S(1)}, f32[16,1024]{1,0:T(8,128)S(1)}, u32[]{:S(2)}, u32[]{:S(2)}) collective-permute-start(f32[16,1024]{1,0:T(8,128)S(1)} %get-tuple-element.69), channel_id=1, source_target_pairs={{0,16},{1,2},{2,1},{3,4},{4,3},{5,6},{6,5},{7,8},{8,7},{9,10},{10,... | collective-permute-start | bytes 196616 | tf_op jit(solution)/shard_map/ppermute | solution.py:64
  47.0 0.4 collective-permute-start.12
  47.4 0.5 collective-permute-done.11.second_ref
  47.9 3.2 %collective-permute-done.12.first_ref = f32[16,1024]{1,0:T(8,128)S(1)} collective-permute-done((f32[16,1024]{1,0:T(8,128)S(1)}, f32[16,1024]{1,0:T(8,128)S(1)}, u32[]{:S(2)}, u32[]{:S(2)}) %collective-permute-start.12) | collective-permute-done | bytes 65568 | tf_op jit(solution)/shard_map/ppermute | solution.py:53
  51.1 0.0 copy-start.4
  51.1 0.7 %copy-done.4 = s32[4]{0:T(128)S(1)} copy-done((s32[4]{0:T(128)S(1)}, s32[4]{0:T(128)}, u32[]{:S(2)}) %copy-start.4) | copy-done | bytes 40
  51.7 1.3 %shard_map.89 = (f32[16,8,1024]{2,1,0:T(8,128)}, f32[16,8,1024]{2,1,0:T(8,128)}, f32[1,4]{1,0:T(1,128)S(1)}) custom-call(f32[16,8,512]{2,1,0:T(8,128)S(1)} %get-tuple-element.63.refs_4_.adj_ref, f32[16,8,512]{2,1,0:T(8,128)S(1)} %get-tuple-element.65.refs_5_.adj_got_ref, f32[16,8,512]{2,1,0:T(8,128)S(1)} %get-tuple-element.66.new_in_ref, ...), custom_call_target="tpu_custom_call" | custom-call | tf_op jit(solution)/shard_map/pallas_call | solution.py:377
  53.1 4.6 %all-to-all-done = f32[256,1,64]{2,1,0:T(1,128)S(1)} async-done(((f32[256,1,64]{2,1,0:T(1,128)}), f32[256,1,64]{2,1,0:T(1,128)S(1)}, u32[]{:S(2)}, u32[]{:S(2)}) %all-to-all-start) | async-done | bytes 65568 | tf_op jit(solution)/shard_map/all_to_all | solution.py:460
  57.7 0.7 %shard_map.90 = f32[1,4]{1,0:T(1,128)} custom-call(f32[256,64]{1,0:T(8,128)S(1)} %bitcast.6, f32[1,4]{1,0:T(1,128)S(1)} %get-tuple-element.74.weight_ref), custom_call_target="tpu_custom_call" | custom-call | tf_op jit(solution)/shard_map/pallas_call | solution.py:377
  (7 shorter events, 0.2 us)
Async XLA Ops:
  0.6 4.6 %copy-start = (f32[16,8,1024]{2,1,0:T(8,128)S(1)}, f32[16,8,1024]{2,1,0:T(8,128)}, u32[]{:S(2)}) copy-start(f32[16,8,1024]{2,1,0:T(8,128)} %refs_1_.1) | copy-start | bytes 1572868
  0.6 1.1 %copy-start.1 = (f32[16,8,1024]{2,1,0:T(8,128)S(1)}, f32[16,8,1024]{2,1,0:T(8,128)}, u32[]{:S(2)}) copy-start(f32[16,8,1024]{2,1,0:T(8,128)} %velocity_ref.1) | copy-start | bytes 1572868
  1.9 4.5 %collective-permute-start = (f32[16,1024]{1,0:T(8,128)S(1)}, f32[16,1024]{1,0:T(8,128)S(1)}, u32[]{:S(2)}, u32[]{:S(2)}) collective-permute-start(f32[16,1024]{1,0:T(8,128)S(1)} %get-tuple-element.43), channel_id=1, source_target_pairs={{0,16},{1,2},{2,1},{3,4},{4,3},{5,6},{6,5},{7,8},{8,7},{9,10},{10,... | collective-permute-start | bytes 196616 | tf_op jit(solution)/shard_map/ppermute | solution.py:64
  5.2 3.7 %collective-permute-start.1 = (f32[16,1024]{1,0:T(8,128)S(1)}, f32[16,1024]{1,0:T(8,128)S(1)}, u32[]{:S(2)}, u32[]{:S(2)}) collective-permute-start(f32[16,1024]{1,0:T(8,128)S(1)} %get-tuple-element.44), channel_id=1, source_target_pairs={{0,1},{1,0},{2,3},{3,2},{4,5},{5,4},{6,7},{7,6},{8,9},{9,8},{10,11... | collective-permute-start | bytes 196616 | tf_op jit(solution)/shard_map/ppermute | solution.py:53
  5.2 0.8 %copy-start.3 = (f32[16,1024]{1,0:T(8,128)S(1)}, f32[16,1024]{1,0:T(8,128)}, u32[]{:S(2)}) copy-start(f32[16,1024]{1,0:T(8,128)} %refs_0_.1) | copy-start | bytes 196612
  9.3 1.9 %collective-permute-start.2 = (f32[7,8,512]{2,1,0:T(8,128)S(1)}, f32[7,8,512]{2,1,0:T(8,128)S(1)}, u32[]{:S(2)}, u32[]{:S(2)}) collective-permute-start(f32[7,8,512]{2,1,0:T(8,128)S(1)} %get-tuple-element.48), channel_id=1, source_target_pairs={{0,16},{16,0},{32,48},{48,32},{64,80},{80,64},{96,112},{112,96},{1... | collective-permute-start | bytes 344072 | tf_op jit(solution)/shard_map/ppermute | solution.py:249
  11.3 4.0 %collective-permute-start.3 = (f32[7,8,256]{2,1,0:T(8,128)S(1)}, f32[7,8,256]{2,1,0:T(8,128)S(1)}, u32[]{:S(2)}, u32[]{:S(2)}) collective-permute-start(f32[7,8,256]{2,1,0:T(8,128)S(1)} %get-tuple-element.50), channel_id=1, source_target_pairs={{0,48},{16,32},{32,16},{48,0},{64,112},{80,96},{96,80},{112,64},{1... | collective-permute-start | bytes 172040 | tf_op jit(solution)/shard_map/ppermute | solution.py:249
  15.3 5.8 %collective-permute-start.4 = (f32[7,8,256]{2,1,0:T(8,128)S(1)}, f32[7,8,256]{2,1,0:T(8,128)S(1)}, u32[]{:S(2)}, u32[]{:S(2)}) collective-permute-start(f32[7,8,256]{2,1,0:T(8,128)S(1)} %get-tuple-element.51.mine_ref), channel_id=1, source_target_pairs={{0,112},{16,96},{32,80},{48,64},{64,48},{80,32},{96,16},{112,0},{1... | collective-permute-start | bytes 172040 | tf_op jit(solution)/shard_map/ppermute | solution.py:249
  18.9 3.4 %collective-permute-start.5 = (f32[7,8,256]{2,1,0:T(8,128)S(1)}, f32[7,8,256]{2,1,0:T(8,128)S(1)}, u32[]{:S(2)}, u32[]{:S(2)}) collective-permute-start(f32[7,8,256]{2,1,0:T(8,128)S(1)} %get-tuple-element.51.mine_ref), channel_id=1, source_target_pairs={{0,16},{16,0},{32,48},{48,32},{64,80},{80,64},{96,112},{112,96},{1... | collective-permute-start | bytes 172040 | tf_op jit(solution)/shard_map/ppermute | solution.py:249
  21.1 4.9 %collective-permute-start.8 = (f32[3,8,256]{2,1,0:T(8,128)S(1)}, f32[3,8,256]{2,1,0:T(8,128)S(1)}, u32[]{:S(2)}, u32[]{:S(2)}) collective-permute-start(f32[3,8,256]{2,1,0:T(8,128)S(1)} %get-tuple-element.52.rim_ref), channel_id=1, source_target_pairs={{0,240},{16,224},{32,208},{48,192},{64,176},{80,160},{96,144},{112... | collective-permute-start | bytes 73736 | tf_op jit(solution)/shard_map/ppermute | solution.py:249
  22.4 5.2 %collective-permute-start.6 = (f32[3,8,256]{2,1,0:T(8,128)S(1)}, f32[3,8,256]{2,1,0:T(8,128)S(1)}, u32[]{:S(2)}, u32[]{:S(2)}) collective-permute-start(f32[3,8,256]{2,1,0:T(8,128)S(1)} %get-tuple-element.53.rim_ref), channel_id=1, source_target_pairs={{0,240},{16,224},{32,208},{48,192},{64,176},{80,160},{96,144},{112... | collective-permute-start | bytes 73736 | tf_op jit(solution)/shard_map/ppermute | solution.py:249
  26.1 3.6 %collective-permute-start.9 = (f32[4,8,256]{2,1,0:T(8,128)S(1)}, f32[4,8,256]{2,1,0:T(8,128)S(1)}, u32[]{:S(2)}, u32[]{:S(2)}) collective-permute-start(f32[4,8,256]{2,1,0:T(8,128)S(1)} %get-tuple-element.60), channel_id=1, source_target_pairs={{0,16},{16,0},{32,48},{48,32},{64,80},{80,64},{96,112},{112,96},{1... | collective-permute-start | bytes 98312 | tf_op jit(solution)/shard_map/ppermute | solution.py:249
  27.6 3.7 %collective-permute-start.7 = (f32[4,8,256]{2,1,0:T(8,128)S(1)}, f32[4,8,256]{2,1,0:T(8,128)S(1)}, u32[]{:S(2)}, u32[]{:S(2)}) collective-permute-start(f32[4,8,256]{2,1,0:T(8,128)S(1)} %get-tuple-element.57), channel_id=1, source_target_pairs={{0,48},{16,32},{32,16},{48,0},{64,112},{80,96},{96,80},{112,64},{1... | collective-permute-start | bytes 98312 | tf_op jit(solution)/shard_map/ppermute | solution.py:249
  31.3 0.8 %copy-start.2 = (s32[16,1024]{1,0:T(8,128)S(1)}, s32[16,1024]{1,0:T(8,128)}, u32[]{:S(2)}) copy-start(s32[16,1024]{1,0:T(8,128)} %refs_4_.1) | copy-start | bytes 196612
  31.4 1.4 %collective-permute-start.10 = (f32[4,8,512]{2,1,0:T(8,128)S(1)}, f32[4,8,512]{2,1,0:T(8,128)S(1)}, u32[]{:S(2)}, u32[]{:S(2)}) collective-permute-start(f32[4,8,512]{2,1,0:T(8,128)S(1)} %get-tuple-element.64), channel_id=1, source_target_pairs={{0,16},{16,0},{32,48},{48,32},{64,80},{80,64},{96,112},{112,96},{1... | collective-permute-start | bytes 196616 | tf_op jit(solution)/shard_map/ppermute | solution.py:249
  34.2 23.4 %all-to-all-start = ((f32[256,1,64]{2,1,0:T(1,128)}), f32[256,1,64]{2,1,0:T(1,128)S(1)}, u32[]{:S(2)}, u32[]{:S(2)}) async-start(f32[256,1,64]{2,1,0:T(1,128)} %bitcast.2), calls=%async_computation | async-start | bytes 262144 | tf_op jit(solution)/shard_map/all_to_all | solution.py:460
  44.8 3.1 %collective-permute-start.11 = (f32[16,1024]{1,0:T(8,128)S(1)}, f32[16,1024]{1,0:T(8,128)S(1)}, u32[]{:S(2)}, u32[]{:S(2)}) collective-permute-start(f32[16,1024]{1,0:T(8,128)S(1)} %get-tuple-element.69), channel_id=1, source_target_pairs={{0,16},{1,2},{2,1},{3,4},{4,3},{5,6},{6,5},{7,8},{8,7},{9,10},{10,... | collective-permute-start | bytes 196616 | tf_op jit(solution)/shard_map/ppermute | solution.py:64
  47.0 4.1 %collective-permute-start.12 = (f32[16,1024]{1,0:T(8,128)S(1)}, f32[16,1024]{1,0:T(8,128)S(1)}, u32[]{:S(2)}, u32[]{:S(2)}) collective-permute-start(f32[16,1024]{1,0:T(8,128)S(1)} %get-tuple-element.70), channel_id=1, source_target_pairs={{0,1},{1,0},{2,3},{3,2},{4,5},{5,4},{6,7},{7,6},{8,9},{9,8},{10,11... | collective-permute-start | bytes 196616 | tf_op jit(solution)/shard_map/ppermute | solution.py:53
  51.1 0.7 %copy-start.4 = (s32[4]{0:T(128)S(1)}, s32[4]{0:T(128)}, u32[]{:S(2)}) copy-start(s32[4]{0:T(128)} %param.9) | copy-start | bytes 52

commit v6 on v5

--- a/solution.py
+++ b/solution.py
@@ -327,26 +327,19 @@
     sums_ref[...] = patch_sums(patch_count, total_rows, lanes, map_ref, adj_ref, new_ref)
 
 
-def adjoint_kernel(
-    stiffness, total_rows, factor_ref, left_ref, adj_down_ref, ends_ref, mine_ref,
-    adj_ref, first_ref, second_ref,
+def adjoint_edges_kernel(mine_ref, got_ref, first_ref, second_ref):
+    for k in range(mine_ref.shape[0]):
+        edges((first_ref, second_ref), k, joined(half_first(), mine_ref[k], got_ref[k]))
+
+
+def shares_kernel(
+    patch_count, stiffness, total_rows, factor_ref, left_ref, adj_down_ref, down_ref, ends_ref, map_ref, mine_ref,
+    adj_ref, new_ref, shares_ref,
 ):
     lanes = lanes_of(False, adj_ref.shape[2])
-    back_sweep(
-        lanes, factor_ref, left_ref, adj_down_ref, ends_ref[0], ends_ref[1], 1.0 / stiffness, adj_ref
-    )
-    for k in range(adj_ref.shape[0]):
-        edges((first_ref, second_ref), k, joined(half_first(), mine_ref[k], adj_ref[k]))
-
-
-def shares_kernel(
-    patch_count, stiffness, total_rows, factor_ref, left_ref, down_ref, ends_ref, map_ref, adj_ref, mine_ref,
-    new_ref, shares_ref,
-):
-    lanes = lanes_of(False, adj_ref.shape[2])
-    back_sweep(
-        lanes, factor_ref, left_ref, down_ref, ends_ref[2], ends_ref[3], 1.0 / stiffness, new_ref
-    )
+    sweep = (lanes, factor_ref, left_ref)
+    back_sweep(*sweep, adj_down_ref, ends_ref[0], ends_ref[1], 1.0 / stiffness, adj_ref)
+    back_sweep(*sweep, down_ref, ends_ref[2], ends_ref[3], 1.0 / stiffness, new_ref)
     sums = mine_ref[...] + patch_sums(patch_count, total_rows, lanes, map_ref, adj_ref, new_ref)
     rows_here = sums.shape[0]
     for i in range(shares_ref.shape[0] // rows_here):
@@ -434,29 +427,22 @@
         mine,
         patch_map,
     )
-    adj_got, first, second = call(
-        with_sizes(adjoint_kernel),
-        [shape_of(*half), shape_of(*plane), shape_of(*plane)],
+    adj_got, new_got, sums = call(
+        with_sizes(functools.partial(shares_kernel, patch_count)),
+        [shape_of(*half), shape_of(*half), shape_of(devices, patch_count // PATCH_ROWS)],
         [],
         factor,
         left,
         adj_down,
-        got,
-        adj_mine,
-    )
-    first, second = pair_swap(first, second)
-    new_got, sums = call(
-        with_sizes(functools.partial(shares_kernel, patch_count)),
-        [shape_of(*half), shape_of(devices, patch_count // PATCH_ROWS)],
-        [],
-        factor,
-        left,
         down,
         got,
         patch_map,
-        adj_got,
         sums,
     )
+    first, second = call(
+        adjoint_edges_kernel, [shape_of(*plane), shape_of(*plane)], [], adj_mine, adj_got
+    )
+    first, second = pair_swap(first, second)
     shares = lax.all_to_all(sums, ("gy", "gx"), 0, 0, tiled=True)
     norm_factor = 1.0 / math.sqrt(planes * groups_x * total_rows * span / (owned * devices))
     grad_velocity, new_velocity, weight = call(

time: 58.6 us -> 58.4 us (level)
  no operation moved by 1% of the time
where the time goes in v6:
time: 58.4 us; the launch traced here: 58.2 us
  starting transfers between devices  30.1 us (52%)
  waiting for transfers between devices  19.2 us (33%)
  Pallas kernels  5.21 us (9%)
  local copies, waits for them, and re-layouts  2.94 us (5%)
  between operations  0.74 us (1%)
    ppermute x9, starting transfers between devices, swap(): return lax.ppermute(array, 'gx', pairs)  13.6 us
    all_to_all x1, starting transfers between devices, local(): shares = lax.all_to_all(sums, ('gy', 'gx'), 0, 0, tiled=True)  10.5 us
    ppermute x9, waiting for transfers between devices, swap(): return lax.ppermute(array, 'gx', pairs)  8.65 us
    ppermute x2, waiting for transfers between devices, near_swap(): lax.ppermute(edge, 'gy', [(i, i ^ 1) for i in range(lax.axis_size('gy'))])  5.7 us
    ppermute x2, starting transfers between devices, far_swap(): return lax.ppermute(edge, ('gx', 'gy'), pairs)  5.56 us
    pallas_call x15, Pallas kernels, call(): pl.pallas_call(kernel, out_shape=outs, in_specs=[VMEM] * len(operands), o...  5.21 us
    all_to_all x1, waiting for transfers between devices, local(): shares = lax.all_to_all(sums, ('gy', 'gx'), 0, 0, tiled=True)  4.35 us
    unnamed x10, local copies, waits for them, and re-layouts  2.94 us
  transfers between devices with their start and end apart: 14, of which 9 were waited for; matrix products, arithmetic and copies ran while one was open for 0% of the time, Pallas kernels for 4%

profile of v6, /device:TPU:1, one launch (start us, length us, event | category | flops | bytes accessed | tf_op | source)
XLA Modules:
  0.0 58.2 jit_solution(5430351700693566893)
XLA Ops:
  0.6 0.0 copy-start
  0.6 0.0 copy-start.1
  0.6 1.1 %copy-done.1 = f32[16,8,1024]{2,1,0:T(8,128)S(1)} copy-done((f32[16,8,1024]{2,1,0:T(8,128)S(1)}, f32[16,8,1024]{2,1,0:T(8,128)}, u32[]{:S(2)}) %copy-start.1) | copy-done | bytes 524312
  1.7 0.1 shard_map.77
  1.9 3.3 %collective-permute-start = (f32[16,1024]{1,0:T(8,128)S(1)}, f32[16,1024]{1,0:T(8,128)S(1)}, u32[]{:S(2)}, u32[]{:S(2)}) collective-permute-start(f32[16,1024]{1,0:T(8,128)S(1)} %get-tuple-element.43), channel_id=1, source_target_pairs={{0,16},{1,2},{2,1},{3,4},{4,3},{5,6},{6,5},{7,8},{8,7},{9,10},{10,... | collective-permute-start | bytes 196616 | tf_op jit(solution)/shard_map/ppermute | solution.py:64
  5.2 0.0 collective-permute-start.1
  5.2 0.0 copy-done
  5.2 0.0 copy-start.3
  5.2 0.8 %copy-done.3 = f32[16,1024]{1,0:T(8,128)S(1)} copy-done((f32[16,1024]{1,0:T(8,128)S(1)}, f32[16,1024]{1,0:T(8,128)}, u32[]{:S(2)}) %copy-start.3) | copy-done | bytes 65560
  6.1 0.3 shard_map.76
  6.4 0.0 collective-permute-done.second_ref
  6.4 2.5 %collective-permute-done.1.first_ref = f32[16,1024]{1,0:T(8,128)S(1)} collective-permute-done((f32[16,1024]{1,0:T(8,128)S(1)}, f32[16,1024]{1,0:T(8,128)S(1)}, u32[]{:S(2)}, u32[]{:S(2)}) %collective-permute-start.1) | collective-permute-done | bytes 65568 | tf_op jit(solution)/shard_map/ppermute | solution.py:53
  8.9 0.5 shard_map.78
  9.3 1.0 %collective-permute-start.2 = (f32[7,8,512]{2,1,0:T(8,128)S(1)}, f32[7,8,512]{2,1,0:T(8,128)S(1)}, u32[]{:S(2)}, u32[]{:S(2)}) collective-permute-start(f32[7,8,512]{2,1,0:T(8,128)S(1)} %get-tuple-element.48), channel_id=1, source_target_pairs={{0,16},{16,0},{32,48},{48,32},{64,80},{80,64},{96,112},{112,96},{1... | collective-permute-start | bytes 344072 | tf_op jit(solution)/shard_map/ppermute | solution.py:249
  10.3 1.0 %collective-permute-done.2.got_ref = f32[7,8,512]{2,1,0:T(8,128)S(1)} collective-permute-done((f32[7,8,512]{2,1,0:T(8,128)S(1)}, f32[7,8,512]{2,1,0:T(8,128)S(1)}, u32[]{:S(2)}, u32[]{:S(2)}) %collective-permute-start.2) | collective-permute-done | bytes 114720 | tf_op jit(solution)/shard_map/ppermute | solution.py:249
  11.3 0.9 %collective-permute-start.3 = (f32[7,8,256]{2,1,0:T(8,128)S(1)}, f32[7,8,256]{2,1,0:T(8,128)S(1)}, u32[]{:S(2)}, u32[]{:S(2)}) collective-permute-start(f32[7,8,256]{2,1,0:T(8,128)S(1)} %get-tuple-element.50), channel_id=1, source_target_pairs={{0,48},{16,32},{32,16},{48,0},{64,112},{80,96},{96,80},{112,64},{1... | collective-permute-start | bytes 172040 | tf_op jit(solution)/shard_map/ppermute | solution.py:249
  12.2 3.0 %collective-permute-done.3.got_ref = f32[7,8,256]{2,1,0:T(8,128)S(1)} collective-permute-done((f32[7,8,256]{2,1,0:T(8,128)S(1)}, f32[7,8,256]{2,1,0:T(8,128)S(1)}, u32[]{:S(2)}, u32[]{:S(2)}) %collective-permute-start.3) | collective-permute-done | bytes 57376 | tf_op jit(solution)/shard_map/ppermute | solution.py:249
  15.3 3.6 %collective-permute-start.4 = (f32[7,8,256]{2,1,0:T(8,128)S(1)}, f32[7,8,256]{2,1,0:T(8,128)S(1)}, u32[]{:S(2)}, u32[]{:S(2)}) collective-permute-start(f32[7,8,256]{2,1,0:T(8,128)S(1)} %get-tuple-element.51.mine_ref), channel_id=1, source_target_pairs={{0,112},{16,96},{32,80},{48,64},{64,48},{80,32},{96,16},{112,0},{1... | collective-permute-start | bytes 172040 | tf_op jit(solution)/shard_map/ppermute | solution.py:249
  18.9 0.2 collective-permute-start.5
  19.1 2.0 %collective-permute-done.4.got_ref = f32[7,8,256]{2,1,0:T(8,128)S(1)} collective-permute-done((f32[7,8,256]{2,1,0:T(8,128)S(1)}, f32[7,8,256]{2,1,0:T(8,128)S(1)}, u32[]{:S(2)}, u32[]{:S(2)}) %collective-permute-start.4) | collective-permute-done | bytes 57376 | tf_op jit(solution)/shard_map/ppermute | solution.py:249
  21.1 1.2 %collective-permute-start.8 = (f32[3,8,256]{2,1,0:T(8,128)S(1)}, f32[3,8,256]{2,1,0:T(8,128)S(1)}, u32[]{:S(2)}, u32[]{:S(2)}) collective-permute-start(f32[3,8,256]{2,1,0:T(8,128)S(1)} %get-tuple-element.52.rim_ref), channel_id=1, source_target_pairs={{0,240},{16,224},{32,208},{48,192},{64,176},{80,160},{96,144},{112... | collective-permute-start | bytes 73736 | tf_op jit(solution)/shard_map/ppermute | solution.py:249
  22.3 0.0 collective-permute-done.5.got_ref
  22.4 3.7 %collective-permute-start.6 = (f32[3,8,256]{2,1,0:T(8,128)S(1)}, f32[3,8,256]{2,1,0:T(8,128)S(1)}, u32[]{:S(2)}, u32[]{:S(2)}) collective-permute-start(f32[3,8,256]{2,1,0:T(8,128)S(1)} %get-tuple-element.53.rim_ref), channel_id=1, source_target_pairs={{0,240},{16,224},{32,208},{48,192},{64,176},{80,160},{96,144},{112... | collective-permute-start | bytes 73736 | tf_op jit(solution)/shard_map/ppermute | solution.py:249
  26.0 0.0 collective-permute-done.8.got_ref
  26.1 0.4 collective-permute-start.9
  26.5 1.0 %collective-permute-done.6.got_ref = f32[3,8,256]{2,1,0:T(8,128)S(1)} collective-permute-done((f32[3,8,256]{2,1,0:T(8,128)S(1)}, f32[3,8,256]{2,1,0:T(8,128)S(1)}, u32[]{:S(2)}, u32[]{:S(2)}) %collective-permute-start.6) | collective-permute-done | bytes 24608 | tf_op jit(solution)/shard_map/ppermute | solution.py:249
  27.6 2.1 %collective-permute-start.7 = (f32[4,8,256]{2,1,0:T(8,128)S(1)}, f32[4,8,256]{2,1,0:T(8,128)S(1)}, u32[]{:S(2)}, u32[]{:S(2)}) collective-permute-start(f32[4,8,256]{2,1,0:T(8,128)S(1)} %get-tuple-element.57), channel_id=1, source_target_pairs={{0,48},{16,32},{32,16},{48,0},{64,112},{80,96},{96,80},{112,64},{1... | collective-permute-start | bytes 98312 | tf_op jit(solution)/shard_map/ppermute | solution.py:249
  29.7 0.0 collective-permute-done.9.high_got_ref
  29.7 1.6 %collective-permute-done.7.low_got_ref = f32[4,8,256]{2,1,0:T(8,128)S(1)} collective-permute-done((f32[4,8,256]{2,1,0:T(8,128)S(1)}, f32[4,8,256]{2,1,0:T(8,128)S(1)}, u32[]{:S(2)}, u32[]{:S(2)}) %collective-permute-start.7) | collective-permute-done | bytes 32800 | tf_op jit(solution)/shard_map/ppermute | solution.py:249
  31.3 0.0 copy-start.2
  31.4 0.4 collective-permute-start.10
  31.8 0.4 copy-done.2
  32.2 0.6 shard_map.86
  32.7 0.0 collective-permute-done.10.refs_4_
  32.7 1.3 %shard_map.87 = (f32[16,8,512]{2,1,0:T(8,128)S(1)}, f32[16,8,512]{2,1,0:T(8,128)S(1)}, f32[256,64]{1,0:T(8,128)}) custom-call(f32[16,8,1024]{2,1,0:T(8,128)S(1)} %get-tuple-element.39.factor_ref.refs_0_, f32[16,8,1024]{2,1,0:T(8,128)S(1)} %get-tuple-element.40.refs_1_, f32[16,8,1024]{2,1,0:T(8,128)S(1)} %get-tuple-element.41.refs_2_, ...), custom_call_target="tpu_custom_call" | custom-call | tf_op jit(solution)/shard_map/pallas_call | solution.py:370
  34.1 10.5 %all-to-all-start = ((f32[256,1,64]{2,1,0:T(1,128)}), f32[256,1,64]{2,1,0:T(1,128)S(1)}, u32[]{:S(2)}, u32[]{:S(2)}) async-start(f32[256,1,64]{2,1,0:T(1,128)} %bitcast.2), calls=%async_computation | async-start | bytes 262144 | tf_op jit(solution)/shard_map/all_to_all | solution.py:446
  44.6 0.2 shard_map.88
  44.8 2.2 %collective-permute-start.11 = (f32[16,1024]{1,0:T(8,128)S(1)}, f32[16,1024]{1,0:T(8,128)S(1)}, u32[]{:S(2)}, u32[]{:S(2)}) collective-permute-start(f32[16,1024]{1,0:T(8,128)S(1)} %get-tuple-element.69), channel_id=1, source_target_pairs={{0,16},{1,2},{2,1},{3,4},{4,3},{5,6},{6,5},{7,8},{8,7},{9,10},{10,... | collective-permute-start | bytes 196616 | tf_op jit(solution)/shard_map/ppermute | solution.py:64
  47.0 0.4 collective-permute-start.12
  47.4 0.5 collective-permute-done.11.second_ref
  47.9 3.2 %collective-permute-done.12.first_ref = f32[16,1024]{1,0:T(8,128)S(1)} collective-permute-done((f32[16,1024]{1,0:T(8,128)S(1)}, f32[16,1024]{1,0:T(8,128)S(1)}, u32[]{:S(2)}, u32[]{:S(2)}) %collective-permute-start.12) | collective-permute-done | bytes 65568 | tf_op jit(solution)/shard_map/ppermute | solution.py:53
  51.1 0.0 copy-start.4
  51.1 0.7 %copy-done.4 = s32[4]{0:T(128)S(1)} copy-done((s32[4]{0:T(128)S(1)}, s32[4]{0:T(128)}, u32[]{:S(2)}) %copy-start.4) | copy-done | bytes 40
  51.8 1.3 %shard_map.89 = (f32[16,8,1024]{2,1,0:T(8,128)}, f32[16,8,1024]{2,1,0:T(8,128)}, f32[1,4]{1,0:T(1,128)S(1)}) custom-call(f32[16,8,512]{2,1,0:T(8,128)S(1)} %get-tuple-element.63.mine_ref.adj_ref, f32[16,8,512]{2,1,0:T(8,128)S(1)} %get-tuple-element.66.got_ref.adj_got_ref, f32[16,8,512]{2,1,0:T(8,128)S(1)} %get-tuple-element.67.new_in_ref, ...), custom_call_target="tpu_custom_call" | custom-call | tf_op jit(solution)/shard_map/pallas_call | solution.py:370
  53.1 4.4 %all-to-all-done = f32[256,1,64]{2,1,0:T(1,128)S(1)} async-done(((f32[256,1,64]{2,1,0:T(1,128)}), f32[256,1,64]{2,1,0:T(1,128)S(1)}, u32[]{:S(2)}, u32[]{:S(2)}) %all-to-all-start) | async-done | bytes 65568 | tf_op jit(solution)/shard_map/all_to_all | solution.py:446
  57.5 0.7 %shard_map.90 = f32[1,4]{1,0:T(1,128)} custom-call(f32[256,64]{1,0:T(8,128)S(1)} %bitcast.6, f32[1,4]{1,0:T(1,128)S(1)} %get-tuple-element.74.weight_ref), custom_call_target="tpu_custom_call" | custom-call | tf_op jit(solution)/shard_map/pallas_call | solution.py:370
  (7 shorter events, 0.2 us)
Async XLA Ops:
  0.6 4.6 %copy-start = (f32[16,8,1024]{2,1,0:T(8,128)S(1)}, f32[16,8,1024]{2,1,0:T(8,128)}, u32[]{:S(2)}) copy-start(f32[16,8,1024]{2,1,0:T(8,128)} %refs_1_.1) | copy-start | bytes 1572868
  0.6 1.1 %copy-start.1 = (f32[16,8,1024]{2,1,0:T(8,128)S(1)}, f32[16,8,1024]{2,1,0:T(8,128)}, u32[]{:S(2)}) copy-start(f32[16,8,1024]{2,1,0:T(8,128)} %velocity_ref.1) | copy-start | bytes 1572868
  1.9 4.5 %collective-permute-start = (f32[16,1024]{1,0:T(8,128)S(1)}, f32[16,1024]{1,0:T(8,128)S(1)}, u32[]{:S(2)}, u32[]{:S(2)}) collective-permute-start(f32[16,1024]{1,0:T(8,128)S(1)} %get-tuple-element.43), channel_id=1, source_target_pairs={{0,16},{1,2},{2,1},{3,4},{4,3},{5,6},{6,5},{7,8},{8,7},{9,10},{10,... | collective-permute-start | bytes 196616 | tf_op jit(solution)/shard_map/ppermute | solution.py:64
  5.2 3.7 %collective-permute-start.1 = (f32[16,1024]{1,0:T(8,128)S(1)}, f32[16,1024]{1,0:T(8,128)S(1)}, u32[]{:S(2)}, u32[]{:S(2)}) collective-permute-start(f32[16,1024]{1,0:T(8,128)S(1)} %get-tuple-element.44), channel_id=1, source_target_pairs={{0,1},{1,0},{2,3},{3,2},{4,5},{5,4},{6,7},{7,6},{8,9},{9,8},{10,11... | collective-permute-start | bytes 196616 | tf_op jit(solution)/shard_map/ppermute | solution.py:53
  5.2 0.8 %copy-start.3 = (f32[16,1024]{1,0:T(8,128)S(1)}, f32[16,1024]{1,0:T(8,128)}, u32[]{:S(2)}) copy-start(f32[16,1024]{1,0:T(8,128)} %refs_0_.1) | copy-start | bytes 196612
  9.3 1.9 %collective-permute-start.2 = (f32[7,8,512]{2,1,0:T(8,128)S(1)}, f32[7,8,512]{2,1,0:T(8,128)S(1)}, u32[]{:S(2)}, u32[]{:S(2)}) collective-permute-start(f32[7,8,512]{2,1,0:T(8,128)S(1)} %get-tuple-element.48), channel_id=1, source_target_pairs={{0,16},{16,0},{32,48},{48,32},{64,80},{80,64},{96,112},{112,96},{1... | collective-permute-start | bytes 344072 | tf_op jit(solution)/shard_map/ppermute | solution.py:249
  11.3 4.0 %collective-permute-start.3 = (f32[7,8,256]{2,1,0:T(8,128)S(1)}, f32[7,8,256]{2,1,0:T(8,128)S(1)}, u32[]{:S(2)}, u32[]{:S(2)}) collective-permute-start(f32[7,8,256]{2,1,0:T(8,128)S(1)} %get-tuple-element.50), channel_id=1, source_target_pairs={{0,48},{16,32},{32,16},{48,0},{64,112},{80,96},{96,80},{112,64},{1... | collective-permute-start | bytes 172040 | tf_op jit(solution)/shard_map/ppermute | solution.py:249
  15.3 5.8 %collective-permute-start.4 = (f32[7,8,256]{2,1,0:T(8,128)S(1)}, f32[7,8,256]{2,1,0:T(8,128)S(1)}, u32[]{:S(2)}, u32[]{:S(2)}) collective-permute-start(f32[7,8,256]{2,1,0:T(8,128)S(1)} %get-tuple-element.51.mine_ref), channel_id=1, source_target_pairs={{0,112},{16,96},{32,80},{48,64},{64,48},{80,32},{96,16},{112,0},{1... | collective-permute-start | bytes 172040 | tf_op jit(solution)/shard_map/ppermute | solution.py:249
  18.9 3.4 %collective-permute-start.5 = (f32[7,8,256]{2,1,0:T(8,128)S(1)}, f32[7,8,256]{2,1,0:T(8,128)S(1)}, u32[]{:S(2)}, u32[]{:S(2)}) collective-permute-start(f32[7,8,256]{2,1,0:T(8,128)S(1)} %get-tuple-element.51.mine_ref), channel_id=1, source_target_pairs={{0,16},{16,0},{32,48},{48,32},{64,80},{80,64},{96,112},{112,96},{1... | collective-permute-start | bytes 172040 | tf_op jit(solution)/shard_map/ppermute | solution.py:249
  21.1 4.9 %collective-permute-start.8 = (f32[3,8,256]{2,1,0:T(8,128)S(1)}, f32[3,8,256]{2,1,0:T(8,128)S(1)}, u32[]{:S(2)}, u32[]{:S(2)}) collective-permute-start(f32[3,8,256]{2,1,0:T(8,128)S(1)} %get-tuple-element.52.rim_ref), channel_id=1, source_target_pairs={{0,240},{16,224},{32,208},{48,192},{64,176},{80,160},{96,144},{112... | collective-permute-start | bytes 73736 | tf_op jit(solution)/shard_map/ppermute | solution.py:249
  22.4 5.2 %collective-permute-start.6 = (f32[3,8,256]{2,1,0:T(8,128)S(1)}, f32[3,8,256]{2,1,0:T(8,128)S(1)}, u32[]{:S(2)}, u32[]{:S(2)}) collective-permute-start(f32[3,8,256]{2,1,0:T(8,128)S(1)} %get-tuple-element.53.rim_ref), channel_id=1, source_target_pairs={{0,240},{16,224},{32,208},{48,192},{64,176},{80,160},{96,144},{112... | collective-permute-start | bytes 73736 | tf_op jit(solution)/shard_map/ppermute | solution.py:249
  26.1 3.6 %collective-permute-start.9 = (f32[4,8,256]{2,1,0:T(8,128)S(1)}, f32[4,8,256]{2,1,0:T(8,128)S(1)}, u32[]{:S(2)}, u32[]{:S(2)}) collective-permute-start(f32[4,8,256]{2,1,0:T(8,128)S(1)} %get-tuple-element.60), channel_id=1, source_target_pairs={{0,16},{16,0},{32,48},{48,32},{64,80},{80,64},{96,112},{112,96},{1... | collective-permute-start | bytes 98312 | tf_op jit(solution)/shard_map/ppermute | solution.py:249
  27.6 3.7 %collective-permute-start.7 = (f32[4,8,256]{2,1,0:T(8,128)S(1)}, f32[4,8,256]{2,1,0:T(8,128)S(1)}, u32[]{:S(2)}, u32[]{:S(2)}) collective-permute-start(f32[4,8,256]{2,1,0:T(8,128)S(1)} %get-tuple-element.57), channel_id=1, source_target_pairs={{0,48},{16,32},{32,16},{48,0},{64,112},{80,96},{96,80},{112,64},{1... | collective-permute-start | bytes 98312 | tf_op jit(solution)/shard_map/ppermute | solution.py:249
  31.3 0.8 %copy-start.2 = (s32[16,1024]{1,0:T(8,128)S(1)}, s32[16,1024]{1,0:T(8,128)}, u32[]{:S(2)}) copy-start(s32[16,1024]{1,0:T(8,128)} %refs_5_.3) | copy-start | bytes 196612
  31.4 1.4 %collective-permute-start.10 = (f32[4,8,512]{2,1,0:T(8,128)S(1)}, f32[4,8,512]{2,1,0:T(8,128)S(1)}, u32[]{:S(2)}, u32[]{:S(2)}) collective-permute-start(f32[4,8,512]{2,1,0:T(8,128)S(1)} %get-tuple-element.64), channel_id=1, source_target_pairs={{0,16},{16,0},{32,48},{48,32},{64,80},{80,64},{96,112},{112,96},{1... | collective-permute-start | bytes 196616 | tf_op jit(solution)/shard_map/ppermute | solution.py:249
  34.1 23.4 %all-to-all-start = ((f32[256,1,64]{2,1,0:T(1,128)}), f32[256,1,64]{2,1,0:T(1,128)S(1)}, u32[]{:S(2)}, u32[]{:S(2)}) async-start(f32[256,1,64]{2,1,0:T(1,128)} %bitcast.2), calls=%async_computation | async-start | bytes 262144 | tf_op jit(solution)/shard_map/all_to_all | solution.py:446
  44.8 3.1 %collective-permute-start.11 = (f32[16,1024]{1,0:T(8,128)S(1)}, f32[16,1024]{1,0:T(8,128)S(1)}, u32[]{:S(2)}, u32[]{:S(2)}) collective-permute-start(f32[16,1024]{1,0:T(8,128)S(1)} %get-tuple-element.69), channel_id=1, source_target_pairs={{0,16},{1,2},{2,1},{3,4},{4,3},{5,6},{6,5},{7,8},{8,7},{9,10},{10,... | collective-permute-start | bytes 196616 | tf_op jit(solution)/shard_map/ppermute | solution.py:64
  47.0 4.1 %collective-permute-start.12 = (f32[16,1024]{1,0:T(8,128)S(1)}, f32[16,1024]{1,0:T(8,128)S(1)}, u32[]{:S(2)}, u32[]{:S(2)}) collective-permute-start(f32[16,1024]{1,0:T(8,128)S(1)} %get-tuple-element.70), channel_id=1, source_target_pairs={{0,1},{1,0},{2,3},{3,2},{4,5},{5,4},{6,7},{7,6},{8,9},{9,8},{10,11... | collective-permute-start | bytes 196616 | tf_op jit(solution)/shard_map/ppermute | solution.py:53
  51.1 0.7 %copy-start.4 = (s32[4]{0:T(128)S(1)}, s32[4]{0:T(128)}, u32[]{:S(2)}) copy-start(s32[4]{0:T(128)} %param.9) | copy-start | bytes 52

commit v7 on v6

--- a/solution.py
+++ b/solution.py
@@ -80,7 +80,13 @@
     return jnp.exp(-wall_decay * heights / total_rows)
 
 
-def matrix_kernel(stiffness, total_rows, coef_ref, target_ref, factor_ref, adj_down_ref, left_ref, rims_ref):
+def matrix_kernel(
+    stiffness, total_rows, coef_ref, target_ref, velocity_ref, map_ref,
+    factor_ref, adj_down_ref, left_ref, rims_ref, base_ref, map_out_ref,
+):
+    map_out_ref[...] = map_ref[...]
+    for k in range(velocity_ref.shape[0]):
+        base_ref[k] = explicit(velocity_ref[k], 0.0, 0.0)
     planes, rows, span = target_ref.shape
     damping = damping_rows(rows, total_rows)
     factor = jnp.zeros((rows, span), F32)
@@ -106,11 +112,14 @@
     rims_ref[3] = value
 
 
-def velocity_kernel(velocity_ref, second_ref, first_ref, factor_ref, rims_ref, down_ref, mine_ref, give_ref):
-    planes, rows, span = velocity_ref.shape
+def velocity_kernel(base_ref, second_ref, first_ref, factor_ref, rims_ref, down_ref, mine_ref, give_ref):
+    planes, rows, span = base_ref.shape
+    row_ids = lax.broadcasted_iota(jnp.int32, (rows, span), 0)
     reduced = jnp.zeros((rows, span), F32)
     for k in range(planes):
-        forcing = explicit(velocity_ref[k], *halo(first_ref, second_ref, k))
+        below, above = halo(first_ref, second_ref, k)
+        outside = jnp.where(row_ids == 0, below, jnp.where(row_ids == rows - 1, above, 0.0))
+        forcing = base_ref[k] + wall_coef * outside
         reduced = (forcing + reduced) * factor_ref[k]
         down_ref[k] = reduced
     value = reduced
@@ -393,18 +402,21 @@
         edge_kernel, [shape_of(*field), shape_of(*plane), shape_of(*plane)], [], velocity
     )
     first, second = pair_swap(first, second)
-    factor, adj_down, left, rims = call(
+    factor, adj_down, left, rims, base, patch_map = call(
         with_sizes(matrix_kernel),
-        [shape_of(*field)] * 3 + [shape_of(5, rows, span)],
+        [shape_of(*field)] * 3
+        + [shape_of(5, rows, span), shape_of(*field), jax.ShapeDtypeStruct(plane, jnp.int32)],
         [],
         shape_coef,
         cotangent,
+        velocity,
+        patch_map,
     )
     down, mine, give = call(
         velocity_kernel,
         [shape_of(*field)] + [shape_of(7, rows, span // 2)] * 2,
         [],
-        velocity,
+        base,
         second,
         first,
         factor,

time: 58.4 us -> 58.1 us (level)
  waiting for transfers between devices: 19.2 us -> 18.3 us
    ppermute x2, waiting for transfers between devices: 5.7 us -> 4.56 us  [near_swap(): lax.ppermute(edge, 'gy', [(i, i ^ 1) for i in range(lax.axis_size('gy'))])]
  transfers between devices with their start and end apart: 14 -> 14, of which waited for: 9 -> 10; matrix products, arithmetic and copies ran while one was open for 0% -> 0% of each run, Pallas kernels for 4% -> 5%
where the time goes in v7:
time: 58.1 us; the launch traced here: 57.8 us
  starting transfers between devices  30.2 us (52%)
  waiting for transfers between devices  18.3 us (31%)
  Pallas kernels  5.26 us (9%)
  local copies, waits for them, and re-layouts  3.37 us (6%)
  between operations  0.74 us (1%)
    ppermute x9, starting transfers between devices, swap(): return lax.ppermute(array, 'gx', pairs)  13.7 us
    all_to_all x1, starting transfers between devices, local(): shares = lax.all_to_all(sums, ('gy', 'gx'), 0, 0, tiled=True)  10.5 us
    ppermute x9, waiting for transfers between devices, swap(): return lax.ppermute(array, 'gx', pairs)  8.88 us
    ppermute x2, starting transfers between devices, far_swap(): return lax.ppermute(edge, ('gx', 'gy'), pairs)  5.56 us
    pallas_call x15, Pallas kernels, call(): pl.pallas_call(kernel, out_shape=outs, in_specs=[VMEM] * len(operands), o...  5.26 us
    ppermute x2, waiting for transfers between devices, near_swap(): lax.ppermute(edge, 'gy', [(i, i ^ 1) for i in range(lax.axis_size('gy'))])  4.56 us
    all_to_all x1, waiting for transfers between devices, local(): shares = lax.all_to_all(sums, ('gy', 'gx'), 0, 0, tiled=True)  4.35 us
    unnamed x10, local copies, waits for them, and re-layouts  3.37 us
  transfers between devices with their start and end apart: 14, of which 10 were waited for; matrix products, arithmetic and copies ran while one was open for 0% of the time, Pallas kernels for 5%

profile of v7, /device:TPU:1, one launch (start us, length us, event | category | flops | bytes accessed | tf_op | source)
XLA Modules:
  0.0 57.8 jit_solution(1927972147376139747)
XLA Ops:
  0.6 0.0 copy-start
  0.6 1.0 %copy-done = f32[16,8,1024]{2,1,0:T(8,128)S(1)} copy-done((f32[16,8,1024]{2,1,0:T(8,128)S(1)}, f32[16,8,1024]{2,1,0:T(8,128)}, u32[]{:S(2)}) %copy-start) | copy-done | bytes 524312
  1.7 0.0 copy-start.1
  1.7 0.1 shard_map.76
  1.8 3.3 %collective-permute-start = (f32[16,1024]{1,0:T(8,128)S(1)}, f32[16,1024]{1,0:T(8,128)S(1)}, u32[]{:S(2)}, u32[]{:S(2)}) collective-permute-start(f32[16,1024]{1,0:T(8,128)S(1)} %get-tuple-element.46), channel_id=1, source_target_pairs={{0,16},{1,2},{2,1},{3,4},{4,3},{5,6},{6,5},{7,8},{8,7},{9,10},{10,... | collective-permute-start | bytes 196616 | tf_op jit(solution)/shard_map/ppermute | solution.py:64
  5.2 0.0 collective-permute-start.1
  5.2 0.0 copy-done.1
  5.2 0.0 copy-start.2
  5.2 0.8 %copy-done.2 = f32[16,1024]{1,0:T(8,128)S(1)} copy-done((f32[16,1024]{1,0:T(8,128)S(1)}, f32[16,1024]{1,0:T(8,128)}, u32[]{:S(2)}) %copy-start.2) | copy-done | bytes 65560
  6.0 0.0 copy-start.3
  6.0 0.8 %copy-done.3 = s32[16,1024]{1,0:T(8,128)S(1)} copy-done((s32[16,1024]{1,0:T(8,128)S(1)}, s32[16,1024]{1,0:T(8,128)}, u32[]{:S(2)}) %copy-start.3) | copy-done | bytes 65560
  6.8 0.6 shard_map.77
  7.4 0.0 collective-permute-done.second_ref
  7.4 1.4 %collective-permute-done.1.first_ref = f32[16,1024]{1,0:T(8,128)S(1)} collective-permute-done((f32[16,1024]{1,0:T(8,128)S(1)}, f32[16,1024]{1,0:T(8,128)S(1)}, u32[]{:S(2)}, u32[]{:S(2)}) %collective-permute-start.1) | collective-permute-done | bytes 65568 | tf_op jit(solution)/shard_map/ppermute | solution.py:53
  8.8 0.2 shard_map.78
  9.0 1.0 %collective-permute-start.2 = (f32[7,8,512]{2,1,0:T(8,128)S(1)}, f32[7,8,512]{2,1,0:T(8,128)S(1)}, u32[]{:S(2)}, u32[]{:S(2)}) collective-permute-start(f32[7,8,512]{2,1,0:T(8,128)S(1)} %get-tuple-element.51), channel_id=1, source_target_pairs={{0,16},{16,0},{32,48},{48,32},{64,80},{80,64},{96,112},{112,96},{1... | collective-permute-start | bytes 344072 | tf_op jit(solution)/shard_map/ppermute | solution.py:258
  10.0 1.0 %collective-permute-done.2.got_ref = f32[7,8,512]{2,1,0:T(8,128)S(1)} collective-permute-done((f32[7,8,512]{2,1,0:T(8,128)S(1)}, f32[7,8,512]{2,1,0:T(8,128)S(1)}, u32[]{:S(2)}, u32[]{:S(2)}) %collective-permute-start.2) | collective-permute-done | bytes 114720 | tf_op jit(solution)/shard_map/ppermute | solution.py:258
  11.0 1.0 %collective-permute-start.3 = (f32[7,8,256]{2,1,0:T(8,128)S(1)}, f32[7,8,256]{2,1,0:T(8,128)S(1)}, u32[]{:S(2)}, u32[]{:S(2)}) collective-permute-start(f32[7,8,256]{2,1,0:T(8,128)S(1)} %get-tuple-element.53), channel_id=1, source_target_pairs={{0,48},{16,32},{32,16},{48,0},{64,112},{80,96},{96,80},{112,64},{1... | collective-permute-start | bytes 172040 | tf_op jit(solution)/shard_map/ppermute | solution.py:258
  12.0 3.0 %collective-permute-done.3.got_ref = f32[7,8,256]{2,1,0:T(8,128)S(1)} collective-permute-done((f32[7,8,256]{2,1,0:T(8,128)S(1)}, f32[7,8,256]{2,1,0:T(8,128)S(1)}, u32[]{:S(2)}, u32[]{:S(2)}) %collective-permute-start.3) | collective-permute-done | bytes 57376 | tf_op jit(solution)/shard_map/ppermute | solution.py:258
  15.0 3.7 %collective-permute-start.4 = (f32[7,8,256]{2,1,0:T(8,128)S(1)}, f32[7,8,256]{2,1,0:T(8,128)S(1)}, u32[]{:S(2)}, u32[]{:S(2)}) collective-permute-start(f32[7,8,256]{2,1,0:T(8,128)S(1)} %get-tuple-element.54.mine_ref), channel_id=1, source_target_pairs={{0,112},{16,96},{32,80},{48,64},{64,48},{80,32},{96,16},{112,0},{1... | collective-permute-start | bytes 172040 | tf_op jit(solution)/shard_map/ppermute | solution.py:258
  18.7 0.2 collective-permute-start.5
  18.9 1.9 %collective-permute-done.4.got_ref = f32[7,8,256]{2,1,0:T(8,128)S(1)} collective-permute-done((f32[7,8,256]{2,1,0:T(8,128)S(1)}, f32[7,8,256]{2,1,0:T(8,128)S(1)}, u32[]{:S(2)}, u32[]{:S(2)}) %collective-permute-start.4) | collective-permute-done | bytes 57376 | tf_op jit(solution)/shard_map/ppermute | solution.py:258
  20.8 1.3 %collective-permute-start.8 = (f32[3,8,256]{2,1,0:T(8,128)S(1)}, f32[3,8,256]{2,1,0:T(8,128)S(1)}, u32[]{:S(2)}, u32[]{:S(2)}) collective-permute-start(f32[3,8,256]{2,1,0:T(8,128)S(1)} %get-tuple-element.55.rim_ref), channel_id=1, source_target_pairs={{0,240},{16,224},{32,208},{48,192},{64,176},{80,160},{96,144},{112... | collective-permute-start | bytes 73736 | tf_op jit(solution)/shard_map/ppermute | solution.py:258
  22.1 0.0 collective-permute-done.5.got_ref
  22.1 3.7 %collective-permute-start.6 = (f32[3,8,256]{2,1,0:T(8,128)S(1)}, f32[3,8,256]{2,1,0:T(8,128)S(1)}, u32[]{:S(2)}, u32[]{:S(2)}) collective-permute-start(f32[3,8,256]{2,1,0:T(8,128)S(1)} %get-tuple-element.56.rim_ref), channel_id=1, source_target_pairs={{0,240},{16,224},{32,208},{48,192},{64,176},{80,160},{96,144},{112... | collective-permute-start | bytes 73736 | tf_op jit(solution)/shard_map/ppermute | solution.py:258
  25.8 0.0 collective-permute-done.8.got_ref
  25.9 0.4 collective-permute-start.9
  26.3 1.0 %collective-permute-done.6.got_ref = f32[3,8,256]{2,1,0:T(8,128)S(1)} collective-permute-done((f32[3,8,256]{2,1,0:T(8,128)S(1)}, f32[3,8,256]{2,1,0:T(8,128)S(1)}, u32[]{:S(2)}, u32[]{:S(2)}) %collective-permute-start.6) | collective-permute-done | bytes 24608 | tf_op jit(solution)/shard_map/ppermute | solution.py:258
  27.4 2.1 %collective-permute-start.7 = (f32[4,8,256]{2,1,0:T(8,128)S(1)}, f32[4,8,256]{2,1,0:T(8,128)S(1)}, u32[]{:S(2)}, u32[]{:S(2)}) collective-permute-start(f32[4,8,256]{2,1,0:T(8,128)S(1)} %get-tuple-element.60), channel_id=1, source_target_pairs={{0,48},{16,32},{32,16},{48,0},{64,112},{80,96},{96,80},{112,64},{1... | collective-permute-start | bytes 98312 | tf_op jit(solution)/shard_map/ppermute | solution.py:258
  29.5 0.0 collective-permute-done.9.high_got_ref
  29.5 1.6 %collective-permute-done.7.low_got_ref = f32[4,8,256]{2,1,0:T(8,128)S(1)} collective-permute-done((f32[4,8,256]{2,1,0:T(8,128)S(1)}, f32[4,8,256]{2,1,0:T(8,128)S(1)}, u32[]{:S(2)}, u32[]{:S(2)}) %collective-permute-start.7) | collective-permute-done | bytes 32800 | tf_op jit(solution)/shard_map/ppermute | solution.py:258
  31.2 0.4 collective-permute-start.10
  31.6 0.6 shard_map.86
  32.2 0.3 collective-permute-done.10.refs_4_
  32.5 1.3 %shard_map.87 = (f32[16,8,512]{2,1,0:T(8,128)S(1)}, f32[16,8,512]{2,1,0:T(8,128)S(1)}, f32[256,64]{1,0:T(8,128)}) custom-call(f32[16,8,1024]{2,1,0:T(8,128)S(1)} %get-tuple-element.42.factor_ref.refs_0_, f32[16,8,1024]{2,1,0:T(8,128)S(1)} %get-tuple-element.43.refs_1_, f32[16,8,1024]{2,1,0:T(8,128)S(1)} %get-tuple-element.44.refs_2_, ...), custom_call_target="tpu_custom_call" | custom-call | tf_op jit(solution)/shard_map/pallas_call | solution.py:379
  33.8 10.5 %all-to-all-start = ((f32[256,1,64]{2,1,0:T(1,128)}), f32[256,1,64]{2,1,0:T(1,128)S(1)}, u32[]{:S(2)}, u32[]{:S(2)}) async-start(f32[256,1,64]{2,1,0:T(1,128)} %bitcast.2), calls=%async_computation | async-start | bytes 262144 | tf_op jit(solution)/shard_map/all_to_all | solution.py:458
  44.3 0.2 shard_map.88
  44.4 2.2 %collective-permute-start.11 = (f32[16,1024]{1,0:T(8,128)S(1)}, f32[16,1024]{1,0:T(8,128)S(1)}, u32[]{:S(2)}, u32[]{:S(2)}) collective-permute-start(f32[16,1024]{1,0:T(8,128)S(1)} %get-tuple-element.73), channel_id=1, source_target_pairs={{0,16},{1,2},{2,1},{3,4},{4,3},{5,6},{6,5},{7,8},{8,7},{9,10},{10,... | collective-permute-start | bytes 196616 | tf_op jit(solution)/shard_map/ppermute | solution.py:64
  46.7 0.4 collective-permute-start.12
  47.1 0.5 collective-permute-done.11.second_ref
  47.6 3.2 %collective-permute-done.12.first_ref = f32[16,1024]{1,0:T(8,128)S(1)} collective-permute-done((f32[16,1024]{1,0:T(8,128)S(1)}, f32[16,1024]{1,0:T(8,128)S(1)}, u32[]{:S(2)}, u32[]{:S(2)}) %collective-permute-start.12) | collective-permute-done | bytes 65568 | tf_op jit(solution)/shard_map/ppermute | solution.py:53
  50.8 0.0 copy-start.4
  50.8 0.7 %copy-done.4 = s32[4]{0:T(128)S(1)} copy-done((s32[4]{0:T(128)S(1)}, s32[4]{0:T(128)}, u32[]{:S(2)}) %copy-start.4) | copy-done | bytes 40
  51.4 1.3 %shard_map.89 = (f32[16,8,1024]{2,1,0:T(8,128)}, f32[16,8,1024]{2,1,0:T(8,128)}, f32[1,4]{1,0:T(1,128)S(1)}) custom-call(f32[16,8,512]{2,1,0:T(8,128)S(1)} %get-tuple-element.67.mine_ref.adj_ref, f32[16,8,512]{2,1,0:T(8,128)S(1)} %get-tuple-element.70.got_ref.adj_got_ref, f32[16,8,512]{2,1,0:T(8,128)S(1)} %get-tuple-element.71.new_in_ref, ...), custom_call_target="tpu_custom_call" | custom-call | tf_op jit(solution)/shard_map/pallas_call | solution.py:379
  52.8 4.4 %all-to-all-done = f32[256,1,64]{2,1,0:T(1,128)S(1)} async-done(((f32[256,1,64]{2,1,0:T(1,128)}), f32[256,1,64]{2,1,0:T(1,128)S(1)}, u32[]{:S(2)}, u32[]{:S(2)}) %all-to-all-start) | async-done | bytes 65568 | tf_op jit(solution)/shard_map/all_to_all | solution.py:458
  57.1 0.7 %shard_map.90 = f32[1,4]{1,0:T(1,128)} custom-call(f32[256,64]{1,0:T(8,128)S(1)} %bitcast.6, f32[1,4]{1,0:T(1,128)S(1)} %get-tuple-element.78.weight_ref), custom_call_target="tpu_custom_call" | custom-call | tf_op jit(solution)/shard_map/pallas_call | solution.py:379
  (7 shorter events, 0.2 us)
Async XLA Ops:
  0.6 1.0 %copy-start = (f32[16,8,1024]{2,1,0:T(8,128)S(1)}, f32[16,8,1024]{2,1,0:T(8,128)}, u32[]{:S(2)}) copy-start(f32[16,8,1024]{2,1,0:T(8,128)} %velocity_ref.1) | copy-start | bytes 1572868
  1.7 3.5 %copy-start.1 = (f32[16,8,1024]{2,1,0:T(8,128)S(1)}, f32[16,8,1024]{2,1,0:T(8,128)}, u32[]{:S(2)}) copy-start(f32[16,8,1024]{2,1,0:T(8,128)} %refs_1_.1) | copy-start | bytes 1572868
  1.8 5.6 %collective-permute-start = (f32[16,1024]{1,0:T(8,128)S(1)}, f32[16,1024]{1,0:T(8,128)S(1)}, u32[]{:S(2)}, u32[]{:S(2)}) collective-permute-start(f32[16,1024]{1,0:T(8,128)S(1)} %get-tuple-element.46), channel_id=1, source_target_pairs={{0,16},{1,2},{2,1},{3,4},{4,3},{5,6},{6,5},{7,8},{8,7},{9,10},{10,... | collective-permute-start | bytes 196616 | tf_op jit(solution)/shard_map/ppermute | solution.py:64
  5.2 3.7 %collective-permute-start.1 = (f32[16,1024]{1,0:T(8,128)S(1)}, f32[16,1024]{1,0:T(8,128)S(1)}, u32[]{:S(2)}, u32[]{:S(2)}) collective-permute-start(f32[16,1024]{1,0:T(8,128)S(1)} %get-tuple-element.47), channel_id=1, source_target_pairs={{0,1},{1,0},{2,3},{3,2},{4,5},{5,4},{6,7},{7,6},{8,9},{9,8},{10,11... | collective-permute-start | bytes 196616 | tf_op jit(solution)/shard_map/ppermute | solution.py:53
  5.2 0.8 %copy-start.2 = (f32[16,1024]{1,0:T(8,128)S(1)}, f32[16,1024]{1,0:T(8,128)}, u32[]{:S(2)}) copy-start(f32[16,1024]{1,0:T(8,128)} %refs_0_.1) | copy-start | bytes 196612
  6.0 0.8 %copy-start.3 = (s32[16,1024]{1,0:T(8,128)S(1)}, s32[16,1024]{1,0:T(8,128)}, u32[]{:S(2)}) copy-start(s32[16,1024]{1,0:T(8,128)} %refs_3_.1) | copy-start | bytes 196612
  9.0 1.9 %collective-permute-start.2 = (f32[7,8,512]{2,1,0:T(8,128)S(1)}, f32[7,8,512]{2,1,0:T(8,128)S(1)}, u32[]{:S(2)}, u32[]{:S(2)}) collective-permute-start(f32[7,8,512]{2,1,0:T(8,128)S(1)} %get-tuple-element.51), channel_id=1, source_target_pairs={{0,16},{16,0},{32,48},{48,32},{64,80},{80,64},{96,112},{112,96},{1... | collective-permute-start | bytes 344072 | tf_op jit(solution)/shard_map/ppermute | solution.py:258
  11.0 4.0 %collective-permute-start.3 = (f32[7,8,256]{2,1,0:T(8,128)S(1)}, f32[7,8,256]{2,1,0:T(8,128)S(1)}, u32[]{:S(2)}, u32[]{:S(2)}) collective-permute-start(f32[7,8,256]{2,1,0:T(8,128)S(1)} %get-tuple-element.53), channel_id=1, source_target_pairs={{0,48},{16,32},{32,16},{48,0},{64,112},{80,96},{96,80},{112,64},{1... | collective-permute-start | bytes 172040 | tf_op jit(solution)/shard_map/ppermute | solution.py:258
  15.0 5.8 %collective-permute-start.4 = (f32[7,8,256]{2,1,0:T(8,128)S(1)}, f32[7,8,256]{2,1,0:T(8,128)S(1)}, u32[]{:S(2)}, u32[]{:S(2)}) collective-permute-start(f32[7,8,256]{2,1,0:T(8,128)S(1)} %get-tuple-element.54.mine_ref), channel_id=1, source_target_pairs={{0,112},{16,96},{32,80},{48,64},{64,48},{80,32},{96,16},{112,0},{1... | collective-permute-start | bytes 172040 | tf_op jit(solution)/shard_map/ppermute | solution.py:258
  18.7 3.4 %collective-permute-start.5 = (f32[7,8,256]{2,1,0:T(8,128)S(1)}, f32[7,8,256]{2,1,0:T(8,128)S(1)}, u32[]{:S(2)}, u32[]{:S(2)}) collective-permute-start(f32[7,8,256]{2,1,0:T(8,128)S(1)} %get-tuple-element.54.mine_ref), channel_id=1, source_target_pairs={{0,16},{16,0},{32,48},{48,32},{64,80},{80,64},{96,112},{112,96},{1... | collective-permute-start | bytes 172040 | tf_op jit(solution)/shard_map/ppermute | solution.py:258
  20.8 5.0 %collective-permute-start.8 = (f32[3,8,256]{2,1,0:T(8,128)S(1)}, f32[3,8,256]{2,1,0:T(8,128)S(1)}, u32[]{:S(2)}, u32[]{:S(2)}) collective-permute-start(f32[3,8,256]{2,1,0:T(8,128)S(1)} %get-tuple-element.55.rim_ref), channel_id=1, source_target_pairs={{0,240},{16,224},{32,208},{48,192},{64,176},{80,160},{96,144},{112... | collective-permute-start | bytes 73736 | tf_op jit(solution)/shard_map/ppermute | solution.py:258
  22.1 5.2 %collective-permute-start.6 = (f32[3,8,256]{2,1,0:T(8,128)S(1)}, f32[3,8,256]{2,1,0:T(8,128)S(1)}, u32[]{:S(2)}, u32[]{:S(2)}) collective-permute-start(f32[3,8,256]{2,1,0:T(8,128)S(1)} %get-tuple-element.56.rim_ref), channel_id=1, source_target_pairs={{0,240},{16,224},{32,208},{48,192},{64,176},{80,160},{96,144},{112... | collective-permute-start | bytes 73736 | tf_op jit(solution)/shard_map/ppermute | solution.py:258
  25.9 3.6 %collective-permute-start.9 = (f32[4,8,256]{2,1,0:T(8,128)S(1)}, f32[4,8,256]{2,1,0:T(8,128)S(1)}, u32[]{:S(2)}, u32[]{:S(2)}) collective-permute-start(f32[4,8,256]{2,1,0:T(8,128)S(1)} %get-tuple-element.63), channel_id=1, source_target_pairs={{0,16},{16,0},{32,48},{48,32},{64,80},{80,64},{96,112},{112,96},{1... | collective-permute-start | bytes 98312 | tf_op jit(solution)/shard_map/ppermute | solution.py:258
  27.4 3.7 %collective-permute-start.7 = (f32[4,8,256]{2,1,0:T(8,128)S(1)}, f32[4,8,256]{2,1,0:T(8,128)S(1)}, u32[]{:S(2)}, u32[]{:S(2)}) collective-permute-start(f32[4,8,256]{2,1,0:T(8,128)S(1)} %get-tuple-element.60), channel_id=1, source_target_pairs={{0,48},{16,32},{32,16},{48,0},{64,112},{80,96},{96,80},{112,64},{1... | collective-permute-start | bytes 98312 | tf_op jit(solution)/shard_map/ppermute | solution.py:258
  31.2 1.3 %collective-permute-start.10 = (f32[4,8,512]{2,1,0:T(8,128)S(1)}, f32[4,8,512]{2,1,0:T(8,128)S(1)}, u32[]{:S(2)}, u32[]{:S(2)}) collective-permute-start(f32[4,8,512]{2,1,0:T(8,128)S(1)} %get-tuple-element.68), channel_id=1, source_target_pairs={{0,16},{16,0},{32,48},{48,32},{64,80},{80,64},{96,112},{112,96},{1... | collective-permute-start | bytes 196616 | tf_op jit(solution)/shard_map/ppermute | solution.py:258
  33.8 23.4 %all-to-all-start = ((f32[256,1,64]{2,1,0:T(1,128)}), f32[256,1,64]{2,1,0:T(1,128)S(1)}, u32[]{:S(2)}, u32[]{:S(2)}) async-start(f32[256,1,64]{2,1,0:T(1,128)} %bitcast.2), calls=%async_computation | async-start | bytes 262144 | tf_op jit(solution)/shard_map/all_to_all | solution.py:458
  44.4 3.1 %collective-permute-start.11 = (f32[16,1024]{1,0:T(8,128)S(1)}, f32[16,1024]{1,0:T(8,128)S(1)}, u32[]{:S(2)}, u32[]{:S(2)}) collective-permute-start(f32[16,1024]{1,0:T(8,128)S(1)} %get-tuple-element.73), channel_id=1, source_target_pairs={{0,16},{1,2},{2,1},{3,4},{4,3},{5,6},{6,5},{7,8},{8,7},{9,10},{10,... | collective-permute-start | bytes 196616 | tf_op jit(solution)/shard_map/ppermute | solution.py:64
  46.7 4.1 %collective-permute-start.12 = (f32[16,1024]{1,0:T(8,128)S(1)}, f32[16,1024]{1,0:T(8,128)S(1)}, u32[]{:S(2)}, u32[]{:S(2)}) collective-permute-start(f32[16,1024]{1,0:T(8,128)S(1)} %get-tuple-element.74), channel_id=1, source_target_pairs={{0,1},{1,0},{2,3},{3,2},{4,5},{5,4},{6,7},{7,6},{8,9},{9,8},{10,11... | collective-permute-start | bytes 196616 | tf_op jit(solution)/shard_map/ppermute | solution.py:53
  50.8 0.7 %copy-start.4 = (s32[4]{0:T(128)S(1)}, s32[4]{0:T(128)}, u32[]{:S(2)}) copy-start(s32[4]{0:T(128)} %param.9) | copy-start | bytes 52

commit v8 on v7

--- a/solution.py
+++ b/solution.py
@@ -299,7 +299,7 @@
         out_ref[k] = value * scale
 
 
-def patch_sums(patch_count, total_rows, lanes, map_ref, adj_ref, new_ref):
+def patch_sums(patch_count, total_rows, lanes, map_ref, adj_ref, new_ref, places_ref=None):
     planes, rows, width = adj_ref.shape
     damping = damping_rows(rows, total_rows)
     patch_rows = PATCH_ROWS
@@ -318,7 +318,10 @@
         parts = jnp.concatenate(
             [jnp.where(in_row, part, 0.0) for part in (first, second, third)], axis=0
         ).astype(jnp.bfloat16)
-        places = jnp.where(lane_ids == patches % patch_lanes, 1.0, 0.0).astype(jnp.bfloat16)
+        if places_ref is None:
+            places = jnp.where(lane_ids == patches % patch_lanes, 1.0, 0.0).astype(jnp.bfloat16)
+        else:
+            places = places_ref[k]
         total = total + lax.dot_general(
             parts, places, (((1,), (1,)), ((), ())), preferred_element_type=F32
         )
@@ -327,13 +330,19 @@
 
 def own_half_kernel(
     patch_count, stiffness, total_rows, factor_ref, left_ref, adj_down_ref, down_ref, ends_ref, map_ref,
-    adj_ref, new_ref, sums_ref,
+    adj_ref, new_ref, sums_ref, places_ref,
 ):
     lanes = lanes_of(True, adj_ref.shape[2])
     sweep = (lanes, factor_ref, left_ref)
     back_sweep(*sweep, adj_down_ref, ends_ref[0], ends_ref[1], 1.0 / stiffness, adj_ref)
     back_sweep(*sweep, down_ref, ends_ref[2], ends_ref[3], 1.0 / stiffness, new_ref)
     sums_ref[...] = patch_sums(patch_count, total_rows, lanes, map_ref, adj_ref, new_ref)
+    other = lanes_of(False, adj_ref.shape[2])
+    patch_lanes, width = places_ref.shape[1:]
+    lane_ids = lax.broadcasted_iota(jnp.int32, (patch_lanes, width), 0)
+    for k in range(places_ref.shape[0]):
+        owners = lane_ids == map_ref[k : k + 1, other] % patch_lanes
+        places_ref[k] = jnp.where(owners, 1.0, 0.0).astype(jnp.bfloat16)
 
 
 def adjoint_edges_kernel(mine_ref, got_ref, first_ref, second_ref):
@@ -342,14 +351,16 @@
 
 
 def shares_kernel(
-    patch_count, stiffness, total_rows, factor_ref, left_ref, adj_down_ref, down_ref, ends_ref, map_ref, mine_ref,
+    patch_count, stiffness, total_rows, factor_ref, left_ref, adj_down_ref, down_ref, ends_ref, map_ref, mine_ref, places_ref,
     adj_ref, new_ref, shares_ref,
 ):
     lanes = lanes_of(False, adj_ref.shape[2])
     sweep = (lanes, factor_ref, left_ref)
     back_sweep(*sweep, adj_down_ref, ends_ref[0], ends_ref[1], 1.0 / stiffness, adj_ref)
     back_sweep(*sweep, down_ref, ends_ref[2], ends_ref[3], 1.0 / stiffness, new_ref)
-    sums = mine_ref[...] + patch_sums(patch_count, total_rows, lanes, map_ref, adj_ref, new_ref)
+    sums = mine_ref[...] + patch_sums(
+        patch_count, total_rows, lanes, map_ref, adj_ref, new_ref, places_ref
+    )
     rows_here = sums.shape[0]
     for i in range(shares_ref.shape[0] // rows_here):
         shares_ref[i * rows_here : (i + 1) * rows_here, :] = sums
@@ -428,9 +439,14 @@
     devices = groups_x * groups_y
     patch_count = owned * devices
     half = (planes, rows, span // 2)
-    adj_mine, new_mine, sums = call(
+    adj_mine, new_mine, sums, places = call(
         with_sizes(functools.partial(own_half_kernel, patch_count)),
-        [shape_of(*half), shape_of(*half), shape_of(PATCH_ROWS, patch_count // PATCH_ROWS)],
+        [
+            shape_of(*half),
+            shape_of(*half),
+            shape_of(PATCH_ROWS, patch_count // PATCH_ROWS),
+            jax.ShapeDtypeStruct((planes, patch_count // PATCH_ROWS, span // 2), jnp.bfloat16),
+        ],
         [],
         factor,
         left,
@@ -450,6 +466,7 @@
         got,
         patch_map,
         sums,
+        places,
     )
     first, second = call(
         adjoint_edges_kernel, [shape_of(*plane), shape_of(*plane)], [], adj_mine, adj_got

time: 58.1 us -> 58 us (level)
  transfers between devices with their start and end apart: 14 -> 14, of which waited for: 10 -> 9; matrix products, arithmetic and copies ran while one was open for 0% -> 0% of each run, Pallas kernels for 5% -> 5%
where the time goes in v8:
time: 58 us; the launch traced here: 57.7 us
  starting transfers between devices  30.1 us (52%)
  waiting for transfers between devices  17.9 us (31%)
  Pallas kernels  5.54 us (10%)
  local copies, waits for them, and re-layouts  3.37 us (6%)
  between operations  0.74 us (1%)
    ppermute x9, starting transfers between devices, swap(): return lax.ppermute(array, 'gx', pairs)  13.7 us
    all_to_all x1, starting transfers between devices, local(): shares = lax.all_to_all(sums, ('gy', 'gx'), 0, 0, tiled=True)  10.4 us
    ppermute x9, waiting for transfers between devices, swap(): return lax.ppermute(array, 'gx', pairs)  8.55 us
    ppermute x2, starting transfers between devices, far_swap(): return lax.ppermute(edge, ('gx', 'gy'), pairs)  5.56 us
    pallas_call x15, Pallas kernels, call(): pl.pallas_call(kernel, out_shape=outs, in_specs=[VMEM] * len(operands), o...  5.54 us
    ppermute x2, waiting for transfers between devices, near_swap(): lax.ppermute(edge, 'gy', [(i, i ^ 1) for i in range(lax.axis_size('gy'))])  4.56 us
    all_to_all x1, waiting for transfers between devices, local(): shares = lax.all_to_all(sums, ('gy', 'gx'), 0, 0, tiled=True)  4.35 us
    unnamed x10, local copies, waits for them, and re-layouts  3.37 us
  transfers between devices with their start and end apart: 14, of which 9 were waited for; matrix products, arithmetic and copies ran while one was open for 0% of the time, Pallas kernels for 5%

profile of v8, /device:TPU:1, one launch (start us, length us, event | category | flops | bytes accessed | tf_op | source)
XLA Modules:
  0.0 57.7 jit_solution(7569168023689024452)
XLA Ops:
  0.6 0.0 copy-start
  0.6 1.0 %copy-done = f32[16,8,1024]{2,1,0:T(8,128)S(1)} copy-done((f32[16,8,1024]{2,1,0:T(8,128)S(1)}, f32[16,8,1024]{2,1,0:T(8,128)}, u32[]{:S(2)}) %copy-start) | copy-done | bytes 524312
  1.7 0.0 copy-start.1
  1.7 0.1 shard_map.76
  1.8 3.3 %collective-permute-start = (f32[16,1024]{1,0:T(8,128)S(1)}, f32[16,1024]{1,0:T(8,128)S(1)}, u32[]{:S(2)}, u32[]{:S(2)}) collective-permute-start(f32[16,1024]{1,0:T(8,128)S(1)} %get-tuple-element.47), channel_id=1, source_target_pairs={{0,16},{1,2},{2,1},{3,4},{4,3},{5,6},{6,5},{7,8},{8,7},{9,10},{10,... | collective-permute-start | bytes 196616 | tf_op jit(solution)/shard_map/ppermute | solution.py:64
  5.2 0.0 collective-permute-start.1
  5.2 0.0 copy-done.1
  5.2 0.0 copy-start.2
  5.2 0.8 %copy-done.2 = f32[16,1024]{1,0:T(8,128)S(1)} copy-done((f32[16,1024]{1,0:T(8,128)S(1)}, f32[16,1024]{1,0:T(8,128)}, u32[]{:S(2)}) %copy-start.2) | copy-done | bytes 65560
  6.0 0.0 copy-start.3
  6.0 0.8 %copy-done.3 = s32[16,1024]{1,0:T(8,128)S(1)} copy-done((s32[16,1024]{1,0:T(8,128)S(1)}, s32[16,1024]{1,0:T(8,128)}, u32[]{:S(2)}) %copy-start.3) | copy-done | bytes 65560
  6.8 0.6 %shard_map.77 = (f32[16,8,1024]{2,1,0:T(8,128)S(1)}, f32[16,8,1024]{2,1,0:T(8,128)S(1)}, f32[16,8,1024]{2,1,0:T(8,128)S(1)}, f32[5,8,1024]{2,1,0:T(8,128)S(1)}, ...) custom-call(f32[16,1024]{1,0:T(8,128)S(1)} %copy-done.2, f32[16,8,1024]{2,1,0:T(8,128)S(1)} %copy-done.1, ...), custom_call_target="tpu_custom_call" | custom-call | tf_op jit(solution)/shard_map/pallas_call | solution.py:390
  7.4 0.0 collective-permute-done.second_ref
  7.4 1.4 %collective-permute-done.1.first_ref = f32[16,1024]{1,0:T(8,128)S(1)} collective-permute-done((f32[16,1024]{1,0:T(8,128)S(1)}, f32[16,1024]{1,0:T(8,128)S(1)}, u32[]{:S(2)}, u32[]{:S(2)}) %collective-permute-start.1) | collective-permute-done | bytes 65568 | tf_op jit(solution)/shard_map/ppermute | solution.py:53
  8.8 0.2 shard_map.78
  9.0 1.0 %collective-permute-start.2 = (f32[7,8,512]{2,1,0:T(8,128)S(1)}, f32[7,8,512]{2,1,0:T(8,128)S(1)}, u32[]{:S(2)}, u32[]{:S(2)}) collective-permute-start(f32[7,8,512]{2,1,0:T(8,128)S(1)} %get-tuple-element.52), channel_id=1, source_target_pairs={{0,16},{16,0},{32,48},{48,32},{64,80},{80,64},{96,112},{112,96},{1... | collective-permute-start | bytes 344072 | tf_op jit(solution)/shard_map/ppermute | solution.py:258
  10.0 1.0 %collective-permute-done.2.got_ref = f32[7,8,512]{2,1,0:T(8,128)S(1)} collective-permute-done((f32[7,8,512]{2,1,0:T(8,128)S(1)}, f32[7,8,512]{2,1,0:T(8,128)S(1)}, u32[]{:S(2)}, u32[]{:S(2)}) %collective-permute-start.2) | collective-permute-done | bytes 114720 | tf_op jit(solution)/shard_map/ppermute | solution.py:258
  11.0 1.0 %collective-permute-start.3 = (f32[7,8,256]{2,1,0:T(8,128)S(1)}, f32[7,8,256]{2,1,0:T(8,128)S(1)}, u32[]{:S(2)}, u32[]{:S(2)}) collective-permute-start(f32[7,8,256]{2,1,0:T(8,128)S(1)} %get-tuple-element.54), channel_id=1, source_target_pairs={{0,48},{16,32},{32,16},{48,0},{64,112},{80,96},{96,80},{112,64},{1... | collective-permute-start | bytes 172040 | tf_op jit(solution)/shard_map/ppermute | solution.py:258
  12.0 3.0 %collective-permute-done.3.got_ref = f32[7,8,256]{2,1,0:T(8,128)S(1)} collective-permute-done((f32[7,8,256]{2,1,0:T(8,128)S(1)}, f32[7,8,256]{2,1,0:T(8,128)S(1)}, u32[]{:S(2)}, u32[]{:S(2)}) %collective-permute-start.3) | collective-permute-done | bytes 57376 | tf_op jit(solution)/shard_map/ppermute | solution.py:258
  15.0 3.7 %collective-permute-start.4 = (f32[7,8,256]{2,1,0:T(8,128)S(1)}, f32[7,8,256]{2,1,0:T(8,128)S(1)}, u32[]{:S(2)}, u32[]{:S(2)}) collective-permute-start(f32[7,8,256]{2,1,0:T(8,128)S(1)} %get-tuple-element.55.mine_ref), channel_id=1, source_target_pairs={{0,112},{16,96},{32,80},{48,64},{64,48},{80,32},{96,16},{112,0},{1... | collective-permute-start | bytes 172040 | tf_op jit(solution)/shard_map/ppermute | solution.py:258
  18.7 0.2 collective-permute-start.5
  18.9 1.9 %collective-permute-done.4.got_ref = f32[7,8,256]{2,1,0:T(8,128)S(1)} collective-permute-done((f32[7,8,256]{2,1,0:T(8,128)S(1)}, f32[7,8,256]{2,1,0:T(8,128)S(1)}, u32[]{:S(2)}, u32[]{:S(2)}) %collective-permute-start.4) | collective-permute-done | bytes 57376 | tf_op jit(solution)/shard_map/ppermute | solution.py:258
  20.8 1.3 %collective-permute-start.8 = (f32[3,8,256]{2,1,0:T(8,128)S(1)}, f32[3,8,256]{2,1,0:T(8,128)S(1)}, u32[]{:S(2)}, u32[]{:S(2)}) collective-permute-start(f32[3,8,256]{2,1,0:T(8,128)S(1)} %get-tuple-element.56.rim_ref), channel_id=1, source_target_pairs={{0,240},{16,224},{32,208},{48,192},{64,176},{80,160},{96,144},{112... | collective-permute-start | bytes 73736 | tf_op jit(solution)/shard_map/ppermute | solution.py:258
  22.1 0.0 collective-permute-done.5.got_ref
  22.1 3.7 %collective-permute-start.6 = (f32[3,8,256]{2,1,0:T(8,128)S(1)}, f32[3,8,256]{2,1,0:T(8,128)S(1)}, u32[]{:S(2)}, u32[]{:S(2)}) collective-permute-start(f32[3,8,256]{2,1,0:T(8,128)S(1)} %get-tuple-element.57.rim_ref), channel_id=1, source_target_pairs={{0,240},{16,224},{32,208},{48,192},{64,176},{80,160},{96,144},{112... | collective-permute-start | bytes 73736 | tf_op jit(solution)/shard_map/ppermute | solution.py:258
  25.8 0.0 collective-permute-done.8.got_ref
  25.9 0.4 collective-permute-start.9
  26.3 1.0 %collective-permute-done.6.got_ref = f32[3,8,256]{2,1,0:T(8,128)S(1)} collective-permute-done((f32[3,8,256]{2,1,0:T(8,128)S(1)}, f32[3,8,256]{2,1,0:T(8,128)S(1)}, u32[]{:S(2)}, u32[]{:S(2)}) %collective-permute-start.6) | collective-permute-done | bytes 24608 | tf_op jit(solution)/shard_map/ppermute | solution.py:258
  27.4 2.1 %collective-permute-start.7 = (f32[4,8,256]{2,1,0:T(8,128)S(1)}, f32[4,8,256]{2,1,0:T(8,128)S(1)}, u32[]{:S(2)}, u32[]{:S(2)}) collective-permute-start(f32[4,8,256]{2,1,0:T(8,128)S(1)} %get-tuple-element.61), channel_id=1, source_target_pairs={{0,48},{16,32},{32,16},{48,0},{64,112},{80,96},{96,80},{112,64},{1... | collective-permute-start | bytes 98312 | tf_op jit(solution)/shard_map/ppermute | solution.py:258
  29.5 0.0 collective-permute-done.9.high_got_ref
  29.5 1.6 %collective-permute-done.7.low_got_ref = f32[4,8,256]{2,1,0:T(8,128)S(1)} collective-permute-done((f32[4,8,256]{2,1,0:T(8,128)S(1)}, f32[4,8,256]{2,1,0:T(8,128)S(1)}, u32[]{:S(2)}, u32[]{:S(2)}) %collective-permute-start.7) | collective-permute-done | bytes 32800 | tf_op jit(solution)/shard_map/ppermute | solution.py:258
  31.2 0.4 collective-permute-start.10
  31.6 0.9 %shard_map.86 = (f32[16,8,512]{2,1,0:T(8,128)S(1)}, f32[16,8,512]{2,1,0:T(8,128)S(1)}, f32[16,64]{1,0:T(8,128)S(1)}, bf16[16,64,512]{2,1,0:T(8,128)(2,1)S(1)}) custom-call(f32[16,8,1024]{2,1,0:T(8,128)S(1)} %get-tuple-element.43.factor_ref.refs_0_, f32[16,8,1024]{2,1,0:T(8,128)S(1)} %get-tuple-element.44.refs_1_, ...), custom_call_target="tpu_custom_call" | custom-call | tf_op jit(solution)/shard_map/pallas_call | solution.py:390
  32.5 0.0 collective-permute-done.10.refs_4_
  32.5 1.2 %shard_map.87 = (f32[16,8,512]{2,1,0:T(8,128)S(1)}, f32[16,8,512]{2,1,0:T(8,128)S(1)}, f32[256,64]{1,0:T(8,128)}) custom-call(f32[16,8,1024]{2,1,0:T(8,128)S(1)} %get-tuple-element.43.factor_ref.refs_0_, f32[16,8,1024]{2,1,0:T(8,128)S(1)} %get-tuple-element.44.refs_1_, f32[16,8,1024]{2,1,0:T(8,128)S(1)} %get-tuple-element.45.refs_2_, ...), custom_call_target="tpu_custom_call" | custom-call | tf_op jit(solution)/shard_map/pallas_call | solution.py:390
  33.7 10.4 %all-to-all-start = ((f32[256,1,64]{2,1,0:T(1,128)}), f32[256,1,64]{2,1,0:T(1,128)S(1)}, u32[]{:S(2)}, u32[]{:S(2)}) async-start(f32[256,1,64]{2,1,0:T(1,128)} %bitcast.2), calls=%async_computation | async-start | bytes 262144 | tf_op jit(solution)/shard_map/all_to_all | solution.py:475
  44.2 0.2 shard_map.88
  44.3 2.2 %collective-permute-start.11 = (f32[16,1024]{1,0:T(8,128)S(1)}, f32[16,1024]{1,0:T(8,128)S(1)}, u32[]{:S(2)}, u32[]{:S(2)}) collective-permute-start(f32[16,1024]{1,0:T(8,128)S(1)} %get-tuple-element.75), channel_id=1, source_target_pairs={{0,16},{1,2},{2,1},{3,4},{4,3},{5,6},{6,5},{7,8},{8,7},{9,10},{10,... | collective-permute-start | bytes 196616 | tf_op jit(solution)/shard_map/ppermute | solution.py:64
  46.6 0.4 collective-permute-start.12
  47.0 0.5 collective-permute-done.11.second_ref
  47.5 3.2 %collective-permute-done.12.first_ref = f32[16,1024]{1,0:T(8,128)S(1)} collective-permute-done((f32[16,1024]{1,0:T(8,128)S(1)}, f32[16,1024]{1,0:T(8,128)S(1)}, u32[]{:S(2)}, u32[]{:S(2)}) %collective-permute-start.12) | collective-permute-done | bytes 65568 | tf_op jit(solution)/shard_map/ppermute | solution.py:53
  50.7 0.0 copy-start.4
  50.7 0.7 %copy-done.4 = s32[4]{0:T(128)S(1)} copy-done((s32[4]{0:T(128)S(1)}, s32[4]{0:T(128)}, u32[]{:S(2)}) %copy-start.4) | copy-done | bytes 40
  51.3 1.3 %shard_map.89 = (f32[16,8,1024]{2,1,0:T(8,128)}, f32[16,8,1024]{2,1,0:T(8,128)}, f32[1,4]{1,0:T(1,128)S(1)}) custom-call(f32[16,8,512]{2,1,0:T(8,128)S(1)} %get-tuple-element.68.mine_ref.adj_ref, f32[16,8,512]{2,1,0:T(8,128)S(1)} %get-tuple-element.72.got_ref.adj_got_ref, f32[16,8,512]{2,1,0:T(8,128)S(1)} %get-tuple-element.73.new_in_ref, ...), custom_call_target="tpu_custom_call" | custom-call | tf_op jit(solution)/shard_map/pallas_call | solution.py:390
  52.7 4.4 %all-to-all-done = f32[256,1,64]{2,1,0:T(1,128)S(1)} async-done(((f32[256,1,64]{2,1,0:T(1,128)}), f32[256,1,64]{2,1,0:T(1,128)S(1)}, u32[]{:S(2)}, u32[]{:S(2)}) %all-to-all-start) | async-done | bytes 65568 | tf_op jit(solution)/shard_map/all_to_all | solution.py:475
  57.0 0.7 %shard_map.90 = f32[1,4]{1,0:T(1,128)} custom-call(f32[256,64]{1,0:T(8,128)S(1)} %bitcast.6, f32[1,4]{1,0:T(1,128)S(1)} %get-tuple-element.80.weight_ref), custom_call_target="tpu_custom_call" | custom-call | tf_op jit(solution)/shard_map/pallas_call | solution.py:390
  (7 shorter events, 0.2 us)
Async XLA Ops:
  0.6 1.0 %copy-start = (f32[16,8,1024]{2,1,0:T(8,128)S(1)}, f32[16,8,1024]{2,1,0:T(8,128)}, u32[]{:S(2)}) copy-start(f32[16,8,1024]{2,1,0:T(8,128)} %velocity_ref.1) | copy-start | bytes 1572868
  1.7 3.5 %copy-start.1 = (f32[16,8,1024]{2,1,0:T(8,128)S(1)}, f32[16,8,1024]{2,1,0:T(8,128)}, u32[]{:S(2)}) copy-start(f32[16,8,1024]{2,1,0:T(8,128)} %refs_1_.1) | copy-start | bytes 1572868
  1.8 5.6 %collective-permute-start = (f32[16,1024]{1,0:T(8,128)S(1)}, f32[16,1024]{1,0:T(8,128)S(1)}, u32[]{:S(2)}, u32[]{:S(2)}) collective-permute-start(f32[16,1024]{1,0:T(8,128)S(1)} %get-tuple-element.47), channel_id=1, source_target_pairs={{0,16},{1,2},{2,1},{3,4},{4,3},{5,6},{6,5},{7,8},{8,7},{9,10},{10,... | collective-permute-start | bytes 196616 | tf_op jit(solution)/shard_map/ppermute | solution.py:64
  5.2 3.7 %collective-permute-start.1 = (f32[16,1024]{1,0:T(8,128)S(1)}, f32[16,1024]{1,0:T(8,128)S(1)}, u32[]{:S(2)}, u32[]{:S(2)}) collective-permute-start(f32[16,1024]{1,0:T(8,128)S(1)} %get-tuple-element.48), channel_id=1, source_target_pairs={{0,1},{1,0},{2,3},{3,2},{4,5},{5,4},{6,7},{7,6},{8,9},{9,8},{10,11... | collective-permute-start | bytes 196616 | tf_op jit(solution)/shard_map/ppermute | solution.py:53
  5.2 0.8 %copy-start.2 = (f32[16,1024]{1,0:T(8,128)S(1)}, f32[16,1024]{1,0:T(8,128)}, u32[]{:S(2)}) copy-start(f32[16,1024]{1,0:T(8,128)} %refs_0_.1) | copy-start | bytes 196612
  6.0 0.8 %copy-start.3 = (s32[16,1024]{1,0:T(8,128)S(1)}, s32[16,1024]{1,0:T(8,128)}, u32[]{:S(2)}) copy-start(s32[16,1024]{1,0:T(8,128)} %refs_3_.1) | copy-start | bytes 196612
  9.0 1.9 %collective-permute-start.2 = (f32[7,8,512]{2,1,0:T(8,128)S(1)}, f32[7,8,512]{2,1,0:T(8,128)S(1)}, u32[]{:S(2)}, u32[]{:S(2)}) collective-permute-start(f32[7,8,512]{2,1,0:T(8,128)S(1)} %get-tuple-element.52), channel_id=1, source_target_pairs={{0,16},{16,0},{32,48},{48,32},{64,80},{80,64},{96,112},{112,96},{1... | collective-permute-start | bytes 344072 | tf_op jit(solution)/shard_map/ppermute | solution.py:258
  11.0 4.0 %collective-permute-start.3 = (f32[7,8,256]{2,1,0:T(8,128)S(1)}, f32[7,8,256]{2,1,0:T(8,128)S(1)}, u32[]{:S(2)}, u32[]{:S(2)}) collective-permute-start(f32[7,8,256]{2,1,0:T(8,128)S(1)} %get-tuple-element.54), channel_id=1, source_target_pairs={{0,48},{16,32},{32,16},{48,0},{64,112},{80,96},{96,80},{112,64},{1... | collective-permute-start | bytes 172040 | tf_op jit(solution)/shard_map/ppermute | solution.py:258
  15.0 5.8 %collective-permute-start.4 = (f32[7,8,256]{2,1,0:T(8,128)S(1)}, f32[7,8,256]{2,1,0:T(8,128)S(1)}, u32[]{:S(2)}, u32[]{:S(2)}) collective-permute-start(f32[7,8,256]{2,1,0:T(8,128)S(1)} %get-tuple-element.55.mine_ref), channel_id=1, source_target_pairs={{0,112},{16,96},{32,80},{48,64},{64,48},{80,32},{96,16},{112,0},{1... | collective-permute-start | bytes 172040 | tf_op jit(solution)/shard_map/ppermute | solution.py:258
  18.7 3.4 %collective-permute-start.5 = (f32[7,8,256]{2,1,0:T(8,128)S(1)}, f32[7,8,256]{2,1,0:T(8,128)S(1)}, u32[]{:S(2)}, u32[]{:S(2)}) collective-permute-start(f32[7,8,256]{2,1,0:T(8,128)S(1)} %get-tuple-element.55.mine_ref), channel_id=1, source_target_pairs={{0,16},{16,0},{32,48},{48,32},{64,80},{80,64},{96,112},{112,96},{1... | collective-permute-start | bytes 172040 | tf_op jit(solution)/shard_map/ppermute | solution.py:258
  20.8 5.0 %collective-permute-start.8 = (f32[3,8,256]{2,1,0:T(8,128)S(1)}, f32[3,8,256]{2,1,0:T(8,128)S(1)}, u32[]{:S(2)}, u32[]{:S(2)}) collective-permute-start(f32[3,8,256]{2,1,0:T(8,128)S(1)} %get-tuple-element.56.rim_ref), channel_id=1, source_target_pairs={{0,240},{16,224},{32,208},{48,192},{64,176},{80,160},{96,144},{112... | collective-permute-start | bytes 73736 | tf_op jit(solution)/shard_map/ppermute | solution.py:258
  22.1 5.2 %collective-permute-start.6 = (f32[3,8,256]{2,1,0:T(8,128)S(1)}, f32[3,8,256]{2,1,0:T(8,128)S(1)}, u32[]{:S(2)}, u32[]{:S(2)}) collective-permute-start(f32[3,8,256]{2,1,0:T(8,128)S(1)} %get-tuple-element.57.rim_ref), channel_id=1, source_target_pairs={{0,240},{16,224},{32,208},{48,192},{64,176},{80,160},{96,144},{112... | collective-permute-start | bytes 73736 | tf_op jit(solution)/shard_map/ppermute | solution.py:258
  25.9 3.6 %collective-permute-start.9 = (f32[4,8,256]{2,1,0:T(8,128)S(1)}, f32[4,8,256]{2,1,0:T(8,128)S(1)}, u32[]{:S(2)}, u32[]{:S(2)}) collective-permute-start(f32[4,8,256]{2,1,0:T(8,128)S(1)} %get-tuple-element.64), channel_id=1, source_target_pairs={{0,16},{16,0},{32,48},{48,32},{64,80},{80,64},{96,112},{112,96},{1... | collective-permute-start | bytes 98312 | tf_op jit(solution)/shard_map/ppermute | solution.py:258
  27.4 3.7 %collective-permute-start.7 = (f32[4,8,256]{2,1,0:T(8,128)S(1)}, f32[4,8,256]{2,1,0:T(8,128)S(1)}, u32[]{:S(2)}, u32[]{:S(2)}) collective-permute-start(f32[4,8,256]{2,1,0:T(8,128)S(1)} %get-tuple-element.61), channel_id=1, source_target_pairs={{0,48},{16,32},{32,16},{48,0},{64,112},{80,96},{96,80},{112,64},{1... | collective-permute-start | bytes 98312 | tf_op jit(solution)/shard_map/ppermute | solution.py:258
  31.2 1.4 %collective-permute-start.10 = (f32[4,8,512]{2,1,0:T(8,128)S(1)}, f32[4,8,512]{2,1,0:T(8,128)S(1)}, u32[]{:S(2)}, u32[]{:S(2)}) collective-permute-start(f32[4,8,512]{2,1,0:T(8,128)S(1)} %get-tuple-element.69), channel_id=1, source_target_pairs={{0,16},{16,0},{32,48},{48,32},{64,80},{80,64},{96,112},{112,96},{1... | collective-permute-start | bytes 196616 | tf_op jit(solution)/shard_map/ppermute | solution.py:258
  33.7 23.3 %all-to-all-start = ((f32[256,1,64]{2,1,0:T(1,128)}), f32[256,1,64]{2,1,0:T(1,128)S(1)}, u32[]{:S(2)}, u32[]{:S(2)}) async-start(f32[256,1,64]{2,1,0:T(1,128)} %bitcast.2), calls=%async_computation | async-start | bytes 262144 | tf_op jit(solution)/shard_map/all_to_all | solution.py:475
  44.3 3.1 %collective-permute-start.11 = (f32[16,1024]{1,0:T(8,128)S(1)}, f32[16,1024]{1,0:T(8,128)S(1)}, u32[]{:S(2)}, u32[]{:S(2)}) collective-permute-start(f32[16,1024]{1,0:T(8,128)S(1)} %get-tuple-element.75), channel_id=1, source_target_pairs={{0,16},{1,2},{2,1},{3,4},{4,3},{5,6},{6,5},{7,8},{8,7},{9,10},{10,... | collective-permute-start | bytes 196616 | tf_op jit(solution)/shard_map/ppermute | solution.py:64
  46.6 4.1 %collective-permute-start.12 = (f32[16,1024]{1,0:T(8,128)S(1)}, f32[16,1024]{1,0:T(8,128)S(1)}, u32[]{:S(2)}, u32[]{:S(2)}) collective-permute-start(f32[16,1024]{1,0:T(8,128)S(1)} %get-tuple-element.76), channel_id=1, source_target_pairs={{0,1},{1,0},{2,3},{3,2},{4,5},{5,4},{6,7},{7,6},{8,9},{9,8},{10,11... | collective-permute-start | bytes 196616 | tf_op jit(solution)/shard_map/ppermute | solution.py:53
  50.7 0.7 %copy-start.4 = (s32[4]{0:T(128)S(1)}, s32[4]{0:T(128)}, u32[]{:S(2)}) copy-start(s32[4]{0:T(128)} %param.9) | copy-start | bytes 52
